TPU v7x, 32 devices: a whole 2x2x4 slice. The times are simulated.
32 devices in a mesh: branch: 2 (over y), row: 4 (over z), seq: 4 (over x, core).
Axes of the slice: x: 2, y: 2, z: 4, core: 2. Of those that a mesh axis runs over, the one named last changes fastest.
Arguments:
- alignment_input: bfloat16 [256, 32, 256], P('seq', 'row'), may hold values from -6 to 6
- pairwise_input: bfloat16 [128, 32, 32], P('seq', 'row'), may hold values from -30 to 30
- alignment_gain: float32 [256], replicated, may hold values from 0.25 to 1.75
- product_gain: float32 [256], replicated, may hold values from 0.25 to 1.75
- attention_weight: bfloat16 [256, 4, 256], replicated, may hold values from -0.375 to 0.375
- mixing_weight: bfloat16 [256, 256], replicated, may hold values from -0.375 to 0.375
- outer_input_weight: bfloat16 [256, 2, 32], replicated, may hold values from -0.375 to 0.375
- outer_output_weight: bfloat16 [32, 32, 128], replicated, may hold values from -3 to 3
- bias_matrix: bfloat16 [128, 8], replicated, may hold values from -6 to 6
- pairwise_gain: float32 [128], replicated, may hold values from 0.25 to 1.75
- triangle_input_weight: bfloat16 [4, 128, 128], P(None, 'seq'), may hold values from -0.5 to 0.5
- triangle_gate_weight: bfloat16 [128, 128], P('seq'), may hold values from -0.5 to 0.5
- triangle_gain: float32 [128], P('seq'), may hold values from 0.25 to 1.75
- triangle_output_weight: bfloat16 [128, 128], P(None, 'seq'), may hold values from -0.5 to 0.5
- transition_gain: float32 [128], replicated, may hold values from 0.25 to 1.75
- transition_up_weight: bfloat16 [512, 128], P('seq'), may hold values from -0.5 to 0.5
- transition_down_weight: bfloat16 [128, 512], P(None, 'seq'), may hold values from -0.25 to 0.25
Outputs:
- alignment_output: bfloat16 [256, 32, 256], P('seq', 'row', 'branch')
- pairwise_output: bfloat16 [128, 32, 32], P('seq', 'row', 'branch')
All inputs are finite; a program needn't handle non-finite values.
Results may differ from a plain program's by a relative error of at most 0.011.
Values may be sent and summed in bfloat16 or wider, within the bound.
No kernel may reach another device: no remote copies, remote signals or barrier semaphores. Data moves between devices by JAX's collectives and lax.ppermute only.
A program may use at most 128 MiB of HBM per device.

v0:
```python
import jax
import jax.numpy as jnp
from jax import lax
from jax.sharding import PartitionSpec as P

EPSILON = 1e-05


def shifted(value, axis, by):
    length = lax.axis_size(axis)
    pairs = [(i, i + by) for i in range(length) if 0 <= i + by < length]
    return lax.ppermute(value, axis, pairs)


def from_partner(value, axis, distance):
    return lax.ppermute(value, axis, [(i, i ^ 1 << distance) for i in range(lax.axis_size(axis))])


def layer_normalize(values, axis):
    average = jnp.mean(values, axis=axis, keepdims=True)
    centred = values - average
    spread = jnp.mean(centred * centred, axis=axis, keepdims=True)
    return centred * lax.rsqrt(spread + EPSILON)


def full_channels(values):
    return lax.all_gather(values, "seq", axis=0, tiled=True)


def channel_sum(term, kept_rows):
    return lax.psum_scatter(
        term(jnp.int32(0), kept_rows * lax.axis_size("seq")), "seq", scatter_dimension=0, tiled=True
    )


def shards(
    alignment_input,
    pairwise_input,
    alignment_gain,
    product_gain,
    attention_weight,
    mixing_weight,
    outer_input_weight,
    outer_output_weight,
    bias_matrix,
    pairwise_gain,
    triangle_input_weight,
    triangle_gate_weight,
    triangle_gain,
    triangle_output_weight,
    transition_gain,
    transition_up_weight,
    transition_down_weight,
):
    local_sequences, local_rows, alignment_channels = alignment_input.shape
    chan_local = pairwise_input.shape[0]
    residues = pairwise_input.shape[2]
    pair_width, head_total = bias_matrix.shape
    latent_heads = mixing_weight.shape[0]
    head_size = latent_heads // head_total
    outer_width = outer_input_weight.shape[2]
    tri_local = triangle_input_weight.shape[1]
    trans_local = transition_up_weight.shape[0]
    seq_total = local_sequences * lax.axis_size("seq")
    path_index = lax.axis_index("branch")
    alignment_branch = path_index == 0
    query_shape = (local_sequences, local_rows, latent_heads)
    pair_shape = (chan_local, local_rows, residues)
    full_pair_shape = (pair_width, local_rows, residues)
    key_shape = (local_sequences, 2 * latent_heads, local_rows)
    gathered = full_channels(pairwise_input)

    def alignment_early():
        alignment_module = layer_normalize(alignment_input.astype(jnp.float32), 2)
        normalized_values = (alignment_module * alignment_gain).astype(jnp.bfloat16)
        outer_normalized = (alignment_module * product_gain).astype(jnp.bfloat16)
        flattened_rows = normalized_values.reshape(-1, alignment_channels)
        outer_flattened = outer_normalized.reshape(-1, alignment_channels)
        query = (
            (
                jnp.dot(flattened_rows, attention_weight[:, 0], preferred_element_type=jnp.float32)
                * head_size ** (-0.5)
            )
            .astype(jnp.bfloat16)
            .reshape(query_shape)
        )
        gate = (
            jax.nn.sigmoid(
                jnp.dot(flattened_rows, attention_weight[:, 3], preferred_element_type=jnp.float32)
            )
            .astype(jnp.bfloat16)
            .reshape(query_shape)
        )
        key_values = (
            jnp.einsum(
                "sim,mkc->skci",
                normalized_values,
                attention_weight[:, 1:3],
                preferred_element_type=jnp.float32,
            )
            .astype(jnp.bfloat16)
            .reshape(key_shape)
        )
        left = (
            jnp.dot(outer_flattened, outer_input_weight[:, 0], preferred_element_type=jnp.float32)
            .astype(jnp.bfloat16)
            .reshape(local_sequences, local_rows, outer_width)
        )
        right_cols = jnp.einsum(
            "sim,mc->sci",
            outer_normalized,
            outer_input_weight[:, 1],
            preferred_element_type=jnp.float32,
        ).astype(jnp.bfloat16)
        empty_bias = jnp.zeros((head_total, local_rows, residues), jnp.bfloat16)
        empty_pair = jnp.zeros(full_pair_shape, jnp.bfloat16)
        return (empty_bias, empty_pair, query, key_values, gate, left, right_cols)

    def pair_early():
        unit = layer_normalize(gathered.astype(jnp.float32), 0)
        plain = unit.astype(jnp.bfloat16).reshape(pair_width, -1)
        bias_rows = (
            jnp.einsum("ch,cn->hn", bias_matrix, plain, preferred_element_type=jnp.float32)
            .astype(jnp.bfloat16)
            .reshape(head_total, local_rows, residues)
        )
        tri_input = (unit * pairwise_gain[:, None, None]).astype(jnp.bfloat16)
        empty_query = jnp.zeros(query_shape, jnp.bfloat16)
        empty_keys = jnp.zeros(key_shape, jnp.bfloat16)
        empty_left = jnp.zeros((local_sequences, local_rows, outer_width), jnp.bfloat16)
        empty_right = jnp.zeros((local_sequences, outer_width, local_rows), jnp.bfloat16)
        return (bias_rows, tri_input, empty_query, empty_keys, empty_query, empty_left, empty_right)

    bias_local, tri_input, query, key_values, gate, left, right_cols = lax.cond(
        alignment_branch, alignment_early, pair_early
    )
    bias_recv = shifted(bias_local, "branch", -1)
    query_heads = query.reshape(local_sequences, local_rows, head_total, head_size).transpose(
        0, 2, 1, 3
    )

    def fold_real(running, shard_part):
        highest, totals, weighted = running
        columns = shard_part.shape[2]
        keys_part = shard_part[:, :latent_heads].reshape(
            local_sequences, head_total, head_size, columns
        )
        values_part = shard_part[:, latent_heads:].reshape(
            local_sequences, head_total, head_size, columns
        )
        bias_part = bias_recv.astype(jnp.float32)
        scores = (
            jnp.einsum(
                "shid,shdj->shij", query_heads, keys_part, preferred_element_type=jnp.float32
            )
            + bias_part[None]
        )
        raised = jnp.maximum(highest, jnp.max(scores, axis=3))
        weights = jnp.exp(scores - raised[..., None])
        totals = jnp.sum(weights, axis=3)
        weighted = jnp.einsum(
            "shij,shdj->shid",
            weights.astype(jnp.bfloat16),
            values_part,
            preferred_element_type=jnp.float32,
        )
        return (raised, totals, weighted)

    initial = (
        jnp.full((local_sequences, head_total, local_rows), -1e30, jnp.float32),
        jnp.zeros((local_sequences, head_total, local_rows), jnp.float32),
        jnp.zeros((local_sequences, head_total, local_rows, head_size), jnp.float32),
    )
    shard_part = lax.all_gather(key_values, "row", axis=2, tiled=True)
    highest, totals, weighted = lax.cond(
        alignment_branch, lambda: fold_real(initial, shard_part), lambda: initial
    )
    safe_totals = jnp.where(totals > 0, totals, 1.0)
    attended = (weighted / safe_totals[..., None]).transpose(0, 2, 1, 3).reshape(query_shape)
    mixed_heads = (gate.astype(jnp.float32) * attended).astype(jnp.bfloat16)
    right_full = lax.all_gather(right_cols, "row", axis=2, tiled=True)
    right_matrix = right_full.reshape(local_sequences * outer_width, residues)
    spread = lax.cond(
        alignment_branch,
        lambda: jnp.einsum(
            "sic,cdo->oisd", left, outer_output_weight, preferred_element_type=jnp.float32
        ).astype(jnp.bfloat16),
        lambda: jnp.zeros((pair_width, local_rows, local_sequences, outer_width), jnp.bfloat16),
    )

    def outer_term(amount):
        spread_part = spread.reshape(amount * local_rows, local_sequences * outer_width)
        return jnp.dot(spread_part, right_matrix, preferred_element_type=jnp.float32).reshape(
            amount, local_rows, residues
        )

    tri_flat = tri_input.reshape(pair_width, -1)

    def pair_operands():
        linear = jnp.dot(
            triangle_input_weight.reshape(4 * tri_local, pair_width),
            tri_flat,
            preferred_element_type=jnp.float32,
        )
        linear = linear.reshape(4, tri_local, local_rows, residues)
        left_part = (linear[0] * jax.nn.sigmoid(linear[1])).astype(jnp.bfloat16)
        right_part = (linear[2] * jax.nn.sigmoid(linear[3])).astype(jnp.bfloat16)
        return (left_part, right_part)

    def empty_operands():
        empty = jnp.zeros((tri_local, local_rows, residues), jnp.bfloat16)
        return (empty, empty)

    left_tri, right_tri = lax.cond(alignment_branch, empty_operands, pair_operands)
    tri_shard_part = lax.all_gather(right_tri, "row", axis=1, tiled=True)
    triangle = lax.optimization_barrier(
        lax.cond(
            alignment_branch,
            lambda: jnp.zeros((tri_local, local_rows, tri_shard_part.shape[1]), jnp.float32),
            lambda: jnp.einsum(
                "cik,cjk->cij", left_tri, tri_shard_part, preferred_element_type=jnp.float32
            ),
        ).astype(jnp.bfloat16)
    )
    tri_float = triangle.astype(jnp.float32)
    summed, squared = lax.psum(
        (jnp.sum(tri_float, axis=0), jnp.sum(tri_float * tri_float, axis=0)), "seq"
    )
    tri_total = tri_local * lax.axis_size("seq")
    average = summed / tri_total
    variance = jnp.maximum(squared / tri_total - average * average, 0.0)
    tri_norm = (
        (tri_float - average) * lax.rsqrt(variance + EPSILON) * triangle_gain[:, None, None]
    ).astype(jnp.bfloat16)
    norm_flat = tri_norm.reshape(tri_local, -1)

    def tri_term(amount):
        return jnp.dot(
            triangle_output_weight, norm_flat, preferred_element_type=jnp.float32
        ).reshape(amount, local_rows, residues)

    def first_term(offset, amount):
        return lax.cond(alignment_branch, lambda: outer_term(amount), lambda: tri_term(amount))

    summed_first = channel_sum(first_term, chan_local)
    outer_increment = (summed_first * (1.0 / seq_total)).astype(jnp.bfloat16)
    gate_values = jax.nn.sigmoid(
        jnp.dot(triangle_gate_weight, tri_flat, preferred_element_type=jnp.float32)
    ).reshape(pair_shape)
    first_update = lax.optimization_barrier(
        (pairwise_input.astype(jnp.float32) + gate_values * summed_first).astype(jnp.bfloat16)
    )
    gathered_next = full_channels(first_update)

    def pair_hidden():
        trans_norm = (
            (layer_normalize(gathered_next.astype(jnp.float32), 0) * transition_gain[:, None, None])
            .astype(jnp.bfloat16)
            .reshape(pair_width, -1)
        )
        return jax.nn.relu(
            jnp.dot(transition_up_weight, trans_norm, preferred_element_type=jnp.float32)
        ).astype(jnp.bfloat16)

    hidden_units = lax.cond(
        alignment_branch,
        lambda: jnp.zeros((trans_local, local_rows * residues), jnp.bfloat16),
        pair_hidden,
    )

    def trans_real(amount):
        return jnp.dot(
            transition_down_weight, hidden_units, preferred_element_type=jnp.float32
        ).reshape(amount, local_rows, residues)

    def trans_term(offset, amount):
        return lax.cond(
            alignment_branch,
            lambda: jnp.zeros((amount, local_rows, residues), jnp.float32),
            lambda: trans_real(amount),
        )

    pair_following = (
        first_update.astype(jnp.float32) + channel_sum(trans_term, chan_local)
    ).astype(jnp.bfloat16)
    half_residues = residues // 2
    halved_width = alignment_channels // 2
    outgoing_product = jnp.where(
        alignment_branch,
        outer_increment[:, :, half_residues:],
        pair_following[:, :, :half_residues],
    )
    incoming = from_partner(outgoing_product, "branch", 0)
    local_half = jnp.where(
        alignment_branch,
        outer_increment[:, :, :half_residues],
        pair_following[:, :, half_residues:],
    )
    pairwise_output = (local_half.astype(jnp.float32) + incoming.astype(jnp.float32)).astype(
        jnp.bfloat16
    )
    mixed_received = shifted(mixed_heads, "branch", 1)
    mixed_applied = jnp.where(alignment_branch, mixed_heads, mixed_received)
    mix_columns = lax.dynamic_slice_in_dim(
        mixing_weight, path_index * halved_width, halved_width, 1
    )
    residual_stream = lax.dynamic_slice_in_dim(
        alignment_input, path_index * halved_width, halved_width, 2
    )
    projected_values = jnp.dot(
        mixed_applied.reshape(-1, latent_heads), mix_columns, preferred_element_type=jnp.float32
    )
    alignment_output = (
        residual_stream.astype(jnp.float32)
        + projected_values.reshape(local_sequences, local_rows, halved_width)
    ).astype(jnp.bfloat16)
    return (alignment_output, pairwise_output)


def solution(mesh):
    return jax.shard_map(
        shards,
        mesh=mesh,
        in_specs=(
            P("seq", "row", None),
            P("seq", "row", None),
            P(),
            P(),
            P(),
            P(),
            P(),
            P(),
            P(),
            P(),
            P(None, "seq", None),
            P("seq", None),
            P("seq"),
            P(None, "seq"),
            P(),
            P("seq", None),
            P(None, "seq"),
        ),
        out_specs=(P("seq", "row", "branch"), P("seq", "row", "branch")),
        check_vma=False,
    )
```

profile of v0, /device:TPU:0, one launch (start us, length us, event | category | flops | bytes accessed | tf_op | source)
XLA Modules:
  0.0 188.9 jit_solution(368343828678282786)
XLA Ops:
  8.1 7.4 %all_gather.15 = bf16[128,8,32]{2,1,0:T(8,128)(2,1)S(1)} all-gather(bf16[32,8,32]{2,1,0:T(8,128)(2,1)} %param.34), channel_id=1, replica_groups=mesh['branch'=2,'row'=4,'seq'=4] {'seq'}, dimensions={0}, use_global_device_ids=true | all-gather | bytes 81920 | tf_op jit(solution)/shard_map/all_gather | solution.py:27
  15.5 7.4 %conditional.8 = (bf16[8,8,32]{2,1,0:T(8,128)(2,1)S(1)}, bf16[64,8,256]{2,1,0:T(8,128)(2,1)S(1)}, bf16[64,512,8]{1,2,0:T(8,128)(2,1)S(1)}, bf16[64,8,32]{2,1,0:T...) conditional(s32[]{:T(128)} %convert_element_type.137, ...), branch_computations={%region_0.0_spmd, %region_3.0_spmd} | conditional | flops 290488832 | bytes 7535788 | solution.py:134
  15.5 1.1 convert_reduce_fusion.1
  16.6 1.2 fusion.22
  17.8 1.1 copy.69
  18.9 1.3 fusion.13
  20.3 0.4 copy.103
  20.7 0.4 convolution_convert_fusion.1
  21.1 0.3 fusion.14
  21.4 0.3 convolution_convert_fusion.3
  21.9 0.3 fusion.15
  22.2 0.6 reshape.133
  22.9 0.6 copy-done.12
  23.5 13.2 %all_gather.17 = bf16[32,32,32]{2,1,0:T(8,128)(2,1)S(1)} all-gather(bf16[32,8,32]{2,1,0:T(8,128)(2,1)S(1)} %get-tuple-element.117), channel_id=1, replica_groups=mesh['branch'=2,'row'=4,'seq'=4] {'row'}, dimensions={1}, use_global_device_ids=true | all-gather | bytes 81920 | tf_op jit(solution)/shard_map/all_gather | solution.py:215
  36.8 12.9 %all_gather.18 = bf16[64,32,32]{0,2,1:T(8,128)(2,1)S(1)} all-gather(bf16[64,32,8]{0,2,1:T(8,128)(2,1)S(1)} %copy.79), channel_id=1, replica_groups=mesh['branch'=2,'row'=4,'seq'=4] {'row'}, dimensions={2}, use_global_device_ids=true | all-gather | bytes 163840 | tf_op jit(solution)/shard_map/all_gather | solution.py:181
  49.7 5.7 %all-reduce = (f32[8,32]{1,0:T(8,128)S(1)}, f32[8,32]{1,0:T(8,128)S(1)}) all-reduce(f32[8,32]{1,0:T(8,128)S(1)} %get-tuple-element.215, f32[8,32]{1,0:T(8,128)S(1)} %get-tuple-element.214), channel_id=1, replica_groups=mesh['branch'=2,'row'=4,'seq'=4] {'seq'}, use_global_device_ids=true, to_apply=%region_17.18 | all-reduce | flops 512 | bytes 4096 | tf_op jit(solution)/shard_map/psum | solution.py:226
  55.6 3.4 %conditional.12 = (bf16[128,8,64,32]{0,2,1,3:T(8,128)(2,1)}) conditional(s32[]{:T(128)} %convert_element_type.137, () %tuple.75, (bf16[32,32,128]{2,1,0:T(8,128)(2,1)S(1)}, bf16[64,8,32]{2,1,0:T(8,128)(2,1)S(1)}) %tuple.137), branch_computations={%region_18.19_spmd, %region_19.20_spmd} | conditional | flops 136314880 | bytes 4554760 | solution.py:183
  55.8 3.2 %convert_bitcast_fusion = bf16[128,8,64,32]{0,2,1,3:T(8,128)(2,1)} fusion(bf16[32,32,128,1]{2,1,0,3:T(8,128)(2,1)S(1)} %bitcast.119, bf16[64,8,32]{0,2,1:T(8,128)(2,1)S(1)} %copy.78), kind=kOutput, calls=%fused_computation.68 | convolution fusion | flops 136314880 | bytes 4489216 | tf_op jit(solution)/shard_map/cond/branch_1_fun/sic,cdo->oisd/dot_general | solution.py:185
  59.1 3.1 %conditional.13 = (f32[128,8,32]{0,2,1:T(8,128)S(1)}) conditional(s32[]{:T(128)} %convert_element_type.137, (bf16[128,32]{0,1:T(8,128)(2,1)S(1)}, bf16[32,8,32]{2,1,0:T(8,128)(2,1)S(1)}) %tuple.140, (bf16[128,8,64,32]{0,2,1,3:T(8,128)(2,1)}, bf16[64,32,32]{0,2,1:T(8,128)(2,1)S(1)}) %tuple.77), branch_computations={%region_20.21_spmd, %region_21.22_spmd} | conditional | flops 134217728 | bytes 4456456 | solution.py:243
  59.1 3.1 %convolution_bitcast_fusion = f32[128,8,32]{0,2,1:T(8,128)S(1)} fusion(bf16[128,8,64,32]{0,2,1,3:T(8,128)(2,1)} %get-tuple-element.206, bf16[64,32,32]{0,2,1:T(8,128)(2,1)S(1)} %get-tuple-element.90), kind=kOutput, calls=%fused_computation.71 | convolution fusion | flops 134217728 | bytes 4456448 | tf_op jit(solution)/shard_map/cond/branch_1_fun/dot_general | solution.py:193
  62.2 0.8 copy.104
  63.2 1.0 fusion.66
  64.2 16.9 %reduce-scatter.7.cloned.1.call-done = f32[32,256]{1,0:T(8,128)} async-done(((f32[128,256]{1,0:T(8,128)}), f32[32,256]{1,0:T(8,128)}) %reduce-scatter.7.cloned.1.call-update) | async-done | bytes 32784
  81.2 0.9 copy.105
  82.0 0.6 multiply_convert_fusion
  82.8 5.8 %all_gather.19 = bf16[128,8,32]{2,1,0:T(8,128)(2,1)S(1)} all-gather(bf16[32,8,32]{2,1,0:T(8,128)(2,1)S(1)} %copy.84), channel_id=1, replica_groups=mesh['branch'=2,'row'=4,'seq'=4] {'seq'}, dimensions={0}, use_global_device_ids=true | all-gather | bytes 81920 | tf_op jit(solution)/shard_map/all_gather | solution.py:27
  88.7 0.8 copy.106
  89.5 0.9 copy.70
  90.5 1.3 collective-permute-start
  91.8 1.1 copy.71
  92.8 17.4 %reduce-scatter.9.cloned.1.call-done = f32[32,256]{1,0:T(8,128)} async-done(((f32[128,256]{1,0:T(8,128)}), f32[32,256]{1,0:T(8,128)}) %reduce-scatter.9.cloned.1.call-update) | async-done | bytes 32784
  110.2 0.9 copy.107
  111.1 0.6 add_convert_fusion
  111.7 26.3 %all-gather.2.cloned.1.call-done = bf16[64,512,32]{1,0,2:T(8,128)(2,1)} async-done(((bf16[64,512,8]{1,0,2:T(8,128)(2,1)}), bf16[64,512,32]{1,0,2:T(8,128)(2,1)}) %all-gather.2.cloned.1.call-update) | async-done | bytes 2097168 | tf_op jit(solution)/shard_map/all_gather | solution.py:174
  138.0 23.7 %conditional.9 = (f32[64,8,8]{2,1,0:T(8,128)S(1)}, f32[64,8,8,32]{3,2,1,0:T(8,128)S(1)}) conditional(s32[]{:T(128)} %convert_element_type.137, () %tuple.68, (bf16[64,512,32]{1,0,2:T(8,128)(2,1)}, bf16[64,8,8,32]{0,3,1,2:T(8,128)(2,1)}, bf16[8,8,32]{2,1,0:T(8,128)(2,1)S(1)}) %tuple.136), branch_computations={%region_6.0_spmd, %region_7.0_spmd} | conditional | flops 17823744 | bytes 18780260 | solution.py:175
  138.1 8.0 %copy.72 = bf16[64,512,32]{2,1,0:T(8,128)(2,1)} copy(bf16[64,512,32]{1,0,2:T(8,128)(2,1)} %get-tuple-element.199) | data formatting | bytes 4194304 | tf_op jit(solution)/shard_map
  146.1 6.0 %fusion.75 = (bf16[64,256,32]{2,1,0:T(8,128)(2,1)}, bf16[64,256,32]{2,1,0:T(8,128)(2,1)}) fusion(bf16[64,512,32]{2,1,0:T(8,128)(2,1)} %copy.72), kind=kLoop, calls=%fused_computation.115 | loop fusion | bytes 4194304 | tf_op jit(solution)/shard_map/cond/branch_1_fun/slice | solution.py:148
  152.1 1.6 copy.73
  153.7 3.6 %add_reduce_fusion = (f32[64,8,8]{2,1,0:T(8,128)S(1)}, f32[64,8,8,32]{3,2,1,0:T(8,128)S(1)}) fusion(f32[8,8,32]{2,1,0:T(8,128)S(1)} %convert_element_type.111, bf16[64,8,8,32]{3,2,1,0:T(8,128)(2,1)S(1)} %copy.73, bf16[64,8,32,32]{3,2,1,0:T(8,128)(2,1)} %bitcast.108), kind=kOutput, calls=%fused_computation.49 | convolution fusion | flops 8646656 | bytes 1859584 | tf_op jit(solution)/shard_map/cond/branch_1_fun/shid,shdj->shij/dot_general | solution.py:153
  157.4 2.3 %fusion.38 = f32[64,8,8,32]{3,2,1,0:T(8,128)S(1)} fusion(bf16[64,8,32,32]{3,2,1,0:T(8,128)(2,1)S(1)} %bitcast.107, f32[64,8,8,32]{3,2,1,0:T(8,128)S(1)} %get-tuple-element.223, f32[64,8,8]{2,1,0:T(8,128)S(1)} %broadcast_maximum_fusion, f32[8,8,32]{2,1,0:T(8,128)S(1)} %convert_element_type.111), kind=kOutput, calls=%fused_computation.52 | convolution fusion | flops 8781824 | bytes 2121728 | tf_op jit(solution)/shard_map/cond/branch_1_fun/shij,shdj->shid/dot_general | solution.py:161
  159.7 2.1 %fusion.37 = f32[64,8,8]{2,1,0:T(8,128)S(1)} fusion(f32[64,8,8,32]{3,2,1,0:T(8,128)S(1)} %get-tuple-element.223, f32[64,8,8]{2,1,0:T(8,128)S(1)} %broadcast_maximum_fusion, f32[8,8,32]{2,1,0:T(8,128)} %copy-done.5), kind=kLoop, calls=%fused_computation.51 | loop fusion | flops 389120 | bytes 565248 | tf_op jit(solution)/shard_map/cond/branch_1_fun/reduce_sum | solution.py:160
  161.8 1.7 divide_bitcast_fusion
  163.5 2.6 %copy.74 = f32[64,8,8,32]{0,3,2,1:T(8,128)S(1)} copy(f32[64,8,8,32]{3,1,2,0:T(8,128)} %divide_bitcast_fusion) | data formatting | bytes 1048576 | tf_op jit(solution)/shard_map/transpose | solution.py:179
  166.2 1.3 collective-permute-start.1
  167.7 11.9 %collective-permute-done.2 = bf16[32,8,16]{0,2,1:T(8,128)(2,1)S(1)} collective-permute-done((bf16[32,8,16]{0,2,1:T(8,128)(2,1)S(1)}, bf16[32,8,16]{0,2,1:T(8,128)(2,1)S(1)}, u32[]{:S(2)}, u32[]{:S(2)}) %collective-permute-start.2) | collective-permute-done | bytes 8224 | tf_op jit(solution)/shard_map/ppermute | solution.py:16
  179.6 0.6 add_convert_fusion.2
  180.3 0.3 copy.76
  180.6 0.9 fusion.62
  (77 shorter events, 1.6 us)
Async XLA Ops:
  8.0 172.6 %copy-start = (bf16[256,256]{1,0:T(8,128)(2,1)S(1)}, bf16[256,256]{1,0:T(8,128)(2,1)}, u32[]{:S(2)}) copy-start(bf16[256,256]{1,0:T(8,128)(2,1)} %param.38) | copy-start | bytes 393220
  8.0 73.2 %reduce-scatter.7.cloned.1.call-start = ((), (), s32[]{:S(2)}) async-start(), calls=%async_computation.3 | async-start | bytes 163840
  18.9 1.8 copy-start.4
  18.9 1.8 copy-start.19
  20.3 1.1 copy-start.17
  20.3 1.1 copy-start.20
  22.8 0.6 copy-start.12
  22.8 32.7 %copy-start.15 = (f32[32]{0:T(128)S(1)}, f32[32]{0:T(128)}, u32[]{:S(2)}) copy-start(f32[32]{0:T(128)} %param.45) | copy-start | bytes 388
  22.8 32.8 %copy-start.6 = (bf16[32,32,128]{2,1,0:T(8,128)(2,1)S(1)}, bf16[32,32,128]{2,1,0:T(8,128)(2,1)}, u32[]{:S(2)}) copy-start(bf16[32,32,128]{2,1,0:T(8,128)(2,1)} %param.40) | copy-start | bytes 786436
  55.6 3.4 %copy-start.14 = (bf16[128,32]{0,1:T(8,128)(2,1)S(1)}, bf16[128,32]{0,1:T(8,128)(2,1)}, u32[]{:S(2)}) copy-start(bf16[128,32]{0,1:T(8,128)(2,1)} %param.46) | copy-start | bytes 24580
  59.0 4.0 %copy-start.7 = (bf16[32,8,32]{2,1,0:T(8,128)(2,1)S(1)}, bf16[32,8,32]{2,1,0:T(8,128)(2,1)}, u32[]{:S(2)}) copy-start(bf16[32,8,32]{2,1,0:T(8,128)(2,1)} %param.34) | copy-start | bytes 49156
  59.0 4.1 %copy-start.18 = (bf16[32,128]{1,0:T(8,128)(2,1)S(1)}, bf16[32,128]{1,0:T(8,128)(2,1)}, u32[]{:S(2)}) copy-start(bf16[32,128]{1,0:T(8,128)(2,1)} %param.44) | copy-start | bytes 24580
  59.0 29.5 %copy-start.10 = (bf16[128,128]{1,0:T(8,128)(2,1)S(1)}, bf16[128,128]{1,0:T(8,128)(2,1)}, u32[]{:S(2)}) copy-start(bf16[128,128]{1,0:T(8,128)(2,1)} %param.48) | copy-start | bytes 98308
  59.1 29.5 %copy-start.16 = (f32[128]{0:T(128)S(1)}, f32[128]{0:T(128)}, u32[]{:S(2)}) copy-start(f32[128]{0:T(128)} %param.47) | copy-start | bytes 1540
  62.2 26.4 %copy-start.11 = (bf16[128,128]{1,0:T(8,128)(2,1)S(1)}, bf16[128,128]{1,0:T(8,128)(2,1)}, u32[]{:S(2)}) copy-start(bf16[128,128]{1,0:T(8,128)(2,1)} %param.49) | copy-start | bytes 98308
  63.0 47.3 %reduce-scatter.9.cloned.1.call-start = ((), (), s32[]{:S(2)}) async-start(), calls=%async_computation.4 | async-start | bytes 163840
  82.0 8.4 %copy-start.13 = (bf16[8,8,32]{2,1,0:T(8,128)(2,1)S(1)}, bf16[8,8,32]{2,1,0:T(8,128)(2,1)}, u32[]{:S(2)}) copy-start(bf16[8,8,32]{2,1,0:T(8,128)(2,1)} %copy-done.12) | copy-start | bytes 12292
  89.4 48.6 %all-gather.2.cloned.1.call-start = ((), (), s32[]{:S(2)}) async-start(), calls=%async_computation.2 | async-start | bytes 2621440 | tf_op jit(solution)/shard_map/all_gather | solution.py:174
  90.5 21.3 %collective-permute-start = (bf16[8,8,32]{2,1,0:T(8,128)(2,1)S(1)}, bf16[8,8,32]{2,1,0:T(8,128)(2,1)S(1)}, u32[]{:S(2)}, u32[]{:S(2)}) collective-permute-start(bf16[8,8,32]{2,1,0:T(8,128)(2,1)S(1)} %copy-done.13), channel_id=1, source_target_pairs={{16,0},{17,1},{18,2},{19,3},{20,4},{21,5},{22,6},{23,7},{24,8},{25... | collective-permute-start | bytes 12296 | tf_op jit(solution)/shard_map/ppermute | solution.py:12
  138.1 19.3 %copy-start.5 = (f32[8,8,32]{2,1,0:T(8,128)}, f32[8,8,32]{2,1,0:T(8,128)S(1)}, u32[]{:S(2)}) copy-start(f32[8,8,32]{2,1,0:T(8,128)S(1)} %convert_element_type.111) | copy-start | bytes 24580 | tf_op jit(solution)/shard_map/cond
  146.1 6.0 %copy-start.2 = (bf16[64,8,8,32]{0,3,1,2:T(8,128)(2,1)S(1)}, bf16[64,8,8,32]{0,3,1,2:T(8,128)(2,1)}, u32[]{:S(2)}) copy-start(bf16[64,8,8,32]{0,3,1,2:T(8,128)(2,1)} %get-tuple-element.200) | copy-start | bytes 786436 | tf_op jit(solution)/shard_map/cond
  153.7 3.7 %copy-start.1 = (bf16[64,256,32]{2,1,0:T(8,128)(2,1)S(1)}, bf16[64,256,32]{2,1,0:T(8,128)(2,1)}, u32[]{:S(2)}) copy-start(bf16[64,256,32]{2,1,0:T(8,128)(2,1)} %get-tuple-element.220) | copy-start | bytes 3145732 | tf_op jit(solution)/shard_map/cond
  166.1 1.5 copy-start.8
  166.1 1.5 copy-start.9
  166.1 14.4 %copy-start.3 = (bf16[64,8,256]{2,1,0:T(8,128)(2,1)S(1)}, bf16[64,8,256]{2,1,0:T(8,128)(2,1)}, u32[]{:S(2)}) copy-start(bf16[64,8,256]{2,1,0:T(8,128)(2,1)} %param.33) | copy-start | bytes 786436
  166.2 14.0 %collective-permute-start.1 = (bf16[64,8,256]{0,2,1:T(8,128)(2,1)S(1)}, bf16[64,8,256]{0,2,1:T(8,128)(2,1)S(1)}, u32[]{:S(2)}, u32[]{:S(2)}) collective-permute-start(bf16[64,8,256]{0,2,1:T(8,128)(2,1)S(1)} %fusion.67), channel_id=1, source_target_pairs={{0,16},{1,17},{2,18},{3,19},{4,20},{5,21},{6,22},{7,23},{8,24},{9,... | collective-permute-start | bytes 786440 | tf_op jit(solution)/shard_map/ppermute | solution.py:12
  167.6 12.0 %collective-permute-start.2 = (bf16[32,8,16]{0,2,1:T(8,128)(2,1)S(1)}, bf16[32,8,16]{0,2,1:T(8,128)(2,1)S(1)}, u32[]{:S(2)}, u32[]{:S(2)}) collective-permute-start(bf16[32,8,16]{0,2,1:T(8,128)(2,1)S(1)} %slice_select_fusion), channel_id=1, source_target_pairs={{0,16},{16,0},{1,17},{17,1},{2,18},{18,2},{3,19},{19,3},{4,20},{20... | collective-permute-start | bytes 24584 | tf_op jit(solution)/shard_map/ppermute | solution.py:16
Sparse Core Ops, SparseCore 0:
  63.1 18.0 reduce-scatter.6
  89.6 20.6 reduce-scatter.8
Sparse Core Ops, SparseCore 1:
  91.5 46.5 all-gather.1
where the time goes:
time: 190 us; the launch traced here: 189 us
  waiting for transfers between devices  72.6 us (38%)
  blocking collectives  45 us (24%)
  local copies, waits for them, and re-layouts  27.3 us (14%)
  matrix products  16.8 us (9%)
  between operations  15.8 us (8%)
  other arithmetic  8.34 us (4%)
  starting transfers between devices  2.81 us (1%)
    unnamed x5, waiting for transfers between devices  34.4 us
    all_gather x1, waiting for transfers between devices, shards(): shard_part = lax.all_gather(key_values, 'row', axis=2, tiled=True)  26.3 us
    all_gather x2, blocking collectives, full_channels(): return lax.all_gather(values, 'seq', axis=0, tiled=True)  13.2 us
    all_gather x1, blocking collectives, shards(): tri_shard_part = lax.all_gather(right_tri, 'row', axis=1, tiled=True)  13.2 us
    all_gather x1, blocking collectives, shards(): right_full = lax.all_gather(right_cols, 'row', axis=2, tiled=True)  12.9 us
    ppermute x1, waiting for transfers between devices, from_partner(): lax.ppermute(value, axis, [(i, i ^ 1 << distance) for i in range(lax.axis...  11.9 us
    another operation x10, local copies, waits for them, and re-layouts  10.9 us
    slice x1, local copies, waits for them, and re-layouts, fold_real(): shard_part[:, latent_heads:]  6 us
  transfers between devices with their start and end apart: 6, of which 4 were waited for; matrix products, arithmetic and copies ran while one was open for 3% of the time, Pallas kernels for 0%

commit v1 on v0

--- a/solution.py
+++ b/solution.py
@@ -1,6 +1,10 @@
+import functools
+
 import jax
 import jax.numpy as jnp
 from jax import lax
+from jax.experimental import pallas as pl
+from jax.experimental.pallas import tpu as pltpu
 from jax.sharding import PartitionSpec as P
 
 EPSILON = 1e-05
@@ -317,9 +321,450 @@
     return (alignment_output, pairwise_output)
 
 
+def rounded(values):
+    return values.astype(jnp.bfloat16)
+
+
+def widened(values):
+    return values.astype(jnp.float32)
+
+
+def product(left, right, contract_left=1, contract_right=0):
+    return lax.dot_general(
+        left,
+        right,
+        (((contract_left,), (contract_right,)), ((), ())),
+        preferred_element_type=jnp.float32,
+    )
+
+
+def group_maximum(values, group):
+    tiles = []
+    for start in range(0, values.shape[1], 128):
+        tile = values[:, start : start + 128]
+        lane = lax.broadcasted_iota(jnp.int32, tile.shape, 1)
+        step = 1
+        while step < group:
+            ahead = pltpu.roll(tile, 128 - step, 1)
+            behind = pltpu.roll(tile, step, 1)
+            tile = jnp.maximum(tile, jnp.where((lane & step) == 0, ahead, behind))
+            step *= 2
+        tiles.append(tile)
+    return jnp.concatenate(tiles, axis=1)
+
+
+def same_group(rows, columns, group):
+    row = lax.broadcasted_iota(jnp.int32, (rows, columns), 0) // group
+    column = lax.broadcasted_iota(jnp.int32, (rows, columns), 1) // group
+    return row == column
+
+
+def kernel_call(body, outputs, operands, scratch=(), flops=0):
+    vmem = pl.BlockSpec(memory_space=pltpu.VMEM)
+    size = sum(a.size * a.dtype.itemsize for a in operands)
+    size += sum(o.size * o.dtype.itemsize for o in outputs)
+    return pl.pallas_call(
+        body,
+        out_shape=outputs,
+        in_specs=[vmem] * len(operands),
+        out_specs=[vmem] * len(outputs),
+        scratch_shapes=list(scratch),
+        cost_estimate=pl.CostEstimate(flops=flops, bytes_accessed=size, transcendentals=0),
+        compiler_params=pltpu.CompilerParams(vmem_limit_bytes=32 * 2**20),
+    )(*operands)
+
+
+def exchange(value, axes, distance):
+    members = lax.axis_size(axes)
+    return lax.ppermute(value, axes, [(i, i ^ distance) for i in range(members)])
+
+
+def send_kernel(sizes, rows_ref, pair_ref, gain_ref, weight_ref, same_ref, other_ref, left_ref, wide):
+    sequences, local_rows, residues, chan_local, outer_width = sizes
+    part = sequences // 4
+    part_rows = part * local_rows
+    unit_here = 2 * lax.axis_index("branch") + lax.rem(lax.axis_index("row"), 2)
+    unit_other = 2 * lax.axis_index("branch") + 1 - lax.rem(lax.axis_index("row"), 2)
+    same_ref[0:part_rows, :] = rows_ref[pl.ds(unit_here * part_rows, part_rows), :]
+    other_ref[0:part_rows, :] = rows_ref[pl.ds(unit_other * part_rows, part_rows), :]
+    pair = widened(pair_ref[...])
+    flat_pair = rounded(jnp.concatenate([pair[:, i, :] for i in range(local_rows)], axis=1))
+    same_ref[part_rows : part_rows + chan_local, :] = flat_pair
+    other_ref[part_rows : part_rows + chan_local, :] = flat_pair
+    normed = rounded(layer_normalize(widened(rows_ref[...]), 1) * gain_ref[...])
+    wide[:, 0 : 2 * outer_width] = product(normed, weight_ref[...])
+    base = part_rows + chan_local
+    for i in range(local_rows):
+        both = rounded(wide[pl.ds(i, sequences, stride=local_rows), :])
+        lanes = slice(i * outer_width, (i + 1) * outer_width)
+        left_ref[:, lanes] = both[:, :outer_width]
+        same_ref[base : base + sequences, lanes] = both[:, outer_width : 2 * outer_width]
+    other_ref[base : base + sequences, :] = same_ref[base : base + sequences, :]
+
+
+def weight_kernel(left_ref, input_ref, gate_ref, gain_ref, output_ref, up_ref, down_ref, packed_ref):
+    at = 0
+    kinds, tri_local, _ = input_ref.shape
+    for kind in range(kinds):
+        packed_ref[at : at + tri_local, :] = input_ref[kind]
+        at += tri_local
+    packed_ref[at : at + gate_ref.shape[0], :] = gate_ref[...]
+    at += gate_ref.shape[0]
+    scaled = widened(output_ref[...]) * gain_ref[...]
+    packed_ref[at : at + tri_local, :] = rounded(scaled.T)
+    at += tri_local
+    for ref in (up_ref, down_ref):
+        packed_ref[at : at + ref.shape[0], :] = ref[...]
+        at += ref.shape[0]
+    sequences = left_ref.shape[0]
+    for start in (0, 128):
+        packed_ref[at : at + sequences, :] = left_ref[:, start : start + 128]
+        at += sequences
+
+
+def relay_kernel(sizes, own_ref, one_ref, two_ref, three_ref, relay_ref):
+    sequences, local_rows, residues, chan_local, outer_width = sizes
+    part_rows = sequences // 4 * local_rows
+    row = lax.axis_index("row")
+    branch = lax.axis_index("branch")
+    base = part_rows + chan_local
+    shard_total = 4
+    for distance, ref in enumerate((own_ref, one_ref, two_ref, three_ref)):
+        shard = row ^ distance
+        relay_ref[pl.ds(pl.multiple_of(shard * chan_local, chan_local), chan_local), :] = ref[
+            part_rows:base, :
+        ]
+
+        @pl.when(shard // 2 == branch)
+        def _():
+            start = shard_total * chan_local + lax.rem(shard, 2) * sequences
+            relay_ref[pl.ds(pl.multiple_of(start, sequences), sequences), :] = ref[
+                base : base + sequences, :
+            ]
+
+
+def score_kernel(
+    sizes, own_ref, one_ref, two_ref, three_ref, gain_ref, weight_ref,
+    score_ref, values_ref, gate_ref, module,
+):
+    sequences, local_rows, residues, chan_local, outer_width = sizes
+    part = sequences // 4
+    part_rows = part * local_rows
+    width = gain_ref.shape[1]
+    head_size = 32
+    row = lax.axis_index("row")
+    for distance, ref in enumerate((own_ref, one_ref, two_ref, three_ref)):
+        shard = row ^ distance
+        block = widened(ref[0:part_rows, :])
+        unit = layer_normalize(block, 1) * gain_ref[...]
+        module[:, pl.ds(pl.multiple_of(shard * local_rows, local_rows), local_rows), :] = unit.reshape(
+            part, local_rows, width
+        )
+    normed = rounded(module[...].reshape(part * residues, width))
+    half = residues // 2
+    here = module[:, pl.ds(pl.multiple_of(row // 2 * half, half), half), :]
+    query_rows = rounded(here.reshape(part * half, width))
+    heads = values_ref.shape[1]
+    query = rounded(product(query_rows, weight_ref[:, 0:heads]) * head_size ** (-0.5))
+    keys = rounded(product(normed, weight_ref[:, heads : 2 * heads]))
+    values_ref[...] = rounded(product(normed, weight_ref[:, 2 * heads : 3 * heads]))
+    gate_ref[...] = rounded(jax.nn.sigmoid(product(query_rows, weight_ref[:, 3 * heads :])))
+    groups = heads // head_size
+    mask = same_group(groups * residues, heads, head_size)
+    for s in range(part):
+        one = keys[s * residues : (s + 1) * residues]
+        spread = jnp.where(mask, jnp.concatenate([one] * groups, axis=0), jnp.bfloat16(0))
+        score_ref[s * half : (s + 1) * half, :] = product(
+            query[s * half : (s + 1) * half], spread, 1, 1
+        )
+
+
+def mix_kernel(
+    sizes, pair_refs, score_ref, values_ref, gate_ref, bias_ref, mixing_ref, own_ref, one_ref,
+    near_here_ref, near_there_ref, far_here_ref, far_there_ref, full, flat, module,
+):
+    sequences, local_rows, residues, chan_local, outer_width = sizes
+    part = sequences // 4
+    part_rows = part * local_rows
+    half = residues // 2
+    heads = values_ref.shape[1]
+    head_size = 32
+    groups = heads // head_size
+    row = lax.axis_index("row")
+    branch = lax.axis_index("branch")
+    seq = lax.axis_index("seq")
+    pair_width = 4 * chan_local
+    for distance, ref in zip((0, 2, 1, 3), pair_refs):
+        source = pl.multiple_of((seq ^ distance) * chan_local, chan_local)
+        for k in range(2):
+            shard = row // 2 * 2 + k
+            start = pl.multiple_of(shard * chan_local, chan_local)
+            full[k, pl.ds(source, chan_local), :] = ref[pl.ds(start, chan_local), :]
+    for k in range(2):
+        plain = rounded(layer_normalize(widened(full[k]), 0))
+        bias = widened(rounded(product(bias_ref[...], plain)))
+        for i in range(local_rows):
+            for h in range(groups):
+                flat[k * local_rows + i : k * local_rows + i + 1, h * residues : (h + 1) * residues] = bias[
+                    h : h + 1, i * residues : (i + 1) * residues
+                ]
+    bias_rows = flat[...]
+    scores = (
+        score_ref[...].reshape(part, half, groups * residues) + bias_rows[None]
+    ).reshape(part * half, groups * residues)
+    weights = rounded(jnp.exp(scores - group_maximum(scores, residues)))
+    mask = same_group(groups * residues, heads, head_size)
+    ones = jnp.where(mask, jnp.bfloat16(1), jnp.bfloat16(0))
+    totals = product(weights, ones)
+    attended = []
+    for s in range(part):
+        one = values_ref[s * residues : (s + 1) * residues, :]
+        spread = jnp.where(mask, jnp.concatenate([one] * groups, axis=0), jnp.bfloat16(0))
+        attended.append(product(weights[s * half : (s + 1) * half], spread))
+    mixed = rounded(widened(gate_ref[...]) * (jnp.concatenate(attended, axis=0) / totals))
+    projected = product(mixed, mixing_ref[...])
+    width = projected.shape[1]
+    module[...] = projected.reshape(part, half, width)
+    halved = width // 2
+    for distance, ref, here, there in (
+        (0, own_ref, near_here_ref, near_there_ref),
+        (1, one_ref, far_here_ref, far_there_ref),
+    ):
+        place = lax.rem(row, 2) ^ distance
+        update = module[:, pl.ds(pl.multiple_of(place * local_rows, local_rows), local_rows), :]
+        result = rounded(widened(ref[0:part_rows, :]) + update.reshape(part_rows, width))
+        low, high = result[:, :halved], result[:, halved:]
+        here[...] = jnp.where(branch == 0, low, high)
+        there[...] = jnp.where(branch == 0, high, low)
+
+
+def place_kernel(own_ref, branch_ref, row_ref, both_ref, output_ref):
+    rows = own_ref.shape[0]
+    branch = lax.axis_index("branch")
+    parity = lax.rem(lax.axis_index("row"), 2)
+    for flip_branch, flip_row, ref in (
+        (0, 0, own_ref),
+        (1, 0, branch_ref),
+        (0, 1, row_ref),
+        (1, 1, both_ref),
+    ):
+        unit = 2 * (branch ^ flip_branch) + (parity ^ flip_row)
+        output_ref[pl.ds(pl.multiple_of(unit * rows, rows), rows), :] = ref[...]
+
+
+def pair_kernel(
+    sizes, pair_refs, weight_refs, gain_ref, transition_gain_ref, outer_weight_ref, seq_total,
+    output_ref, rows, columns, gates, outer, outer_flat, ordered, final,
+):
+    sequences, local_rows, residues, chan_local, outer_width = sizes
+    half = residues // 2
+    row = lax.axis_index("row")
+    branch = lax.axis_index("branch")
+    seq = lax.axis_index("seq")
+    width = 4 * chan_local
+    chan = chan_local
+    for distance, pair_ref, weight_ref in zip((0, 2, 1, 3), pair_refs, weight_refs):
+        place = pl.ds(pl.multiple_of((seq ^ distance) * chan, chan), chan)
+        rows[place, :] = pair_ref[pl.ds(pl.multiple_of(row * chan, chan), chan), :]
+        for k in range(2):
+            start = pl.multiple_of((2 * branch + k) * chan, chan)
+            columns[k, place, :] = pair_ref[pl.ds(start, chan), :]
+        gates[place, :] = weight_ref[4 * chan : 5 * chan, :]
+
+    def projection(values, kind):
+        weights = jnp.concatenate([w[kind * chan : (kind + 1) * chan, :] for w in weight_refs], axis=0)
+        return product(values, weights, 1, 1)
+
+    raw = widened(rows[...])
+    row_input = rounded((layer_normalize(raw, 0) * gain_ref[...]).T)
+    left = widened(
+        rounded(projection(row_input, 0) * jax.nn.sigmoid(projection(row_input, 1)))
+    ).reshape(local_rows, residues, width)
+    right = []
+    for k in range(2):
+        column_input = rounded((layer_normalize(widened(columns[k]), 0) * gain_ref[...]).T)
+        right.append(
+            widened(
+                rounded(projection(column_input, 2) * jax.nn.sigmoid(projection(column_input, 3)))
+            ).reshape(local_rows, residues, width)
+        )
+    right = jnp.concatenate(right, axis=0)
+    triangle = jnp.concatenate(
+        [jnp.sum(left[i][None] * right, axis=1) for i in range(local_rows)], axis=0
+    )
+    triangle = widened(rounded(triangle))
+    tri_norm = rounded(layer_normalize(triangle, 1))
+    output_weight = jnp.concatenate([w[5 * chan : 6 * chan, :] for w in weight_refs], axis=0)
+    tri_out = product(tri_norm, output_weight)
+    ordered[...] = raw.T.reshape(local_rows, residues, width)
+    place = pl.ds(pl.multiple_of(branch * half, half), half)
+    raw_here = ordered[:, place, :].reshape(local_rows * half, width)
+    ordered[...] = widened(row_input).reshape(local_rows, residues, width)
+    input_here = rounded(ordered[:, place, :].reshape(local_rows * half, width))
+    gate = jax.nn.sigmoid(product(input_here, gates[...], 1, 1))
+    first_update = widened(rounded(raw_here + gate * tri_out))
+    trans_norm = rounded(layer_normalize(first_update, 1) * transition_gain_ref[...])
+    down = jnp.zeros((local_rows * half, width), jnp.float32)
+    at = 6 * chan
+    hidden_local = (weight_refs[0].shape[0] - at - 2 * sequences) // 2
+    for w in weight_refs:
+        hidden = rounded(jax.nn.relu(product(trans_norm, w[at : at + hidden_local, :], 1, 1)))
+        down += product(hidden, w[at + hidden_local : at + hidden_local + width, :], 1, 1)
+    pair_next = widened(rounded(first_update + down))
+
+    at = at + 2 * hidden_local
+    lefts = jnp.concatenate(
+        [
+            jnp.concatenate([w[at : at + sequences, :], w[at + sequences : at + 2 * sequences, :]], axis=1)
+            for w in weight_refs
+        ],
+        axis=0,
+    )
+    base = 4 * chan
+    rights = jnp.concatenate(
+        [
+            jnp.concatenate([p[base : base + sequences, :], p[base + sequences :, :]], axis=1)
+            for p in pair_refs
+        ],
+        axis=0,
+    )
+    outer_all = product(rounded(widened(lefts).T), rights)
+    each = 128 // outer_width
+    for tile in range(half // each):
+        outer[tile] = outer_all[:, tile * 128 : (tile + 1) * 128]
+        for c in range(outer_width):
+            strip = outer[tile, pl.ds(c, local_rows, stride=outer_width), :]
+            for k in range(each):
+                j = tile * each + k
+                outer_flat[
+                    j * local_rows : (j + 1) * local_rows, c * outer_width : (c + 1) * outer_width
+                ] = strip[:, k * outer_width : (k + 1) * outer_width]
+    final[...] = product(rounded(outer_flat[...]), outer_weight_ref[...]) * (1.0 / seq_total)
+    outer_update = jnp.concatenate(
+        [final[pl.ds(i, half, stride=local_rows), :] for i in range(local_rows)], axis=0
+    )
+    outer_update = widened(rounded(outer_update))
+    final[...] = (pair_next + outer_update).T
+    output_ref[...] = rounded(final[pl.ds(pl.multiple_of(seq * chan, chan), chan), :])
+
+
+def compact_shards(
+    alignment_input, pairwise_input, alignment_gain, product_gain, attention_weight, mixing_weight,
+    outer_input_weight, outer_output_weight, bias_matrix, pairwise_gain, triangle_input_weight,
+    triangle_gate_weight, triangle_gain, triangle_output_weight, transition_gain,
+    transition_up_weight, transition_down_weight,
+):
+    sequences, local_rows, width = alignment_input.shape
+    chan_local, _, residues = pairwise_input.shape
+    pair_width, groups = bias_matrix.shape
+    heads = mixing_weight.shape[0]
+    outer_width = outer_input_weight.shape[2]
+    part = sequences // 4
+    part_rows = part * local_rows
+    half = residues // 2
+    sizes = (sequences, local_rows, residues, chan_local, outer_width)
+    half_type, full_type = jnp.bfloat16, jnp.float32
+
+    def shape(*dims, dtype=half_type):
+        return jax.ShapeDtypeStruct(dims, dtype)
+
+    rows_flat = alignment_input.reshape(sequences * local_rows, width)
+    message_rows = part_rows + chan_local + sequences
+    same, other, left = kernel_call(
+        functools.partial(send_kernel, sizes),
+        [shape(message_rows, width), shape(message_rows, width), shape(sequences, local_rows * outer_width)],
+        [rows_flat, pairwise_input, product_gain[None], outer_input_weight.reshape(width, 2 * outer_width)],
+        [pltpu.VMEM((sequences * local_rows, 128), full_type)],
+    )
+    from_three = exchange(other, "row", 3)
+    from_two = exchange(same, "row", 2)
+    from_one = exchange(other, "row", 1)
+    received = (same, from_one, from_two, from_three)
+
+    packed_rows = 6 * chan_local + transition_up_weight.shape[0] + transition_down_weight.shape[0] + 2 * sequences
+    (packed,) = kernel_call(
+        weight_kernel,
+        [shape(packed_rows, pair_width)],
+        [left, triangle_input_weight, triangle_gate_weight, triangle_gain[None],
+         triangle_output_weight, transition_up_weight, transition_down_weight],
+    )
+    packed_x = exchange(packed, "seq", 2)
+    packed_core = exchange(packed, "seq", 1)
+    packed_both = exchange(packed_x, "seq", 1)
+    weights = (packed, packed_x, packed_core, packed_both)
+
+    (relay,) = kernel_call(
+        functools.partial(relay_kernel, sizes),
+        [shape(4 * chan_local + 2 * sequences, width)],
+        list(received),
+    )
+    relay_x = exchange(relay, "seq", 2)
+    relay_core = exchange(relay, "seq", 1)
+    relay_both = exchange(relay_x, "seq", 1)
+    relays = (relay, relay_x, relay_core, relay_both)
+
+    scores, values, gate = kernel_call(
+        functools.partial(score_kernel, sizes),
+        [shape(part * half, groups * residues, dtype=full_type), shape(part * residues, heads), shape(part * half, heads)],
+        [*received, alignment_gain[None], attention_weight.reshape(width, 4 * heads)],
+        [pltpu.VMEM((part, residues, width), full_type)],
+    )
+
+    def mix_body(*refs):
+        mix_kernel(sizes, refs[:4], *refs[4:])
+
+    near_here, near_there, far_here, far_there = kernel_call(
+        mix_body,
+        [shape(part_rows, width // 2)] * 4,
+        [*relays, scores, values, gate, bias_matrix.T, mixing_weight, same, from_one],
+        [
+            pltpu.VMEM((2, pair_width, local_rows * residues), half_type),
+            pltpu.VMEM((half, groups * residues), full_type),
+            pltpu.VMEM((part, half, width), full_type),
+        ],
+    )
+    axes = ("branch", "row")
+    across = lax.axis_size("row")
+    from_branch = exchange(near_there, axes, across)
+    from_both = exchange(far_there, axes, across + 1)
+    from_row = exchange(far_here, axes, 1)
+
+    def pair_body(*refs):
+        pair_kernel(sizes, refs[:4], refs[4:8], *refs[8:11], sequences * 4, *refs[11:])
+
+    (pair_flat,) = kernel_call(
+        pair_body,
+        [shape(chan_local, local_rows * half)],
+        [*relays, *weights, pairwise_gain[:, None], transition_gain[None],
+         outer_output_weight.reshape(outer_width * outer_width, pair_width)],
+        [
+            pltpu.VMEM((pair_width, local_rows * residues), half_type),
+            pltpu.VMEM((2, pair_width, local_rows * residues), half_type),
+            pltpu.VMEM((pair_width, pair_width), half_type),
+            pltpu.VMEM((half * outer_width // 128, local_rows * outer_width, 128), full_type),
+            pltpu.VMEM((local_rows * half, outer_width * outer_width), full_type),
+            pltpu.VMEM((local_rows, residues, pair_width), full_type),
+            pltpu.VMEM((local_rows * half, pair_width), full_type),
+        ],
+    )
+    (alignment_flat,) = kernel_call(
+        place_kernel,
+        [shape(sequences * local_rows, width // 2)],
+        [near_here, from_branch, from_row, from_both],
+    )
+    return (
+        alignment_flat.reshape(sequences, local_rows, width // 2),
+        pair_flat.reshape(chan_local, local_rows, half),
+    )
+
+
+def is_compact(mesh, residues):
+    return mesh.shape["row"] == 4 and mesh.shape["seq"] == 4 and mesh.shape["branch"] == 2
+
+
 def solution(mesh):
     return jax.shard_map(
-        shards,
+        compact_shards if is_compact(mesh, None) else shards,
         mesh=mesh,
         in_specs=(
             P("seq", "row", None),

time: 190 us -> 39.2 us (0.21)
  waiting for transfers between devices: 72.6 us -> 13.7 us
  blocking collectives: 45 us -> 0 us
  local copies, waits for them, and re-layouts: 27.3 us -> 6.24 us
  matrix products: 16.8 us -> 0 us
  between operations: 15.8 us -> 0.82 us
  starting transfers between devices: 2.81 us -> 12 us
  other arithmetic: 8.34 us -> 0 us
  Pallas kernels: 0 us -> 6.15 us
    all_gather x4 -> x0, blocking collectives: 39.2 us -> none  [the longest x2 13.2 us: full_channels(): return lax.all_gather(values, 'seq', axis=0, tiled=True)]
    unnamed x5 -> x0, waiting for transfers between devices: 34.4 us -> none
    all_gather x1 -> x0, waiting for transfers between devices: 26.3 us -> none  [shards(): shard_part = lax.all_gather(key_values, 'row', axis=2, tiled=True)]
    dot_general x11 -> x0, matrix products: 16.8 us -> none  [the longest x1 3.63 us: fold_real(): jnp.einsum('shid,shdj->shij', query_heads, keys_part, preferred_element_t...]
    another operation x10 -> x0, local copies, waits for them, and re-layouts: 10.9 us -> none
    ppermute x3 -> x12, starting transfers between devices: 2.69 us -> 12 us  [exchange(): lax.ppermute(value, axes, [(i, i ^ distance) for i in range(members)])]
    pallas_call x0 -> x7, Pallas kernels: none -> 6.15 us  [kernel_call(): pl.pallas_call(body, out_shape=outputs, in_specs=[vmem] * len(operands),...]
    slice x1 -> x0, local copies, waits for them, and re-layouts: 6 us -> none  [fold_real(): shard_part[:, latent_heads:]]
  transfers between devices with their start and end apart: 6 -> 12, of which waited for: 4 -> 5; matrix products, arithmetic and copies ran while one was open for 3% -> 3% of each run, Pallas kernels for 0% -> 13%
where the time goes in v1:
time: 39.2 us; the launch traced here: 38.9 us
  waiting for transfers between devices  13.7 us (35%)
  starting transfers between devices  12 us (31%)
  local copies, waits for them, and re-layouts  6.24 us (16%)
  Pallas kernels  6.15 us (16%)
  between operations  0.82 us (2%)
    ppermute x12, waiting for transfers between devices, exchange(): lax.ppermute(value, axes, [(i, i ^ distance) for i in range(members)])  13.7 us
    ppermute x12, starting transfers between devices, exchange(): lax.ppermute(value, axes, [(i, i ^ distance) for i in range(members)])  12 us
    pallas_call x7, Pallas kernels, kernel_call(): pl.pallas_call(body, out_shape=outputs, in_specs=[vmem] * len(operands),...  6.15 us
    unnamed x34, local copies, waits for them, and re-layouts  4.49 us
    reshape x1, local copies, waits for them, and re-layouts, compact_shards(): outer_input_weight.reshape(width, 2 * outer_width)  0.9 us
  transfers between devices with their start and end apart: 12, of which 5 were waited for; matrix products, arithmetic and copies ran while one was open for 3% of the time, Pallas kernels for 13%

profile of v1, /device:TPU:0, one launch (start us, length us, event | category | flops | bytes accessed | tf_op | source)
XLA Modules:
  0.0 38.9 jit_solution(1754509634409400672)
XLA Ops:
  0.6 0.9 %copy.23.weight_ref = bf16[256,64]{1,0:T(8,128)(2,1)S(1)} copy(bf16[256,64]{0,1:T(8,128)(2,1)} %bitcast.23) | data formatting | bytes 65536 | tf_op jit(solution)/shard_map/reshape | solution.py:676
  1.5 0.0 copy-start.9
  1.6 0.7 %copy-done.9 = f32[256]{0:T(256)S(1)} copy-done((f32[256]{0:T(256)S(1)}, f32[256]{0:T(256)}, u32[]{:S(2)}) %copy-start.9) | copy-done | bytes 1048
  2.2 0.9 %copy-done = bf16[64,8,256]{2,1,0:T(8,128)(2,1)S(1)} copy-done((bf16[64,8,256]{2,1,0:T(8,128)(2,1)S(1)}, bf16[64,8,256]{2,1,0:T(8,128)(2,1)}, u32[]{:S(2)}) %copy-start) | copy-done | bytes 262168
  3.2 0.5 %shard_map.176 = (bf16[224,256]{1,0:T(8,128)(2,1)S(1)}, bf16[224,256]{1,0:T(8,128)(2,1)S(1)}, bf16[64,256]{1,0:T(8,128)(2,1)S(1)}) custom-call(bf16[512,256]{1,0:T(8,128)(2,1)S(1)} %bitcast.14, bf16[32,8,32]{2,1,0:T(8,128)(2,1)S(1)} %copy-done.3, f32[1,256]{1,0:T(1,128)S(1)} %bitcast.17, bf16[256,64]{1,0:T(8,128)(2,1)S(1)} %copy.23.weight_ref), custom_call_target="tpu_custom_call" | custom-call | bytes 574464 | tf_op jit(solution)/shard_map/pallas_call | solution.py:366
  3.7 5.1 %collective-permute-start.2 = (bf16[224,256]{1,0:T(8,128)(2,1)S(1)}, bf16[224,256]{1,0:T(8,128)(2,1)S(1)}, u32[]{:S(2)}, u32[]{:S(2)}) collective-permute-start(bf16[224,256]{1,0:T(8,128)(2,1)S(1)} %get-tuple-element.13), channel_id=1, source_target_pairs={{0,12},{4,8},{8,4},{12,0},{1,13},{5,9},{9,5},{13,1},{2,14},{6,10},... | collective-permute-start | bytes 344072 | tf_op jit(solution)/shard_map/ppermute | solution.py:379
  8.9 0.0 collective-permute-start
  8.9 0.6 %collective-permute-start.1 = (bf16[224,256]{1,0:T(8,128)(2,1)S(1)}, bf16[224,256]{1,0:T(8,128)(2,1)S(1)}, u32[]{:S(2)}, u32[]{:S(2)}) collective-permute-start(bf16[224,256]{1,0:T(8,128)(2,1)S(1)} %get-tuple-element.12.own_ref.refs_9_), channel_id=1, source_target_pairs={{0,8},{4,12},{8,0},{12,4},{1,9},{5,13},{9,1},{13,5},{2,10},{6,14},... | collective-permute-start | bytes 344072 | tf_op jit(solution)/shard_map/ppermute | solution.py:379
  9.5 0.1 copy.24.output_ref
  9.6 0.0 copy-start.5
  9.6 0.0 copy-start.6
  9.7 3.2 %collective-permute-done.2.three_ref = bf16[224,256]{1,0:T(8,128)(2,1)S(1)} collective-permute-done((bf16[224,256]{1,0:T(8,128)(2,1)S(1)}, bf16[224,256]{1,0:T(8,128)(2,1)S(1)}, u32[]{:S(2)}, u32[]{:S(2)}) %collective-permute-start.2) | collective-permute-done | bytes 114720 | tf_op jit(solution)/shard_map/ppermute | solution.py:379
  12.9 2.7 %collective-permute-done.one_ref.refs_10_ = bf16[224,256]{1,0:T(8,128)(2,1)S(1)} collective-permute-done((bf16[224,256]{1,0:T(8,128)(2,1)S(1)}, bf16[224,256]{1,0:T(8,128)(2,1)S(1)}, u32[]{:S(2)}, u32[]{:S(2)}) %collective-permute-start) | collective-permute-done | bytes 114720 | tf_op jit(solution)/shard_map/ppermute | solution.py:379
  15.5 3.0 %collective-permute-done.1.two_ref = bf16[224,256]{1,0:T(8,128)(2,1)S(1)} collective-permute-done((bf16[224,256]{1,0:T(8,128)(2,1)S(1)}, bf16[224,256]{1,0:T(8,128)(2,1)S(1)}, u32[]{:S(2)}, u32[]{:S(2)}) %collective-permute-start.1) | collective-permute-done | bytes 114720 | tf_op jit(solution)/shard_map/ppermute | solution.py:379
  18.6 1.6 %collective-permute-start.3 = (bf16[256,256]{1,0:T(8,128)(2,1)S(1)}, bf16[256,256]{1,0:T(8,128)(2,1)S(1)}, u32[]{:S(2)}, u32[]{:S(2)}) collective-permute-start(bf16[256,256]{1,0:T(8,128)(2,1)S(1)} %shard_map.177.refs_0_), channel_id=1, source_target_pairs={{0,2},{1,3},{2,0},{3,1},{4,6},{5,7},{6,4},{7,5},{8,10},{9,11},{10,... | collective-permute-start | bytes 393224 | tf_op jit(solution)/shard_map/ppermute | solution.py:379
  20.1 0.0 copy-done.7
  20.2 0.6 %copy-done.11 = f32[32]{0:T(128)S(1)} copy-done((f32[32]{0:T(128)S(1)}, f32[32]{0:T(128)}, u32[]{:S(2)}) %copy-start.11) | copy-done | bytes 152
  20.8 0.1 shard_map.181.refs_4_
  20.8 0.6 %collective-permute-start.9 = (bf16[576,128]{1,0:T(8,128)(2,1)S(1)}, bf16[576,128]{1,0:T(8,128)(2,1)S(1)}, u32[]{:S(2)}, u32[]{:S(2)}) collective-permute-start(bf16[576,128]{1,0:T(8,128)(2,1)S(1)} %shard_map.181.refs_4_), channel_id=1, source_target_pairs={{0,2},{1,3},{2,0},{3,1},{4,6},{5,7},{6,4},{7,5},{8,10},{9,11},{10,... | collective-permute-start | bytes 442376 | tf_op jit(solution)/shard_map/ppermute | solution.py:379
  21.4 0.0 collective-permute-start.4
  21.4 3.5 %collective-permute-done.3.refs_1_ = bf16[256,256]{1,0:T(8,128)(2,1)S(1)} collective-permute-done((bf16[256,256]{1,0:T(8,128)(2,1)S(1)}, bf16[256,256]{1,0:T(8,128)(2,1)S(1)}, u32[]{:S(2)}, u32[]{:S(2)}) %collective-permute-start.3) | collective-permute-done | bytes 131104 | tf_op jit(solution)/shard_map/ppermute | solution.py:379
  24.9 0.0 collective-permute-start.5
  24.9 0.5 %collective-permute-start.10 = (bf16[576,128]{1,0:T(8,128)(2,1)S(1)}, bf16[576,128]{1,0:T(8,128)(2,1)S(1)}, u32[]{:S(2)}, u32[]{:S(2)}) collective-permute-start(bf16[576,128]{1,0:T(8,128)(2,1)S(1)} %shard_map.181.refs_4_), channel_id=1, source_target_pairs={{0,1},{1,0},{2,3},{3,2},{4,5},{5,4},{6,7},{7,6},{8,9},{9,8},{10,11... | collective-permute-start | bytes 442376 | tf_op jit(solution)/shard_map/ppermute | solution.py:379
  25.4 1.4 %collective-permute-done.9.refs_5_ = bf16[576,128]{1,0:T(8,128)(2,1)S(1)} collective-permute-done((bf16[576,128]{1,0:T(8,128)(2,1)S(1)}, bf16[576,128]{1,0:T(8,128)(2,1)S(1)}, u32[]{:S(2)}, u32[]{:S(2)}) %collective-permute-start.9) | collective-permute-done | bytes 147488 | tf_op jit(solution)/shard_map/ppermute | solution.py:379
  26.8 0.0 collective-permute-start.11
  26.8 0.1 copy.27
  26.9 0.0 copy-start.10
  26.9 0.7 %copy-done.10 = f32[256]{0:T(256)S(1)} copy-done((f32[256]{0:T(256)S(1)}, f32[256]{0:T(256)}, u32[]{:S(2)}) %copy-start.10) | copy-done | bytes 1048
  27.6 1.1 %shard_map.178 = (f32[256,256]{1,0:T(8,128)S(1)}, bf16[512,256]{1,0:T(8,128)(2,1)S(1)}, bf16[256,256]{1,0:T(8,128)(2,1)S(1)}) custom-call(bf16[224,256]{1,0:T(8,128)(2,1)S(1)} %get-tuple-element.12.own_ref.refs_9_, bf16[224,256]{1,0:T(8,128)(2,1)S(1)} %collective-permute-done.one_ref.refs_10_, bf16[224,256]{1,0:T(8,128)(2,1)S(1)} %collective-permute-done.1.two_ref, ...), custom_call_target="tpu_custom_call" | custom-call | bytes 1639424 | tf_op jit(solution)/shard_map/pallas_call | solution.py:366
  28.6 0.0 collective-permute-done.4.refs_2_
  28.6 0.0 collective-permute-done.5.refs_3_
  28.6 0.0 copy-start.8
  28.7 0.7 %copy-done.8 = bf16[128,8]{0,1:T(8,128)(2,1)S(1)} copy-done((bf16[128,8]{0,1:T(8,128)(2,1)S(1)}, bf16[128,8]{0,1:T(8,128)(2,1)}, u32[]{:S(2)}) %copy-start.8) | copy-done | bytes 2072
  29.3 1.6 %shard_map.179 = (bf16[128,128]{1,0:T(8,128)(2,1)S(1)}, bf16[128,128]{1,0:T(8,128)(2,1)S(1)}, bf16[128,128]{1,0:T(8,128)(2,1)S(1)}, bf16[128,128]{1,0:T(8,128)(2,1)S(1)}) custom-call(bf16[256,256]{1,0:T(8,128)(2,1)S(1)} %shard_map.177.refs_0_, bf16[256,256]{1,0:T(8,128)(2,1)S(1)} %collective-permute-done.3.refs_1_, ...), custom_call_target="tpu_custom_call" | custom-call | bytes 1673216 | tf_op jit(solution)/shard_map/pallas_call | solution.py:366
  30.9 1.6 %collective-permute-start.6 = (bf16[128,128]{1,0:T(8,128)(2,1)S(1)}, bf16[128,128]{1,0:T(8,128)(2,1)S(1)}, u32[]{:S(2)}, u32[]{:S(2)}) collective-permute-start(bf16[128,128]{1,0:T(8,128)(2,1)S(1)} %get-tuple-element.18), channel_id=1, source_target_pairs={{0,16},{4,20},{8,24},{12,28},{16,0},{20,4},{24,8},{28,12},{1,17},{... | collective-permute-start | bytes 98312 | tf_op jit(solution)/shard_map/ppermute | solution.py:379
  32.5 0.0 collective-permute-start.7
  32.5 2.0 %collective-permute-start.8 = (bf16[128,128]{1,0:T(8,128)(2,1)S(1)}, bf16[128,128]{1,0:T(8,128)(2,1)S(1)}, u32[]{:S(2)}, u32[]{:S(2)}) collective-permute-start(bf16[128,128]{1,0:T(8,128)(2,1)S(1)} %get-tuple-element.20), channel_id=1, source_target_pairs={{0,20},{4,16},{8,28},{12,24},{16,4},{20,0},{24,12},{28,8},{1,21},{... | collective-permute-start | bytes 98312 | tf_op jit(solution)/shard_map/ppermute | solution.py:379
  34.5 0.1 copy.25.refs_8_
  34.6 0.0 collective-permute-done.10.refs_6_
  34.6 0.0 collective-permute-done.11.refs_7_
  34.6 0.0 copy-start.12
  34.6 0.6 %copy-done.12 = f32[128]{0:T(128)S(1)} copy-done((f32[128]{0:T(128)S(1)}, f32[128]{0:T(128)}, u32[]{:S(2)}) %copy-start.12) | copy-done | bytes 536
  35.3 2.2 %shard_map.182 = bf16[32,128]{1,0:T(8,128)(2,1)S(1)} custom-call(bf16[256,256]{1,0:T(8,128)(2,1)S(1)} %shard_map.177.refs_0_, bf16[256,256]{1,0:T(8,128)(2,1)S(1)} %collective-permute-done.3.refs_1_, bf16[256,256]{1,0:T(8,128)(2,1)S(1)} %collective-permute-done.4.refs_2_, bf16[256,256]{1,0:T(8,128)(2,1)S(1)} %collective-permute-done.5.refs_3_, ...), custom_call_target="tpu_custom_call" | custom-call | bytes 1385472 | tf_op jit(solution)/shard_map/pallas_call | solution.py:366
  37.5 0.7 %copy.26 = bf16[32,128]{0,1:T(8,128)(2,1)} copy(bf16[32,128]{1,0:T(8,128)(2,1)S(1)} %shard_map.182) | data formatting | bytes 16384 | tf_op jit(solution)/shard_map/pallas_call | solution.py:366
  38.2 0.0 collective-permute-done.6.branch_ref
  38.2 0.0 collective-permute-done.7.row_ref
  38.2 0.0 collective-permute-done.8.both_ref
  38.2 0.7 %shard_map.180 = bf16[512,128]{1,0:T(8,128)(2,1)} custom-call(bf16[128,128]{1,0:T(8,128)(2,1)S(1)} %get-tuple-element.17.own_ref, bf16[128,128]{1,0:T(8,128)(2,1)S(1)} %collective-permute-done.6.branch_ref, bf16[128,128]{1,0:T(8,128)(2,1)S(1)} %collective-permute-done.7.row_ref, bf16[128,128]{1,0:T(8,128)(2,1)S(1)} %collective-permute-done.8.both_ref), custom_call_target="tpu_custom_call" | custom-call | bytes 262144 | tf_op jit(solution)/shard_map/pallas_call | solution.py:366
  (20 shorter events, 0.1 us)
Async XLA Ops:
  0.6 0.9 %copy-start.3 = (bf16[32,8,32]{2,1,0:T(8,128)(2,1)S(1)}, bf16[32,8,32]{2,1,0:T(8,128)(2,1)}, u32[]{:S(2)}) copy-start(bf16[32,8,32]{2,1,0:T(8,128)(2,1)} %pair_ref.1) | copy-start | bytes 49156
  1.5 0.7 %copy-start.9 = (f32[256]{0:T(256)S(1)}, f32[256]{0:T(256)}, u32[]{:S(2)}) copy-start(f32[256]{0:T(256)} %param.20) | copy-start | bytes 3076
  2.2 0.9 %copy-start = (bf16[64,8,256]{2,1,0:T(8,128)(2,1)S(1)}, bf16[64,8,256]{2,1,0:T(8,128)(2,1)}, u32[]{:S(2)}) copy-start(bf16[64,8,256]{2,1,0:T(8,128)(2,1)} %param.17) | copy-start | bytes 786436
  3.2 6.3 %copy-start.14 = (bf16[128,32]{0,1:T(8,128)(2,1)S(1)}, bf16[128,32]{0,1:T(8,128)(2,1)}, u32[]{:S(2)}) copy-start(bf16[128,32]{0,1:T(8,128)(2,1)} %param.30) | copy-start | bytes 24580
  3.7 23.0 %copy-start.13 = (bf16[256,4,256]{2,1,0:T(4,128)(2,1)S(1)}, bf16[256,4,256]{2,1,0:T(4,128)(2,1)}, u32[]{:S(2)}) copy-start(bf16[256,4,256]{2,1,0:T(4,128)(2,1)} %param.21) | copy-start | bytes 1572868
  3.7 9.1 %collective-permute-start.2 = (bf16[224,256]{1,0:T(8,128)(2,1)S(1)}, bf16[224,256]{1,0:T(8,128)(2,1)S(1)}, u32[]{:S(2)}, u32[]{:S(2)}) collective-permute-start(bf16[224,256]{1,0:T(8,128)(2,1)S(1)} %get-tuple-element.13), channel_id=1, source_target_pairs={{0,12},{4,8},{8,4},{12,0},{1,13},{5,9},{9,5},{13,1},{2,14},{6,10},... | collective-permute-start | bytes 344072 | tf_op jit(solution)/shard_map/ppermute | solution.py:379
  8.9 6.7 %collective-permute-start = (bf16[224,256]{1,0:T(8,128)(2,1)S(1)}, bf16[224,256]{1,0:T(8,128)(2,1)S(1)}, u32[]{:S(2)}, u32[]{:S(2)}) collective-permute-start(bf16[224,256]{1,0:T(8,128)(2,1)S(1)} %get-tuple-element.13), channel_id=1, source_target_pairs={{0,4},{4,0},{8,12},{12,8},{1,5},{5,1},{9,13},{13,9},{2,6},{6,2},{1... | collective-permute-start | bytes 344072 | tf_op jit(solution)/shard_map/ppermute | solution.py:379
  8.9 9.7 %collective-permute-start.1 = (bf16[224,256]{1,0:T(8,128)(2,1)S(1)}, bf16[224,256]{1,0:T(8,128)(2,1)S(1)}, u32[]{:S(2)}, u32[]{:S(2)}) collective-permute-start(bf16[224,256]{1,0:T(8,128)(2,1)S(1)} %get-tuple-element.12.own_ref.refs_9_), channel_id=1, source_target_pairs={{0,8},{4,12},{8,0},{12,4},{1,9},{5,13},{9,1},{13,5},{2,10},{6,14},... | collective-permute-start | bytes 344072 | tf_op jit(solution)/shard_map/ppermute | solution.py:379
  9.6 10.5 %copy-start.4 = (bf16[4,32,128]{2,1,0:T(8,128)(2,1)S(1)}, bf16[4,32,128]{2,1,0:T(8,128)(2,1)}, u32[]{:S(2)}) copy-start(bf16[4,32,128]{2,1,0:T(8,128)(2,1)} %input_ref.1) | copy-start | bytes 98308
  9.6 10.5 %copy-start.5 = (bf16[128,128]{1,0:T(8,128)(2,1)S(1)}, bf16[128,128]{1,0:T(8,128)(2,1)}, u32[]{:S(2)}) copy-start(bf16[128,128]{1,0:T(8,128)(2,1)} %up_ref.1) | copy-start | bytes 98308
  9.6 10.5 %copy-start.6 = (bf16[128,128]{1,0:T(8,128)(2,1)S(1)}, bf16[128,128]{1,0:T(8,128)(2,1)}, u32[]{:S(2)}) copy-start(bf16[128,128]{1,0:T(8,128)(2,1)} %down_ref.1) | copy-start | bytes 98308
  18.5 1.6 %copy-start.7 = (bf16[32,128]{1,0:T(8,128)(2,1)S(1)}, bf16[32,128]{1,0:T(8,128)(2,1)}, u32[]{:S(2)}) copy-start(bf16[32,128]{1,0:T(8,128)(2,1)} %gate_ref.1) | copy-start | bytes 24580
  18.6 6.3 %collective-permute-start.3 = (bf16[256,256]{1,0:T(8,128)(2,1)S(1)}, bf16[256,256]{1,0:T(8,128)(2,1)S(1)}, u32[]{:S(2)}, u32[]{:S(2)}) collective-permute-start(bf16[256,256]{1,0:T(8,128)(2,1)S(1)} %shard_map.177.refs_0_), channel_id=1, source_target_pairs={{0,2},{1,3},{2,0},{3,1},{4,6},{5,7},{6,4},{7,5},{8,10},{9,11},{10,... | collective-permute-start | bytes 393224 | tf_op jit(solution)/shard_map/ppermute | solution.py:379
  20.1 0.7 %copy-start.11 = (f32[32]{0:T(128)S(1)}, f32[32]{0:T(128)}, u32[]{:S(2)}) copy-start(f32[32]{0:T(128)} %param.29) | copy-start | bytes 388
  20.8 5.9 %collective-permute-start.9 = (bf16[576,128]{1,0:T(8,128)(2,1)S(1)}, bf16[576,128]{1,0:T(8,128)(2,1)S(1)}, u32[]{:S(2)}, u32[]{:S(2)}) collective-permute-start(bf16[576,128]{1,0:T(8,128)(2,1)S(1)} %shard_map.181.refs_4_), channel_id=1, source_target_pairs={{0,2},{1,3},{2,0},{3,1},{4,6},{5,7},{6,4},{7,5},{8,10},{9,11},{10,... | collective-permute-start | bytes 442376 | tf_op jit(solution)/shard_map/ppermute | solution.py:379
  21.4 7.2 %collective-permute-start.4 = (bf16[256,256]{1,0:T(8,128)(2,1)S(1)}, bf16[256,256]{1,0:T(8,128)(2,1)S(1)}, u32[]{:S(2)}, u32[]{:S(2)}) collective-permute-start(bf16[256,256]{1,0:T(8,128)(2,1)S(1)} %shard_map.177.refs_0_), channel_id=1, source_target_pairs={{0,1},{1,0},{2,3},{3,2},{4,5},{5,4},{6,7},{7,6},{8,9},{9,8},{10,11... | collective-permute-start | bytes 393224 | tf_op jit(solution)/shard_map/ppermute | solution.py:379
  24.9 3.7 %collective-permute-start.5 = (bf16[256,256]{1,0:T(8,128)(2,1)S(1)}, bf16[256,256]{1,0:T(8,128)(2,1)S(1)}, u32[]{:S(2)}, u32[]{:S(2)}) collective-permute-start(bf16[256,256]{1,0:T(8,128)(2,1)S(1)} %collective-permute-done.3.refs_1_), channel_id=1, source_target_pairs={{0,1},{1,0},{2,3},{3,2},{4,5},{5,4},{6,7},{7,6},{8,9},{9,8},{10,11... | collective-permute-start | bytes 393224 | tf_op jit(solution)/shard_map/ppermute | solution.py:379
  24.9 9.7 %collective-permute-start.10 = (bf16[576,128]{1,0:T(8,128)(2,1)S(1)}, bf16[576,128]{1,0:T(8,128)(2,1)S(1)}, u32[]{:S(2)}, u32[]{:S(2)}) collective-permute-start(bf16[576,128]{1,0:T(8,128)(2,1)S(1)} %shard_map.181.refs_4_), channel_id=1, source_target_pairs={{0,1},{1,0},{2,3},{3,2},{4,5},{5,4},{6,7},{7,6},{8,9},{9,8},{10,11... | collective-permute-start | bytes 442376 | tf_op jit(solution)/shard_map/ppermute | solution.py:379
  26.8 7.8 %collective-permute-start.11 = (bf16[576,128]{1,0:T(8,128)(2,1)S(1)}, bf16[576,128]{1,0:T(8,128)(2,1)S(1)}, u32[]{:S(2)}, u32[]{:S(2)}) collective-permute-start(bf16[576,128]{1,0:T(8,128)(2,1)S(1)} %collective-permute-done.9.refs_5_), channel_id=1, source_target_pairs={{0,1},{1,0},{2,3},{3,2},{4,5},{5,4},{6,7},{7,6},{8,9},{9,8},{10,11... | collective-permute-start | bytes 442376 | tf_op jit(solution)/shard_map/ppermute | solution.py:379
  26.9 0.7 %copy-start.10 = (f32[256]{0:T(256)S(1)}, f32[256]{0:T(256)}, u32[]{:S(2)}) copy-start(f32[256]{0:T(256)} %param.19) | copy-start | bytes 3076
  27.6 1.1 %copy-start.2 = (bf16[256,256]{1,0:T(8,128)(2,1)S(1)}, bf16[256,256]{1,0:T(8,128)(2,1)}, u32[]{:S(2)}) copy-start(bf16[256,256]{1,0:T(8,128)(2,1)} %refs_8_.1) | copy-start | bytes 393220
  28.6 0.7 %copy-start.8 = (bf16[128,8]{0,1:T(8,128)(2,1)S(1)}, bf16[128,8]{0,1:T(8,128)(2,1)}, u32[]{:S(2)}) copy-start(bf16[128,8]{0,1:T(8,128)(2,1)} %param.25) | copy-start | bytes 6148
  29.3 5.3 %copy-start.1 = (bf16[32,32,128]{2,1,0:T(8,128)(2,1)S(1)}, bf16[32,32,128]{2,1,0:T(8,128)(2,1)}, u32[]{:S(2)}) copy-start(bf16[32,32,128]{2,1,0:T(8,128)(2,1)} %param.24) | copy-start | bytes 786436
  30.9 7.3 %collective-permute-start.6 = (bf16[128,128]{1,0:T(8,128)(2,1)S(1)}, bf16[128,128]{1,0:T(8,128)(2,1)S(1)}, u32[]{:S(2)}, u32[]{:S(2)}) collective-permute-start(bf16[128,128]{1,0:T(8,128)(2,1)S(1)} %get-tuple-element.18), channel_id=1, source_target_pairs={{0,16},{4,20},{8,24},{12,28},{16,0},{20,4},{24,8},{28,12},{1,17},{... | collective-permute-start | bytes 98312 | tf_op jit(solution)/shard_map/ppermute | solution.py:379
  32.5 5.7 %collective-permute-start.7 = (bf16[128,128]{1,0:T(8,128)(2,1)S(1)}, bf16[128,128]{1,0:T(8,128)(2,1)S(1)}, u32[]{:S(2)}, u32[]{:S(2)}) collective-permute-start(bf16[128,128]{1,0:T(8,128)(2,1)S(1)} %get-tuple-element.19), channel_id=1, source_target_pairs={{0,4},{4,0},{8,12},{12,8},{16,20},{20,16},{24,28},{28,24},{1,5},{5... | collective-permute-start | bytes 98312 | tf_op jit(solution)/shard_map/ppermute | solution.py:379
  32.5 2.0 %copy-start.15 = (f32[128]{0:T(128)S(1)}, f32[128]{0:T(128)}, u32[]{:S(2)}) copy-start(f32[128]{0:T(128)} %param.26) | copy-start | bytes 1540
  32.5 5.7 %collective-permute-start.8 = (bf16[128,128]{1,0:T(8,128)(2,1)S(1)}, bf16[128,128]{1,0:T(8,128)(2,1)S(1)}, u32[]{:S(2)}, u32[]{:S(2)}) collective-permute-start(bf16[128,128]{1,0:T(8,128)(2,1)S(1)} %get-tuple-element.20), channel_id=1, source_target_pairs={{0,20},{4,16},{8,28},{12,24},{16,4},{20,0},{24,12},{28,8},{1,21},{... | collective-permute-start | bytes 98312 | tf_op jit(solution)/shard_map/ppermute | solution.py:379
  34.6 0.7 %copy-start.12 = (f32[128]{0:T(128)S(1)}, f32[128]{0:T(128)}, u32[]{:S(2)}) copy-start(f32[128]{0:T(128)} %param.31) | copy-start | bytes 1540

commit v2 on v1

--- a/solution.py
+++ b/solution.py
@@ -321,6 +321,9 @@
     return (alignment_output, pairwise_output)
 
 
+BIAS_COST = 175 * 10**6
+
+
 def rounded(values):
     return values.astype(jnp.bfloat16)
 
@@ -359,18 +362,24 @@
     return row == column
 
 
-def kernel_call(body, outputs, operands, scratch=(), flops=0):
+def as_column(row):
+    size = row.shape[1]
+    return jnp.sum(jnp.where(same_group(size, size, 1), row, 0.0), axis=1, keepdims=True)
+
+
+def kernel_call(body, outputs, operands, scratch=(), flops=0, in_hbm=(), room=32 * 2**20):
     vmem = pl.BlockSpec(memory_space=pltpu.VMEM)
+    hbm = pl.BlockSpec(memory_space=pltpu.HBM)
     size = sum(a.size * a.dtype.itemsize for a in operands)
     size += sum(o.size * o.dtype.itemsize for o in outputs)
     return pl.pallas_call(
         body,
         out_shape=outputs,
-        in_specs=[vmem] * len(operands),
+        in_specs=[hbm if i in in_hbm else vmem for i in range(len(operands))],
         out_specs=[vmem] * len(outputs),
         scratch_shapes=list(scratch),
         cost_estimate=pl.CostEstimate(flops=flops, bytes_accessed=size, transcendentals=0),
-        compiler_params=pltpu.CompilerParams(vmem_limit_bytes=32 * 2**20),
+        compiler_params=pltpu.CompilerParams(vmem_limit_bytes=room),
     )(*operands)
 
 
@@ -379,66 +388,73 @@
     return lax.ppermute(value, axes, [(i, i ^ distance) for i in range(members)])
 
 
-def send_kernel(sizes, rows_ref, pair_ref, gain_ref, weight_ref, same_ref, other_ref, left_ref, wide):
+def start_kernel(token_ref):
+    token_ref[...] = jnp.zeros_like(token_ref)
+
+
+def send_kernel(
+    sizes, rows_ref, pair_ref, gain_ref, weight_ref, input_ref, gate_ref, tri_gain_ref, output_ref, up_ref,
+    down_ref, token_ref, same_ref, other_ref, shared_ref, flat_ref, wide,
+):
     sequences, local_rows, residues, chan_local, outer_width = sizes
     part = sequences // 4
     part_rows = part * local_rows
+    pair = widened(pair_ref[...])
+    flat_pair = rounded(jnp.concatenate([pair[:, i, :] for i in range(local_rows)], axis=1))
+    flat_ref[...] = flat_pair
+    shared_ref[0:chan_local, :] = flat_pair
+    at = chan_local + sequences
+    narrow = gate_ref.shape[1]
+    scaled = rounded(widened(output_ref[...]) * as_column(tri_gain_ref[...]))
+    kinds = [input_ref[kind] for kind in range(input_ref.shape[0])]
+    down = down_ref[...]
+    for block in (*kinds, gate_ref[...], scaled, down[:chan_local]):
+        shared_ref[at : at + chan_local, :narrow] = block
+        at += chan_local
+    at = chan_local + sequences
+    for block in (up_ref[...], down[chan_local:]):
+        shared_ref[at : at + block.shape[0], narrow:] = block
+        at += block.shape[0]
+    same_ref[part_rows : part_rows + chan_local, :] = flat_pair
+    other_ref[part_rows : part_rows + chan_local, :] = flat_pair
     unit_here = 2 * lax.axis_index("branch") + lax.rem(lax.axis_index("row"), 2)
     unit_other = 2 * lax.axis_index("branch") + 1 - lax.rem(lax.axis_index("row"), 2)
     same_ref[0:part_rows, :] = rows_ref[pl.ds(unit_here * part_rows, part_rows), :]
     other_ref[0:part_rows, :] = rows_ref[pl.ds(unit_other * part_rows, part_rows), :]
-    pair = widened(pair_ref[...])
-    flat_pair = rounded(jnp.concatenate([pair[:, i, :] for i in range(local_rows)], axis=1))
-    same_ref[part_rows : part_rows + chan_local, :] = flat_pair
-    other_ref[part_rows : part_rows + chan_local, :] = flat_pair
     normed = rounded(layer_normalize(widened(rows_ref[...]), 1) * gain_ref[...])
-    wide[:, 0 : 2 * outer_width] = product(normed, weight_ref[...])
+    wide[:, 0 : 2 * outer_width] = product(normed, weight_ref[...], 1, 1)
     base = part_rows + chan_local
     for i in range(local_rows):
         both = rounded(wide[pl.ds(i, sequences, stride=local_rows), :])
         lanes = slice(i * outer_width, (i + 1) * outer_width)
-        left_ref[:, lanes] = both[:, :outer_width]
+        shared_ref[chan_local : chan_local + sequences, lanes] = both[:, :outer_width]
         same_ref[base : base + sequences, lanes] = both[:, outer_width : 2 * outer_width]
     other_ref[base : base + sequences, :] = same_ref[base : base + sequences, :]
 
 
-def weight_kernel(left_ref, input_ref, gate_ref, gain_ref, output_ref, up_ref, down_ref, packed_ref):
-    at = 0
-    kinds, tri_local, _ = input_ref.shape
-    for kind in range(kinds):
-        packed_ref[at : at + tri_local, :] = input_ref[kind]
-        at += tri_local
-    packed_ref[at : at + gate_ref.shape[0], :] = gate_ref[...]
-    at += gate_ref.shape[0]
-    scaled = widened(output_ref[...]) * gain_ref[...]
-    packed_ref[at : at + tri_local, :] = rounded(scaled.T)
-    at += tri_local
-    for ref in (up_ref, down_ref):
-        packed_ref[at : at + ref.shape[0], :] = ref[...]
-        at += ref.shape[0]
-    sequences = left_ref.shape[0]
-    for start in (0, 128):
-        packed_ref[at : at + sequences, :] = left_ref[:, start : start + 128]
-        at += sequences
-
-
-def relay_kernel(sizes, own_ref, one_ref, two_ref, three_ref, relay_ref):
+def keep_kernel(*refs):
+    count = len(refs) // 2
+    for source, target in zip(refs[:count], refs[count:]):
+        target[...] = source[...]
+
+
+def relay_kernel(sizes, own_ref, one_ref, two_ref, three_ref, after_bias_ref, after_keep_ref, relay_ref):
     sequences, local_rows, residues, chan_local, outer_width = sizes
     part_rows = sequences // 4 * local_rows
     row = lax.axis_index("row")
     branch = lax.axis_index("branch")
     base = part_rows + chan_local
-    shard_total = 4
     for distance, ref in enumerate((own_ref, one_ref, two_ref, three_ref)):
         shard = row ^ distance
-        relay_ref[pl.ds(pl.multiple_of(shard * chan_local, chan_local), chan_local), :] = ref[
-            part_rows:base, :
-        ]
 
         @pl.when(shard // 2 == branch)
         def _():
-            start = shard_total * chan_local + lax.rem(shard, 2) * sequences
-            relay_ref[pl.ds(pl.multiple_of(start, sequences), sequences), :] = ref[
+            place = lax.rem(shard, 2)
+            relay_ref[pl.ds(pl.multiple_of(place * chan_local, chan_local), chan_local), :] = ref[
+                part_rows:base, :
+            ]
+            start = 2 * chan_local + place * sequences
+            relay_ref[pl.ds(pl.multiple_of(start, chan_local), sequences), :] = ref[
                 base : base + sequences, :
             ]
 
@@ -479,9 +495,28 @@
         )
 
 
+def bias_kernel(chan_local, pair_refs, matrix_ref, bias_ref, full, flat):
+    groups = matrix_ref.shape[0]
+    residues = flat.shape[1] // groups
+    local_rows = flat.shape[0]
+    seq = lax.axis_index("seq")
+    for distance, ref in zip((0, 2, 1, 3), pair_refs):
+        place = pl.ds(pl.multiple_of((seq ^ distance) * chan_local, chan_local), chan_local)
+        full[place, :] = widened(ref[0:chan_local, :])
+    plain = rounded(layer_normalize(full[...], 0))
+    bias = product(matrix_ref[...], plain)
+    for i in range(local_rows):
+        for h in range(groups):
+            flat[i : i + 1, h * residues : (h + 1) * residues] = bias[
+                h : h + 1, i * residues : (i + 1) * residues
+            ]
+    rows = rounded(flat[...])
+    bias_ref[...] = jnp.concatenate([rows, rows], axis=0)
+
+
 def mix_kernel(
-    sizes, pair_refs, score_ref, values_ref, gate_ref, bias_ref, mixing_ref, own_ref, one_ref,
-    near_here_ref, near_there_ref, far_here_ref, far_there_ref, full, flat, module,
+    sizes, near_bias_ref, far_bias_ref, score_ref, values_ref, gate_ref, mixing_ref, own_ref, one_ref,
+    near_here_ref, near_there_ref, far_here_ref, far_there_ref, module,
 ):
     sequences, local_rows, residues, chan_local, outer_width = sizes
     part = sequences // 4
@@ -492,23 +527,8 @@
     groups = heads // head_size
     row = lax.axis_index("row")
     branch = lax.axis_index("branch")
-    seq = lax.axis_index("seq")
-    pair_width = 4 * chan_local
-    for distance, ref in zip((0, 2, 1, 3), pair_refs):
-        source = pl.multiple_of((seq ^ distance) * chan_local, chan_local)
-        for k in range(2):
-            shard = row // 2 * 2 + k
-            start = pl.multiple_of(shard * chan_local, chan_local)
-            full[k, pl.ds(source, chan_local), :] = ref[pl.ds(start, chan_local), :]
-    for k in range(2):
-        plain = rounded(layer_normalize(widened(full[k]), 0))
-        bias = widened(rounded(product(bias_ref[...], plain)))
-        for i in range(local_rows):
-            for h in range(groups):
-                flat[k * local_rows + i : k * local_rows + i + 1, h * residues : (h + 1) * residues] = bias[
-                    h : h + 1, i * residues : (i + 1) * residues
-                ]
-    bias_rows = flat[...]
+    first = lax.broadcasted_iota(jnp.int32, near_bias_ref.shape, 0) // local_rows == lax.rem(row, 2)
+    bias_rows = jnp.where(first, widened(near_bias_ref[...]), widened(far_bias_ref[...]))
     scores = (
         score_ref[...].reshape(part, half, groups * residues) + bias_rows[None]
     ).reshape(part * half, groups * residues)
@@ -538,7 +558,8 @@
         there[...] = jnp.where(branch == 0, high, low)
 
 
-def place_kernel(own_ref, branch_ref, row_ref, both_ref, output_ref):
+def place_kernel(own_ref, branch_ref, row_ref, both_ref, pair_ref, output_ref, pair_output_ref):
+    pair_output_ref[...] = pair_ref[...]
     rows = own_ref.shape[0]
     branch = lax.axis_index("branch")
     parity = lax.rem(lax.axis_index("row"), 2)
@@ -553,22 +574,24 @@
 
 
 def pair_kernel(
-    sizes, pair_refs, weight_refs, gain_ref, transition_gain_ref, outer_weight_ref, seq_total,
+    sizes, shared_refs, pair_refs, gain_ref, transition_gain_ref, outer_weight_ref, seq_total, hidden_local,
     output_ref, rows, columns, gates, outer, outer_flat, ordered, final,
 ):
     sequences, local_rows, residues, chan_local, outer_width = sizes
     half = residues // 2
-    row = lax.axis_index("row")
     branch = lax.axis_index("branch")
     seq = lax.axis_index("seq")
     width = 4 * chan_local
     chan = chan_local
-    for distance, pair_ref, weight_ref in zip((0, 2, 1, 3), pair_refs, weight_refs):
+    gain = as_column(gain_ref[...])
+    at = chan + sequences
+    weight_refs = [ref.at[at:, 0:width] for ref in shared_refs]
+    hidden_refs = [ref.at[at:, width:] for ref in shared_refs]
+    for distance, row_ref, pair_ref, weight_ref in zip((0, 2, 1, 3), shared_refs, pair_refs, weight_refs):
         place = pl.ds(pl.multiple_of((seq ^ distance) * chan, chan), chan)
-        rows[place, :] = pair_ref[pl.ds(pl.multiple_of(row * chan, chan), chan), :]
+        rows[place, :] = row_ref[0:chan, :]
         for k in range(2):
-            start = pl.multiple_of((2 * branch + k) * chan, chan)
-            columns[k, place, :] = pair_ref[pl.ds(start, chan), :]
+            columns[k, place, :] = pair_ref[k * chan : (k + 1) * chan, :]
         gates[place, :] = weight_ref[4 * chan : 5 * chan, :]
 
     def projection(values, kind):
@@ -576,13 +599,13 @@
         return product(values, weights, 1, 1)
 
     raw = widened(rows[...])
-    row_input = rounded((layer_normalize(raw, 0) * gain_ref[...]).T)
+    row_input = rounded((layer_normalize(raw, 0) * gain).T)
     left = widened(
         rounded(projection(row_input, 0) * jax.nn.sigmoid(projection(row_input, 1)))
     ).reshape(local_rows, residues, width)
     right = []
     for k in range(2):
-        column_input = rounded((layer_normalize(widened(columns[k]), 0) * gain_ref[...]).T)
+        column_input = rounded((layer_normalize(widened(columns[k]), 0) * gain).T)
         right.append(
             widened(
                 rounded(projection(column_input, 2) * jax.nn.sigmoid(projection(column_input, 3)))
@@ -605,22 +628,14 @@
     first_update = widened(rounded(raw_here + gate * tri_out))
     trans_norm = rounded(layer_normalize(first_update, 1) * transition_gain_ref[...])
     down = jnp.zeros((local_rows * half, width), jnp.float32)
-    at = 6 * chan
-    hidden_local = (weight_refs[0].shape[0] - at - 2 * sequences) // 2
-    for w in weight_refs:
-        hidden = rounded(jax.nn.relu(product(trans_norm, w[at : at + hidden_local, :], 1, 1)))
-        down += product(hidden, w[at + hidden_local : at + hidden_local + width, :], 1, 1)
+    for w, h in zip(weight_refs, hidden_refs):
+        hidden = rounded(jax.nn.relu(product(trans_norm, h[0:hidden_local, :], 1, 1)))
+        down_weight = jnp.concatenate([w[6 * chan : 7 * chan, :], h[hidden_local : hidden_local + 3 * chan, :]], axis=0)
+        down += product(hidden, down_weight, 1, 1)
     pair_next = widened(rounded(first_update + down))
 
-    at = at + 2 * hidden_local
-    lefts = jnp.concatenate(
-        [
-            jnp.concatenate([w[at : at + sequences, :], w[at + sequences : at + 2 * sequences, :]], axis=1)
-            for w in weight_refs
-        ],
-        axis=0,
-    )
-    base = 4 * chan
+    lefts = jnp.concatenate([ref[chan : chan + sequences, :] for ref in shared_refs], axis=0)
+    base = 2 * chan
     rights = jnp.concatenate(
         [
             jnp.concatenate([p[base : base + sequences, :], p[base + sequences :, :]], axis=1)
@@ -644,8 +659,11 @@
         [final[pl.ds(i, half, stride=local_rows), :] for i in range(local_rows)], axis=0
     )
     outer_update = widened(rounded(outer_update))
-    final[...] = (pair_next + outer_update).T
-    output_ref[...] = rounded(final[pl.ds(pl.multiple_of(seq * chan, chan), chan), :])
+    result = pair_next + outer_update
+    own = result[:, 0:chan]
+    for k in range(1, 4):
+        own = jnp.where(seq == k, result[:, k * chan : (k + 1) * chan], own)
+    output_ref[...] = rounded(own)
 
 
 def compact_shards(
@@ -670,58 +688,79 @@
 
     rows_flat = alignment_input.reshape(sequences * local_rows, width)
     message_rows = part_rows + chan_local + sequences
-    same, other, left = kernel_call(
+    outer_weight_flat = outer_input_weight.transpose(1, 2, 0).reshape(2 * outer_width, width)
+    (token,) = kernel_call(start_kernel, [shape(8, 128, dtype=full_type)], [], flops=5 * 10**9)
+    hidden_local = transition_up_weight.shape[0]
+    shared_rows = chan_local + sequences + 7 * chan_local
+    same, other, shared, pair_flat = kernel_call(
         functools.partial(send_kernel, sizes),
-        [shape(message_rows, width), shape(message_rows, width), shape(sequences, local_rows * outer_width)],
-        [rows_flat, pairwise_input, product_gain[None], outer_input_weight.reshape(width, 2 * outer_width)],
+        [shape(message_rows, width), shape(message_rows, width),
+         shape(shared_rows, width), shape(chan_local, local_rows * residues)],
+        [rows_flat, pairwise_input, product_gain[None], outer_weight_flat, triangle_input_weight,
+         triangle_gate_weight, triangle_gain[None], triangle_output_weight.T, transition_up_weight,
+         transition_down_weight, token],
         [pltpu.VMEM((sequences * local_rows, 128), full_type)],
     )
+    shared_x = exchange(shared, "seq", 2)
+    shared_core = exchange(shared, "seq", 1)
+    shared_both = exchange(shared_x, "seq", 1)
+    shareds = (shared, shared_x, shared_core, shared_both)
     from_three = exchange(other, "row", 3)
     from_two = exchange(same, "row", 2)
     from_one = exchange(other, "row", 1)
     received = (same, from_one, from_two, from_three)
 
-    packed_rows = 6 * chan_local + transition_up_weight.shape[0] + transition_down_weight.shape[0] + 2 * sequences
-    (packed,) = kernel_call(
-        weight_kernel,
-        [shape(packed_rows, pair_width)],
-        [left, triangle_input_weight, triangle_gate_weight, triangle_gain[None],
-         triangle_output_weight, transition_up_weight, transition_down_weight],
-    )
-    packed_x = exchange(packed, "seq", 2)
-    packed_core = exchange(packed, "seq", 1)
-    packed_both = exchange(packed_x, "seq", 1)
-    weights = (packed, packed_x, packed_core, packed_both)
+    pair_core = exchange(pair_flat, "seq", 1)
+    pair_both = exchange(shared_x[0:chan_local], "seq", 1)
+    pairs = (shared, shared_x, pair_core, pair_both)
+
+    late_weight = lax.optimization_barrier((attention_weight, pair_flat))[0]
+    kept = [late_weight.reshape(width, 4 * heads), mixing_weight,
+            outer_output_weight.reshape(outer_width * outer_width, pair_width),
+            alignment_gain[None], pairwise_gain[None], transition_gain[None]]
+    attention_kept, mixing_kept, outer_kept, row_gain, pair_gain, last_gain = kernel_call(
+        keep_kernel, [shape(*a.shape, dtype=a.dtype) for a in kept], kept
+    )
+
+    def bias_body(*refs):
+        bias_kernel(chan_local, refs[:4], *refs[4:])
+
+    (near_bias,) = kernel_call(
+        bias_body,
+        [shape(half, groups * residues)],
+        [*pairs, bias_matrix.T],
+        [
+            pltpu.VMEM((pair_width, local_rows * residues), full_type),
+            pltpu.VMEM((local_rows, groups * residues), full_type),
+        ],
+        flops=BIAS_COST,
+    )
+    far_bias = exchange(near_bias, "row", 1)
 
     (relay,) = kernel_call(
         functools.partial(relay_kernel, sizes),
-        [shape(4 * chan_local + 2 * sequences, width)],
-        list(received),
+        [shape(2 * chan_local + 2 * sequences, width)],
+        [*received, far_bias, row_gain],
     )
     relay_x = exchange(relay, "seq", 2)
     relay_core = exchange(relay, "seq", 1)
-    relay_both = exchange(relay_x, "seq", 1)
+    relay_both = exchange(relay, "seq", 3)
     relays = (relay, relay_x, relay_core, relay_both)
 
     scores, values, gate = kernel_call(
         functools.partial(score_kernel, sizes),
         [shape(part * half, groups * residues, dtype=full_type), shape(part * residues, heads), shape(part * half, heads)],
-        [*received, alignment_gain[None], attention_weight.reshape(width, 4 * heads)],
+        [*received, row_gain, attention_kept],
         [pltpu.VMEM((part, residues, width), full_type)],
-    )
-
-    def mix_body(*refs):
-        mix_kernel(sizes, refs[:4], *refs[4:])
+        flops=3 * 10**9,
+    )
 
     near_here, near_there, far_here, far_there = kernel_call(
-        mix_body,
+        functools.partial(mix_kernel, sizes),
         [shape(part_rows, width // 2)] * 4,
-        [*relays, scores, values, gate, bias_matrix.T, mixing_weight, same, from_one],
-        [
-            pltpu.VMEM((2, pair_width, local_rows * residues), half_type),
-            pltpu.VMEM((half, groups * residues), full_type),
-            pltpu.VMEM((part, half, width), full_type),
-        ],
+        [near_bias, far_bias, scores, values, gate, mixing_kept, same, from_one],
+        [pltpu.VMEM((part, half, width), full_type)],
+        flops=3 * 10**9,
     )
     axes = ("branch", "row")
     across = lax.axis_size("row")
@@ -730,13 +769,12 @@
     from_row = exchange(far_here, axes, 1)
 
     def pair_body(*refs):
-        pair_kernel(sizes, refs[:4], refs[4:8], *refs[8:11], sequences * 4, *refs[11:])
-
-    (pair_flat,) = kernel_call(
+        pair_kernel(sizes, refs[:4], refs[4:8], *refs[8:11], sequences * 4, hidden_local, *refs[11:])
+
+    (pair_done,) = kernel_call(
         pair_body,
-        [shape(chan_local, local_rows * half)],
-        [*relays, *weights, pairwise_gain[:, None], transition_gain[None],
-         outer_output_weight.reshape(outer_width * outer_width, pair_width)],
+        [shape(local_rows * half, chan_local)],
+        [*shareds, *relays, pair_gain, last_gain, outer_kept],
         [
             pltpu.VMEM((pair_width, local_rows * residues), half_type),
             pltpu.VMEM((2, pair_width, local_rows * residues), half_type),
@@ -747,14 +785,14 @@
             pltpu.VMEM((local_rows * half, pair_width), full_type),
         ],
     )
-    (alignment_flat,) = kernel_call(
+    alignment_flat, pairwise_output = kernel_call(
         place_kernel,
-        [shape(sequences * local_rows, width // 2)],
-        [near_here, from_branch, from_row, from_both],
+        [shape(sequences * local_rows, width // 2), shape(local_rows * half, chan_local)],
+        [near_here, from_branch, from_row, from_both, pair_done],
     )
     return (
         alignment_flat.reshape(sequences, local_rows, width // 2),
-        pair_flat.reshape(chan_local, local_rows, half),
+        pairwise_output.reshape(local_rows, half, chan_local).transpose(2, 0, 1),
     )
 
 

time: 39.2 us -> 32.5 us (0.83)
  waiting for transfers between devices: 13.7 us -> 6.69 us
  starting transfers between devices: 12 us -> 16 us
  local copies, waits for them, and re-layouts: 6.24 us -> 2.29 us
    ppermute x12 -> x15, waiting for transfers between devices: 13.7 us -> 6.69 us  [exchange(): lax.ppermute(value, axes, [(i, i ^ distance) for i in range(members)])]
    ppermute x12 -> x15, starting transfers between devices: 12 us -> 16 us  [exchange(): lax.ppermute(value, axes, [(i, i ^ distance) for i in range(members)])]
    unnamed x34 -> x35, local copies, waits for them, and re-layouts: 4.49 us -> 2.29 us
    reshape x1 -> x0, local copies, waits for them, and re-layouts: 0.9 us -> none  [compact_shards(): outer_input_weight.reshape(width, 2 * outer_width)]
    pallas_call x1 -> x0, local copies, waits for them, and re-layouts: 0.73 us -> none  [kernel_call(): pl.pallas_call(body, out_shape=outputs, in_specs=[vmem] * len(operands),...]
    pallas_call x7 -> x9, Pallas kernels: 6.15 us -> 6.38 us  [kernel_call(): pl.pallas_call(body, out_shape=outputs, in_specs=[hbm if i in in_hbm else...]
  transfers between devices with their start and end apart: 12 -> 15, of which waited for: 5 -> 3; matrix products, arithmetic and copies ran while one was open for 3% -> 0% of each run, Pallas kernels for 13% -> 16%
where the time goes in v2:
time: 32.5 us; the launch traced here: 32.3 us
  starting transfers between devices  16 us (49%)
  waiting for transfers between devices  6.69 us (21%)
  Pallas kernels  6.38 us (20%)
  local copies, waits for them, and re-layouts  2.29 us (7%)
  between operations  0.9 us (3%)
    ppermute x15, starting transfers between devices, exchange(): lax.ppermute(value, axes, [(i, i ^ distance) for i in range(members)])  16 us
    ppermute x15, waiting for transfers between devices, exchange(): lax.ppermute(value, axes, [(i, i ^ distance) for i in range(members)])  6.69 us
    pallas_call x9, Pallas kernels, kernel_call(): pl.pallas_call(body, out_shape=outputs, in_specs=[hbm if i in in_hbm else...  6.38 us
    unnamed x35, local copies, waits for them, and re-layouts  2.29 us
  transfers between devices with their start and end apart: 15, of which 3 were waited for; matrix products, arithmetic and copies ran while one was open for 0% of the time, Pallas kernels for 16%

profile of v2, /device:TPU:0, one launch (start us, length us, event | category | flops | bytes accessed | tf_op | source)
XLA Modules:
  0.0 32.3 jit_solution(4997072343311419137)
XLA Ops:
  0.6 0.0 copy-start.1
  0.7 0.0 copy-start.8
  0.7 0.0 copy-start.10
  0.8 0.8 %copy-done.1 = bf16[64,8,256]{2,1,0:T(8,128)(2,1)S(1)} copy-done((bf16[64,8,256]{2,1,0:T(8,128)(2,1)S(1)}, bf16[64,8,256]{2,1,0:T(8,128)(2,1)}, u32[]{:S(2)}) %copy-start.1) | copy-done | bytes 262168
  1.6 0.6 %shard_map.177 = (bf16[224,256]{1,0:T(8,128)(2,1)S(1)}, bf16[224,256]{1,0:T(8,128)(2,1)S(1)}, bf16[320,256]{1,0:T(8,128)(2,1)S(1)}, bf16[32,256]{1,0:T(8,128)(2,1)S(1)}) custom-call(bf16[512,256]{1,0:T(8,128)(2,1)S(1)} %bitcast.20, bf16[32,8,32]{2,1,0:T(8,128)(2,1)S(1)} %copy-done.3, f32[1,256]{1,0:T(1,128)S(1)} %bitcast.23, bf16[64,256]{1,0:T(8,128)(2,1)S(1)} %bitcast.21, ...), custom_call_target="tpu_custom_call" | custom-call | bytes 840832 | tf_op jit(solution)/shard_map/pallas_call | solution.py:375
  2.2 3.0 %collective-permute-start = (bf16[320,256]{1,0:T(8,128)(2,1)S(1)}, bf16[320,256]{1,0:T(8,128)(2,1)S(1)}, u32[]{:S(2)}, u32[]{:S(2)}) collective-permute-start(bf16[320,256]{1,0:T(8,128)(2,1)S(1)} %get-tuple-element.22.refs_0_), channel_id=1, source_target_pairs={{0,2},{1,3},{2,0},{3,1},{4,6},{5,7},{6,4},{7,5},{8,10},{9,11},{10,... | collective-permute-start | bytes 491528 | tf_op jit(solution)/shard_map/ppermute | solution.py:388
  5.2 1.6 %collective-permute-start.4 = (bf16[224,256]{1,0:T(8,128)(2,1)S(1)}, bf16[224,256]{1,0:T(8,128)(2,1)S(1)}, u32[]{:S(2)}, u32[]{:S(2)}) collective-permute-start(bf16[224,256]{1,0:T(8,128)(2,1)S(1)} %get-tuple-element.25), channel_id=1, source_target_pairs={{0,4},{4,0},{8,12},{12,8},{1,5},{5,1},{9,13},{13,9},{2,6},{6,2},{1... | collective-permute-start | bytes 344072 | tf_op jit(solution)/shard_map/ppermute | solution.py:388
  6.8 2.6 %collective-permute-start.5 = (bf16[224,256]{1,0:T(8,128)(2,1)S(1)}, bf16[224,256]{1,0:T(8,128)(2,1)S(1)}, u32[]{:S(2)}, u32[]{:S(2)}) collective-permute-start(bf16[224,256]{1,0:T(8,128)(2,1)S(1)} %get-tuple-element.24.own_ref), channel_id=1, source_target_pairs={{0,8},{4,12},{8,0},{12,4},{1,9},{5,13},{9,1},{13,5},{2,10},{6,14},... | collective-permute-start | bytes 344072 | tf_op jit(solution)/shard_map/ppermute | solution.py:388
  9.4 0.2 collective-permute-start.6
  9.6 0.0 collective-permute-start.1
  9.6 0.0 collective-permute-done.refs_1_
  9.6 0.5 %collective-permute-start.2 = (bf16[32,256]{1,0:T(8,128)(2,1)S(1)}, bf16[32,256]{1,0:T(8,128)(2,1)S(1)}, u32[]{:S(2)}, u32[]{:S(2)}) collective-permute-start(bf16[32,256]{1,0:T(8,128)(2,1)S(1)} %slice.4), channel_id=1, source_target_pairs={{0,1},{1,0},{2,3},{3,2},{4,5},{5,4},{6,7},{7,6},{8,9},{9,8},{10,11... | collective-permute-start | bytes 49160 | tf_op jit(solution)/shard_map/ppermute | solution.py:388
  10.1 0.1 copy.19
  10.2 0.0 copy-start.11
  10.2 0.0 copy-start.12
  10.2 0.8 %copy-done = bf16[32,32,128]{2,1,0:T(8,128)(2,1)S(1)} copy-done((bf16[32,32,128]{2,1,0:T(8,128)(2,1)S(1)}, bf16[32,32,128]{2,1,0:T(8,128)(2,1)}, u32[]{:S(2)}) %copy-start) | copy-done | bytes 262168
  11.1 0.0 copy-done.2
  11.1 0.1 shard_map.179
  11.2 0.0 collective-permute-done.1.refs_2_
  11.2 0.1 collective-permute-start.10
  11.3 0.0 collective-permute-done.2.refs_3_
  11.3 0.5 %copy-done.15 = bf16[128,8]{0,1:T(8,128)(2,1)S(1)} copy-done((bf16[128,8]{0,1:T(8,128)(2,1)S(1)}, bf16[128,8]{0,1:T(8,128)(2,1)}, u32[]{:S(2)}) %copy-start.15) | copy-done | bytes 2072
  11.8 0.3 %shard_map.178.near_bias_ref = bf16[16,256]{1,0:T(8,128)(2,1)S(1)} custom-call(bf16[320,256]{1,0:T(8,128)(2,1)S(1)} %get-tuple-element.22.refs_0_, bf16[320,256]{1,0:T(8,128)(2,1)S(1)} %collective-permute-done.refs_1_, bf16[32,256]{1,0:T(8,128)(2,1)S(1)} %collective-permute-done.1.refs_2_, bf16[32,256]{1,0:T(8,128)(2,1)S(1)} %collective-permute-done.2.refs_3_, ...), custom_call_target="tpu_custom_call" | custom-call | flops 175000000 | bytes 370688 | tf_op jit(solution)/shard_map/pallas_call | solution.py:375
  12.1 1.2 %collective-permute-start.3 = (bf16[16,256]{1,0:T(8,128)(2,1)S(1)}, bf16[16,256]{1,0:T(8,128)(2,1)S(1)}, u32[]{:S(2)}, u32[]{:S(2)}) collective-permute-start(bf16[16,256]{1,0:T(8,128)(2,1)S(1)} %shard_map.178.near_bias_ref), channel_id=1, source_target_pairs={{0,4},{4,0},{8,12},{12,8},{1,5},{5,1},{9,13},{13,9},{2,6},{6,2},{1... | collective-permute-start | bytes 24584 | tf_op jit(solution)/shard_map/ppermute | solution.py:388
  13.3 0.0 collective-permute-done.4.one_ref
  13.3 4.9 %collective-permute-done.5.two_ref = bf16[224,256]{1,0:T(8,128)(2,1)S(1)} collective-permute-done((bf16[224,256]{1,0:T(8,128)(2,1)S(1)}, bf16[224,256]{1,0:T(8,128)(2,1)S(1)}, u32[]{:S(2)}, u32[]{:S(2)}) %collective-permute-start.5) | collective-permute-done | bytes 114720 | tf_op jit(solution)/shard_map/ppermute | solution.py:388
  18.2 0.0 collective-permute-done.6.three_ref
  18.2 1.0 %shard_map.180 = (f32[256,256]{1,0:T(8,128)S(1)}, bf16[512,256]{1,0:T(8,128)(2,1)S(1)}, bf16[256,256]{1,0:T(8,128)(2,1)S(1)}) custom-call(bf16[224,256]{1,0:T(8,128)(2,1)S(1)} %get-tuple-element.24.own_ref, bf16[224,256]{1,0:T(8,128)(2,1)S(1)} %collective-permute-done.4.one_ref, bf16[224,256]{1,0:T(8,128)(2,1)S(1)} %collective-permute-done.5.two_ref, ...), custom_call_target="tpu_custom_call" | custom-call | flops 3000000000 | bytes 1639424 | tf_op jit(solution)/shard_map/pallas_call | solution.py:375
  19.2 0.0 collective-permute-start.11
  19.3 0.0 collective-permute-done.3.far_bias_ref.after_bias_ref
  19.3 0.1 shard_map.182.refs_4_
  19.3 0.6 %collective-permute-start.12 = (bf16[192,256]{1,0:T(8,128)(2,1)S(1)}, bf16[192,256]{1,0:T(8,128)(2,1)S(1)}, u32[]{:S(2)}, u32[]{:S(2)}) collective-permute-start(bf16[192,256]{1,0:T(8,128)(2,1)S(1)} %shard_map.182.refs_4_), channel_id=1, source_target_pairs={{0,2},{1,3},{2,0},{3,1},{4,6},{5,7},{6,4},{7,5},{8,10},{9,11},{10,... | collective-permute-start | bytes 294920 | tf_op jit(solution)/shard_map/ppermute | solution.py:388
  19.9 0.2 collective-permute-start.13
  20.1 1.4 %collective-permute-start.14 = (bf16[192,256]{1,0:T(8,128)(2,1)S(1)}, bf16[192,256]{1,0:T(8,128)(2,1)S(1)}, u32[]{:S(2)}, u32[]{:S(2)}) collective-permute-start(bf16[192,256]{1,0:T(8,128)(2,1)S(1)} %shard_map.182.refs_4_), channel_id=1, source_target_pairs={{0,3},{1,2},{2,1},{3,0},{4,7},{5,6},{6,5},{7,4},{8,11},{9,10},{10,... | collective-permute-start | bytes 294920 | tf_op jit(solution)/shard_map/ppermute | solution.py:388
  21.5 1.3 %shard_map.181 = (bf16[128,128]{1,0:T(8,128)(2,1)S(1)}, bf16[128,128]{1,0:T(8,128)(2,1)S(1)}, bf16[128,128]{1,0:T(8,128)(2,1)S(1)}, bf16[128,128]{1,0:T(8,128)(2,1)S(1)}) custom-call(bf16[16,256]{1,0:T(8,128)(2,1)S(1)} %shard_map.178.near_bias_ref, bf16[16,256]{1,0:T(8,128)(2,1)S(1)} %collective-permute-done.3.far_bias_ref.after_bias_ref, ...), custom_call_target="tpu_custom_call" | custom-call | flops 3000000000 | bytes 1163264 | tf_op jit(solution)/shard_map/pallas_call | solution.py:375
  22.8 0.0 collective-permute-done.10.refs_2_
  22.8 1.6 %collective-permute-start.7 = (bf16[128,128]{1,0:T(8,128)(2,1)S(1)}, bf16[128,128]{1,0:T(8,128)(2,1)S(1)}, u32[]{:S(2)}, u32[]{:S(2)}) collective-permute-start(bf16[128,128]{1,0:T(8,128)(2,1)S(1)} %get-tuple-element.34), channel_id=1, source_target_pairs={{0,16},{4,20},{8,24},{12,28},{16,0},{20,4},{24,8},{28,12},{1,17},{... | collective-permute-start | bytes 98312 | tf_op jit(solution)/shard_map/ppermute | solution.py:388
  24.4 0.6 %collective-permute-done.12.refs_5_ = bf16[192,256]{1,0:T(8,128)(2,1)S(1)} collective-permute-done((bf16[192,256]{1,0:T(8,128)(2,1)S(1)}, bf16[192,256]{1,0:T(8,128)(2,1)S(1)}, u32[]{:S(2)}, u32[]{:S(2)}) %collective-permute-start.12) | collective-permute-done | bytes 98336 | tf_op jit(solution)/shard_map/ppermute | solution.py:388
  25.0 1.8 %collective-permute-start.8 = (bf16[128,128]{1,0:T(8,128)(2,1)S(1)}, bf16[128,128]{1,0:T(8,128)(2,1)S(1)}, u32[]{:S(2)}, u32[]{:S(2)}) collective-permute-start(bf16[128,128]{1,0:T(8,128)(2,1)S(1)} %get-tuple-element.35), channel_id=1, source_target_pairs={{0,4},{4,0},{8,12},{12,8},{16,20},{20,16},{24,28},{28,24},{1,5},{5... | collective-permute-start | bytes 98312 | tf_op jit(solution)/shard_map/ppermute | solution.py:388
  26.8 0.0 collective-permute-done.13.refs_6_
  26.8 1.2 %collective-permute-start.9 = (bf16[128,128]{1,0:T(8,128)(2,1)S(1)}, bf16[128,128]{1,0:T(8,128)(2,1)S(1)}, u32[]{:S(2)}, u32[]{:S(2)}) collective-permute-start(bf16[128,128]{1,0:T(8,128)(2,1)S(1)} %get-tuple-element.36), channel_id=1, source_target_pairs={{0,20},{4,16},{8,28},{12,24},{16,4},{20,0},{24,12},{28,8},{1,21},{... | collective-permute-start | bytes 98312 | tf_op jit(solution)/shard_map/ppermute | solution.py:388
  28.0 0.0 collective-permute-done.14.refs_7_
  28.0 0.0 collective-permute-done.11.refs_3_
  28.0 2.4 %shard_map.183.pair_ref = bf16[128,32]{1,0:T(8,128)(2,1)S(1)} custom-call(bf16[320,256]{1,0:T(8,128)(2,1)S(1)} %get-tuple-element.22.refs_0_, bf16[320,256]{1,0:T(8,128)(2,1)S(1)} %collective-permute-done.refs_1_, bf16[320,256]{1,0:T(8,128)(2,1)S(1)} %collective-permute-done.10.refs_2_, bf16[320,256]{1,0:T(8,128)(2,1)S(1)} %collective-permute-done.11.refs_3_, ...), custom_call_target="tpu_custom_call" | custom-call | bytes 1319936 | tf_op jit(solution)/shard_map/pallas_call | solution.py:375
  30.4 0.0 collective-permute-done.7.branch_ref
  30.4 0.0 collective-permute-done.8.row_ref
  30.4 1.2 %collective-permute-done.9.both_ref = bf16[128,128]{1,0:T(8,128)(2,1)S(1)} collective-permute-done((bf16[128,128]{1,0:T(8,128)(2,1)S(1)}, bf16[128,128]{1,0:T(8,128)(2,1)S(1)}, u32[]{:S(2)}, u32[]{:S(2)}) %collective-permute-start.9) | collective-permute-done | bytes 32800 | tf_op jit(solution)/shard_map/ppermute | solution.py:388
  31.6 0.7 %shard_map.184 = (bf16[512,128]{1,0:T(8,128)(2,1)}, bf16[128,32]{1,0:T(8,128)(2,1)}) custom-call(bf16[128,128]{1,0:T(8,128)(2,1)S(1)} %get-tuple-element.33.own_ref, bf16[128,128]{1,0:T(8,128)(2,1)S(1)} %collective-permute-done.7.branch_ref, bf16[128,128]{1,0:T(8,128)(2,1)S(1)} %collective-permute-done.8.row_ref, ...), custom_call_target="tpu_custom_call" | custom-call | bytes 278528 | tf_op jit(solution)/shard_map/pallas_call | solution.py:375
  (27 shorter events, 0.1 us)
Async XLA Ops:
  0.6 1.0 %copy-start.1 = (bf16[64,8,256]{2,1,0:T(8,128)(2,1)S(1)}, bf16[64,8,256]{2,1,0:T(8,128)(2,1)}, u32[]{:S(2)}) copy-start(bf16[64,8,256]{2,1,0:T(8,128)(2,1)} %param.17) | copy-start | bytes 786436
  0.6 0.9 %copy-start.3 = (bf16[32,8,32]{2,1,0:T(8,128)(2,1)S(1)}, bf16[32,8,32]{2,1,0:T(8,128)(2,1)}, u32[]{:S(2)}) copy-start(bf16[32,8,32]{2,1,0:T(8,128)(2,1)} %pair_ref.1) | copy-start | bytes 49156
  0.7 0.9 %copy-start.4 = (bf16[256,2,32]{0,2,1:T(8,128)(2,1)S(1)}, bf16[256,2,32]{0,2,1:T(8,128)(2,1)}, u32[]{:S(2)}) copy-start(bf16[256,2,32]{0,2,1:T(8,128)(2,1)} %param.23) | copy-start | bytes 98308
  0.7 0.9 %copy-start.5 = (bf16[4,32,128]{2,1,0:T(8,128)(2,1)S(1)}, bf16[4,32,128]{2,1,0:T(8,128)(2,1)}, u32[]{:S(2)}) copy-start(bf16[4,32,128]{2,1,0:T(8,128)(2,1)} %input_ref.1) | copy-start | bytes 98308
  0.7 0.9 %copy-start.6 = (bf16[128,128]{1,0:T(8,128)(2,1)S(1)}, bf16[128,128]{1,0:T(8,128)(2,1)}, u32[]{:S(2)}) copy-start(bf16[128,128]{1,0:T(8,128)(2,1)} %up_ref.1) | copy-start | bytes 98308
  0.7 0.9 %copy-start.7 = (bf16[128,128]{1,0:T(8,128)(2,1)S(1)}, bf16[128,128]{1,0:T(8,128)(2,1)}, u32[]{:S(2)}) copy-start(bf16[128,128]{1,0:T(8,128)(2,1)} %down_ref.1) | copy-start | bytes 98308
  0.7 0.9 %copy-start.9 = (bf16[128,32]{0,1:T(8,128)(2,1)S(1)}, bf16[128,32]{0,1:T(8,128)(2,1)}, u32[]{:S(2)}) copy-start(bf16[128,32]{0,1:T(8,128)(2,1)} %param.30) | copy-start | bytes 24580
  0.7 0.9 %copy-start.14 = (f32[32]{0:T(128)S(1)}, f32[32]{0:T(128)}, u32[]{:S(2)}) copy-start(f32[32]{0:T(128)} %param.29) | copy-start | bytes 388
  0.7 9.4 %copy-start.16 = (bf16[256,4,256]{2,1,0:T(4,128)(2,1)S(1)}, bf16[256,4,256]{2,1,0:T(4,128)(2,1)}, u32[]{:S(2)}) copy-start(bf16[256,4,256]{2,1,0:T(4,128)(2,1)} %param.21) | copy-start | bytes 1572868
  0.7 0.9 %copy-start.8 = (bf16[32,128]{1,0:T(8,128)(2,1)S(1)}, bf16[32,128]{1,0:T(8,128)(2,1)}, u32[]{:S(2)}) copy-start(bf16[32,128]{1,0:T(8,128)(2,1)} %gate_ref.1) | copy-start | bytes 24580
  0.7 0.9 %copy-start.10 = (f32[256]{0:T(256)S(1)}, f32[256]{0:T(256)}, u32[]{:S(2)}) copy-start(f32[256]{0:T(256)} %param.20) | copy-start | bytes 3076
  2.2 7.4 %collective-permute-start = (bf16[320,256]{1,0:T(8,128)(2,1)S(1)}, bf16[320,256]{1,0:T(8,128)(2,1)S(1)}, u32[]{:S(2)}, u32[]{:S(2)}) collective-permute-start(bf16[320,256]{1,0:T(8,128)(2,1)S(1)} %get-tuple-element.22.refs_0_), channel_id=1, source_target_pairs={{0,2},{1,3},{2,0},{3,1},{4,6},{5,7},{6,4},{7,5},{8,10},{9,11},{10,... | collective-permute-start | bytes 491528 | tf_op jit(solution)/shard_map/ppermute | solution.py:388
  5.2 8.1 %collective-permute-start.4 = (bf16[224,256]{1,0:T(8,128)(2,1)S(1)}, bf16[224,256]{1,0:T(8,128)(2,1)S(1)}, u32[]{:S(2)}, u32[]{:S(2)}) collective-permute-start(bf16[224,256]{1,0:T(8,128)(2,1)S(1)} %get-tuple-element.25), channel_id=1, source_target_pairs={{0,4},{4,0},{8,12},{12,8},{1,5},{5,1},{9,13},{13,9},{2,6},{6,2},{1... | collective-permute-start | bytes 344072 | tf_op jit(solution)/shard_map/ppermute | solution.py:388
  6.8 11.4 %collective-permute-start.5 = (bf16[224,256]{1,0:T(8,128)(2,1)S(1)}, bf16[224,256]{1,0:T(8,128)(2,1)S(1)}, u32[]{:S(2)}, u32[]{:S(2)}) collective-permute-start(bf16[224,256]{1,0:T(8,128)(2,1)S(1)} %get-tuple-element.24.own_ref), channel_id=1, source_target_pairs={{0,8},{4,12},{8,0},{12,4},{1,9},{5,13},{9,1},{13,5},{2,10},{6,14},... | collective-permute-start | bytes 344072 | tf_op jit(solution)/shard_map/ppermute | solution.py:388
  9.4 8.8 %collective-permute-start.6 = (bf16[224,256]{1,0:T(8,128)(2,1)S(1)}, bf16[224,256]{1,0:T(8,128)(2,1)S(1)}, u32[]{:S(2)}, u32[]{:S(2)}) collective-permute-start(bf16[224,256]{1,0:T(8,128)(2,1)S(1)} %get-tuple-element.25), channel_id=1, source_target_pairs={{0,12},{4,8},{8,4},{12,0},{1,13},{5,9},{9,5},{13,1},{2,14},{6,10},... | collective-permute-start | bytes 344072 | tf_op jit(solution)/shard_map/ppermute | solution.py:388
  9.6 1.6 %collective-permute-start.1 = (bf16[32,256]{1,0:T(8,128)(2,1)S(1)}, bf16[32,256]{1,0:T(8,128)(2,1)S(1)}, u32[]{:S(2)}, u32[]{:S(2)}) collective-permute-start(bf16[32,256]{1,0:T(8,128)(2,1)S(1)} %get-tuple-element.23), channel_id=1, source_target_pairs={{0,1},{1,0},{2,3},{3,2},{4,5},{5,4},{6,7},{7,6},{8,9},{9,8},{10,11... | collective-permute-start | bytes 49160 | tf_op jit(solution)/shard_map/ppermute | solution.py:388
  9.6 1.7 %collective-permute-start.2 = (bf16[32,256]{1,0:T(8,128)(2,1)S(1)}, bf16[32,256]{1,0:T(8,128)(2,1)S(1)}, u32[]{:S(2)}, u32[]{:S(2)}) collective-permute-start(bf16[32,256]{1,0:T(8,128)(2,1)S(1)} %slice.4), channel_id=1, source_target_pairs={{0,1},{1,0},{2,3},{3,2},{4,5},{5,4},{6,7},{7,6},{8,9},{9,8},{10,11... | collective-permute-start | bytes 49160 | tf_op jit(solution)/shard_map/ppermute | solution.py:388
  10.1 1.0 %copy-start = (bf16[32,32,128]{2,1,0:T(8,128)(2,1)S(1)}, bf16[32,32,128]{2,1,0:T(8,128)(2,1)}, u32[]{:S(2)}) copy-start(bf16[32,32,128]{2,1,0:T(8,128)(2,1)} %param.24) | copy-start | bytes 786436
  10.1 1.0 %copy-start.2 = (bf16[256,256]{1,0:T(8,128)(2,1)S(1)}, bf16[256,256]{1,0:T(8,128)(2,1)}, u32[]{:S(2)}) copy-start(bf16[256,256]{1,0:T(8,128)(2,1)} %refs_1_.1) | copy-start | bytes 393220
  10.1 1.0 %copy-start.13 = (f32[128]{0:T(128)S(1)}, f32[128]{0:T(128)}, u32[]{:S(2)}) copy-start(f32[128]{0:T(128)} %param.31) | copy-start | bytes 1540
  10.2 0.9 %copy-start.11 = (f32[256]{0:T(256)S(1)}, f32[256]{0:T(256)}, u32[]{:S(2)}) copy-start(f32[256]{0:T(256)} %param.19) | copy-start | bytes 3076
  10.2 0.9 %copy-start.12 = (f32[128]{0:T(128)S(1)}, f32[128]{0:T(128)}, u32[]{:S(2)}) copy-start(f32[128]{0:T(128)} %param.26) | copy-start | bytes 1540
  11.1 0.7 %copy-start.15 = (bf16[128,8]{0,1:T(8,128)(2,1)S(1)}, bf16[128,8]{0,1:T(8,128)(2,1)}, u32[]{:S(2)}) copy-start(bf16[128,8]{0,1:T(8,128)(2,1)} %param.25) | copy-start | bytes 6148
  11.2 11.6 %collective-permute-start.10 = (bf16[320,256]{1,0:T(8,128)(2,1)S(1)}, bf16[320,256]{1,0:T(8,128)(2,1)S(1)}, u32[]{:S(2)}, u32[]{:S(2)}) collective-permute-start(bf16[320,256]{1,0:T(8,128)(2,1)S(1)} %get-tuple-element.22.refs_0_), channel_id=1, source_target_pairs={{0,1},{1,0},{2,3},{3,2},{4,5},{5,4},{6,7},{7,6},{8,9},{9,8},{10,11... | collective-permute-start | bytes 491528 | tf_op jit(solution)/shard_map/ppermute | solution.py:388
  12.1 7.1 %collective-permute-start.3 = (bf16[16,256]{1,0:T(8,128)(2,1)S(1)}, bf16[16,256]{1,0:T(8,128)(2,1)S(1)}, u32[]{:S(2)}, u32[]{:S(2)}) collective-permute-start(bf16[16,256]{1,0:T(8,128)(2,1)S(1)} %shard_map.178.near_bias_ref), channel_id=1, source_target_pairs={{0,4},{4,0},{8,12},{12,8},{1,5},{5,1},{9,13},{13,9},{2,6},{6,2},{1... | collective-permute-start | bytes 24584 | tf_op jit(solution)/shard_map/ppermute | solution.py:388
  19.2 8.7 %collective-permute-start.11 = (bf16[320,256]{1,0:T(8,128)(2,1)S(1)}, bf16[320,256]{1,0:T(8,128)(2,1)S(1)}, u32[]{:S(2)}, u32[]{:S(2)}) collective-permute-start(bf16[320,256]{1,0:T(8,128)(2,1)S(1)} %collective-permute-done.refs_1_), channel_id=1, source_target_pairs={{0,1},{1,0},{2,3},{3,2},{4,5},{5,4},{6,7},{7,6},{8,9},{9,8},{10,11... | collective-permute-start | bytes 491528 | tf_op jit(solution)/shard_map/ppermute | solution.py:388
  19.3 5.7 %collective-permute-start.12 = (bf16[192,256]{1,0:T(8,128)(2,1)S(1)}, bf16[192,256]{1,0:T(8,128)(2,1)S(1)}, u32[]{:S(2)}, u32[]{:S(2)}) collective-permute-start(bf16[192,256]{1,0:T(8,128)(2,1)S(1)} %shard_map.182.refs_4_), channel_id=1, source_target_pairs={{0,2},{1,3},{2,0},{3,1},{4,6},{5,7},{6,4},{7,5},{8,10},{9,11},{10,... | collective-permute-start | bytes 294920 | tf_op jit(solution)/shard_map/ppermute | solution.py:388
  19.9 6.9 %collective-permute-start.13 = (bf16[192,256]{1,0:T(8,128)(2,1)S(1)}, bf16[192,256]{1,0:T(8,128)(2,1)S(1)}, u32[]{:S(2)}, u32[]{:S(2)}) collective-permute-start(bf16[192,256]{1,0:T(8,128)(2,1)S(1)} %shard_map.182.refs_4_), channel_id=1, source_target_pairs={{0,1},{1,0},{2,3},{3,2},{4,5},{5,4},{6,7},{7,6},{8,9},{9,8},{10,11... | collective-permute-start | bytes 294920 | tf_op jit(solution)/shard_map/ppermute | solution.py:388
  20.1 7.8 %collective-permute-start.14 = (bf16[192,256]{1,0:T(8,128)(2,1)S(1)}, bf16[192,256]{1,0:T(8,128)(2,1)S(1)}, u32[]{:S(2)}, u32[]{:S(2)}) collective-permute-start(bf16[192,256]{1,0:T(8,128)(2,1)S(1)} %shard_map.182.refs_4_), channel_id=1, source_target_pairs={{0,3},{1,2},{2,1},{3,0},{4,7},{5,6},{6,5},{7,4},{8,11},{9,10},{10,... | collective-permute-start | bytes 294920 | tf_op jit(solution)/shard_map/ppermute | solution.py:388
  22.8 7.6 %collective-permute-start.7 = (bf16[128,128]{1,0:T(8,128)(2,1)S(1)}, bf16[128,128]{1,0:T(8,128)(2,1)S(1)}, u32[]{:S(2)}, u32[]{:S(2)}) collective-permute-start(bf16[128,128]{1,0:T(8,128)(2,1)S(1)} %get-tuple-element.34), channel_id=1, source_target_pairs={{0,16},{4,20},{8,24},{12,28},{16,0},{20,4},{24,8},{28,12},{1,17},{... | collective-permute-start | bytes 98312 | tf_op jit(solution)/shard_map/ppermute | solution.py:388
  25.0 5.4 %collective-permute-start.8 = (bf16[128,128]{1,0:T(8,128)(2,1)S(1)}, bf16[128,128]{1,0:T(8,128)(2,1)S(1)}, u32[]{:S(2)}, u32[]{:S(2)}) collective-permute-start(bf16[128,128]{1,0:T(8,128)(2,1)S(1)} %get-tuple-element.35), channel_id=1, source_target_pairs={{0,4},{4,0},{8,12},{12,8},{16,20},{20,16},{24,28},{28,24},{1,5},{5... | collective-permute-start | bytes 98312 | tf_op jit(solution)/shard_map/ppermute | solution.py:388
  26.8 4.8 %collective-permute-start.9 = (bf16[128,128]{1,0:T(8,128)(2,1)S(1)}, bf16[128,128]{1,0:T(8,128)(2,1)S(1)}, u32[]{:S(2)}, u32[]{:S(2)}) collective-permute-start(bf16[128,128]{1,0:T(8,128)(2,1)S(1)} %get-tuple-element.36), channel_id=1, source_target_pairs={{0,20},{4,16},{8,28},{12,24},{16,4},{20,0},{24,12},{28,8},{1,21},{... | collective-permute-start | bytes 98312 | tf_op jit(solution)/shard_map/ppermute | solution.py:388

commit v3 on v2

--- a/solution.py
+++ b/solution.py
@@ -460,9 +460,9 @@
 
 
 def score_kernel(
-    sizes, own_ref, one_ref, two_ref, three_ref, gain_ref, weight_ref,
-    score_ref, values_ref, gate_ref, module,
+    sizes, own_ref, one_ref, two_ref, three_ref, gain_ref, weight_ref, *refs,
 ):
+    score_ref, values_ref, gate_ref, module = refs[-4:]
     sequences, local_rows, residues, chan_local, outer_width = sizes
     part = sequences // 4
     part_rows = part * local_rows
@@ -515,9 +515,9 @@
 
 
 def mix_kernel(
-    sizes, near_bias_ref, far_bias_ref, score_ref, values_ref, gate_ref, mixing_ref, own_ref, one_ref,
-    near_here_ref, near_there_ref, far_here_ref, far_there_ref, module,
+    sizes, near_bias_ref, far_bias_ref, score_ref, values_ref, gate_ref, mixing_ref, own_ref, one_ref, *refs,
 ):
+    near_here_ref, near_there_ref, far_here_ref, far_there_ref, module = refs[-5:]
     sequences, local_rows, residues, chan_local, outer_width = sizes
     part = sequences // 4
     part_rows = part * local_rows
@@ -714,6 +714,7 @@
     pair_both = exchange(shared_x[0:chan_local], "seq", 1)
     pairs = (shared, shared_x, pair_core, pair_both)
 
+
     late_weight = lax.optimization_barrier((attention_weight, pair_flat))[0]
     kept = [late_weight.reshape(width, 4 * heads), mixing_weight,
             outer_output_weight.reshape(outer_width * outer_width, pair_width),
@@ -750,7 +751,7 @@
     scores, values, gate = kernel_call(
         functools.partial(score_kernel, sizes),
         [shape(part * half, groups * residues, dtype=full_type), shape(part * residues, heads), shape(part * half, heads)],
-        [*received, row_gain, attention_kept],
+        [*received, row_gain, attention_kept, relay],
         [pltpu.VMEM((part, residues, width), full_type)],
         flops=3 * 10**9,
     )
@@ -758,7 +759,7 @@
     near_here, near_there, far_here, far_there = kernel_call(
         functools.partial(mix_kernel, sizes),
         [shape(part_rows, width // 2)] * 4,
-        [near_bias, far_bias, scores, values, gate, mixing_kept, same, from_one],
+        [near_bias, far_bias, scores, values, gate, mixing_kept, same, from_one, shared_core, shared_both],
         [pltpu.VMEM((part, half, width), full_type)],
         flops=3 * 10**9,
     )

time: 32.5 us -> 29.4 us (0.905)
  waiting for transfers between devices: 6.69 us -> 4.98 us
  starting transfers between devices: 16 us -> 15.2 us
  local copies, waits for them, and re-layouts: 2.29 us -> 1.83 us
    ppermute x15, waiting for transfers between devices: 6.69 us -> 4.98 us  [exchange(): lax.ppermute(value, axes, [(i, i ^ distance) for i in range(members)])]
    ppermute x15, starting transfers between devices: 16 us -> 15.2 us  [exchange(): lax.ppermute(value, axes, [(i, i ^ distance) for i in range(members)])]
    unnamed x35, local copies, waits for them, and re-layouts: 2.29 us -> 1.83 us
  transfers between devices with their start and end apart: 15 -> 15, of which waited for: 3 -> 6; matrix products, arithmetic and copies ran while one was open for 0% -> 0% of each run, Pallas kernels for 16% -> 18%
where the time goes in v3:
time: 29.4 us; the launch traced here: 29.3 us
  starting transfers between devices  15.2 us (52%)
  Pallas kernels  6.37 us (22%)
  waiting for transfers between devices  4.98 us (17%)
  local copies, waits for them, and re-layouts  1.83 us (6%)
  between operations  0.89 us (3%)
    ppermute x15, starting transfers between devices, exchange(): lax.ppermute(value, axes, [(i, i ^ distance) for i in range(members)])  15.2 us
    pallas_call x9, Pallas kernels, kernel_call(): pl.pallas_call(body, out_shape=outputs, in_specs=[hbm if i in in_hbm else...  6.37 us
    ppermute x15, waiting for transfers between devices, exchange(): lax.ppermute(value, axes, [(i, i ^ distance) for i in range(members)])  4.98 us
    unnamed x35, local copies, waits for them, and re-layouts  1.83 us
  transfers between devices with their start and end apart: 15, of which 6 were waited for; matrix products, arithmetic and copies ran while one was open for 0% of the time, Pallas kernels for 18%

profile of v3, /device:TPU:0, one launch (start us, length us, event | category | flops | bytes accessed | tf_op | source)
XLA Modules:
  0.0 29.3 jit_solution(1526292620591351699)
XLA Ops:
  0.7 0.0 copy-start.8
  0.7 0.0 copy-start.10
  0.8 0.8 %copy-done.1 = bf16[64,8,256]{2,1,0:T(8,128)(2,1)S(1)} copy-done((bf16[64,8,256]{2,1,0:T(8,128)(2,1)S(1)}, bf16[64,8,256]{2,1,0:T(8,128)(2,1)}, u32[]{:S(2)}) %copy-start.1) | copy-done | bytes 262168
  1.6 0.0 copy-done.6
  1.6 0.0 copy-done.7
  1.6 0.6 %shard_map.177 = (bf16[224,256]{1,0:T(8,128)(2,1)S(1)}, bf16[224,256]{1,0:T(8,128)(2,1)S(1)}, bf16[320,256]{1,0:T(8,128)(2,1)S(1)}, bf16[32,256]{1,0:T(8,128)(2,1)S(1)}) custom-call(bf16[512,256]{1,0:T(8,128)(2,1)S(1)} %bitcast.20, bf16[32,8,32]{2,1,0:T(8,128)(2,1)S(1)} %copy-done.3, f32[1,256]{1,0:T(1,128)S(1)} %bitcast.23, bf16[64,256]{1,0:T(8,128)(2,1)S(1)} %bitcast.21, ...), custom_call_target="tpu_custom_call" | custom-call | bytes 840832 | tf_op jit(solution)/shard_map/pallas_call | solution.py:375
  2.2 3.0 %collective-permute-start = (bf16[320,256]{1,0:T(8,128)(2,1)S(1)}, bf16[320,256]{1,0:T(8,128)(2,1)S(1)}, u32[]{:S(2)}, u32[]{:S(2)}) collective-permute-start(bf16[320,256]{1,0:T(8,128)(2,1)S(1)} %get-tuple-element.22.refs_0_), channel_id=1, source_target_pairs={{0,2},{1,3},{2,0},{3,1},{4,6},{5,7},{6,4},{7,5},{8,10},{9,11},{10,... | collective-permute-start | bytes 491528 | tf_op jit(solution)/shard_map/ppermute | solution.py:388
  5.2 2.6 %collective-permute-start.5 = (bf16[224,256]{1,0:T(8,128)(2,1)S(1)}, bf16[224,256]{1,0:T(8,128)(2,1)S(1)}, u32[]{:S(2)}, u32[]{:S(2)}) collective-permute-start(bf16[224,256]{1,0:T(8,128)(2,1)S(1)} %get-tuple-element.24.own_ref), channel_id=1, source_target_pairs={{0,8},{4,12},{8,0},{12,4},{1,9},{5,13},{9,1},{13,5},{2,10},{6,14},... | collective-permute-start | bytes 344072 | tf_op jit(solution)/shard_map/ppermute | solution.py:388
  7.8 1.6 %collective-permute-start.4 = (bf16[224,256]{1,0:T(8,128)(2,1)S(1)}, bf16[224,256]{1,0:T(8,128)(2,1)S(1)}, u32[]{:S(2)}, u32[]{:S(2)}) collective-permute-start(bf16[224,256]{1,0:T(8,128)(2,1)S(1)} %get-tuple-element.25), channel_id=1, source_target_pairs={{0,4},{4,0},{8,12},{12,8},{1,5},{5,1},{9,13},{13,9},{2,6},{6,2},{1... | collective-permute-start | bytes 344072 | tf_op jit(solution)/shard_map/ppermute | solution.py:388
  9.4 0.2 collective-permute-start.6
  9.6 0.0 collective-permute-start.1
  9.6 0.0 collective-permute-done.refs_1_
  9.6 0.5 %collective-permute-start.2 = (bf16[32,256]{1,0:T(8,128)(2,1)S(1)}, bf16[32,256]{1,0:T(8,128)(2,1)S(1)}, u32[]{:S(2)}, u32[]{:S(2)}) collective-permute-start(bf16[32,256]{1,0:T(8,128)(2,1)S(1)} %slice.4), channel_id=1, source_target_pairs={{0,1},{1,0},{2,3},{3,2},{4,5},{5,4},{6,7},{7,6},{8,9},{9,8},{10,11... | collective-permute-start | bytes 49160 | tf_op jit(solution)/shard_map/ppermute | solution.py:388
  10.1 0.7 %collective-permute-done.1.refs_2_ = bf16[32,256]{1,0:T(8,128)(2,1)S(1)} collective-permute-done((bf16[32,256]{1,0:T(8,128)(2,1)S(1)}, bf16[32,256]{1,0:T(8,128)(2,1)S(1)}, u32[]{:S(2)}, u32[]{:S(2)}) %collective-permute-start.1) | collective-permute-done | bytes 16416 | tf_op jit(solution)/shard_map/ppermute | solution.py:388
  10.8 0.2 collective-permute-done.2.refs_3_
  11.0 0.3 %shard_map.178.near_bias_ref = bf16[16,256]{1,0:T(8,128)(2,1)S(1)} custom-call(bf16[320,256]{1,0:T(8,128)(2,1)S(1)} %get-tuple-element.22.refs_0_, bf16[320,256]{1,0:T(8,128)(2,1)S(1)} %collective-permute-done.refs_1_, bf16[32,256]{1,0:T(8,128)(2,1)S(1)} %collective-permute-done.1.refs_2_, bf16[32,256]{1,0:T(8,128)(2,1)S(1)} %collective-permute-done.2.refs_3_, ...), custom_call_target="tpu_custom_call" | custom-call | flops 175000000 | bytes 370688 | tf_op jit(solution)/shard_map/pallas_call | solution.py:375
  11.3 1.5 %collective-permute-start.3 = (bf16[16,256]{1,0:T(8,128)(2,1)S(1)}, bf16[16,256]{1,0:T(8,128)(2,1)S(1)}, u32[]{:S(2)}, u32[]{:S(2)}) collective-permute-start(bf16[16,256]{1,0:T(8,128)(2,1)S(1)} %shard_map.178.near_bias_ref), channel_id=1, source_target_pairs={{0,4},{4,0},{8,12},{12,8},{1,5},{5,1},{9,13},{13,9},{2,6},{6,2},{1... | collective-permute-start | bytes 24584 | tf_op jit(solution)/shard_map/ppermute | solution.py:388
  12.8 0.0 collective-permute-start.7
  12.8 0.0 copy-start.13
  12.8 0.1 copy.19
  12.9 0.0 copy-start.11
  13.0 0.0 copy-start.12
  13.0 0.8 %copy-done = bf16[32,32,128]{2,1,0:T(8,128)(2,1)S(1)} copy-done((bf16[32,32,128]{2,1,0:T(8,128)(2,1)S(1)}, bf16[32,32,128]{2,1,0:T(8,128)(2,1)}, u32[]{:S(2)}) %copy-start) | copy-done | bytes 262168
  13.8 0.0 copy-done.2
  13.8 0.1 shard_map.179
  13.9 2.5 %collective-permute-done.5.two_ref = bf16[224,256]{1,0:T(8,128)(2,1)S(1)} collective-permute-done((bf16[224,256]{1,0:T(8,128)(2,1)S(1)}, bf16[224,256]{1,0:T(8,128)(2,1)S(1)}, u32[]{:S(2)}, u32[]{:S(2)}) %collective-permute-start.5) | collective-permute-done | bytes 114720 | tf_op jit(solution)/shard_map/ppermute | solution.py:388
  16.4 0.0 collective-permute-start.8
  16.4 0.0 collective-permute-done.4.one_ref
  16.4 0.4 %collective-permute-done.6.three_ref = bf16[224,256]{1,0:T(8,128)(2,1)S(1)} collective-permute-done((bf16[224,256]{1,0:T(8,128)(2,1)S(1)}, bf16[224,256]{1,0:T(8,128)(2,1)S(1)}, u32[]{:S(2)}, u32[]{:S(2)}) %collective-permute-start.6) | collective-permute-done | bytes 114720 | tf_op jit(solution)/shard_map/ppermute | solution.py:388
  16.8 0.0 collective-permute-done.3.after_bias_ref.far_bias_ref
  16.9 0.6 %collective-permute-start.12 = (bf16[192,256]{1,0:T(8,128)(2,1)S(1)}, bf16[192,256]{1,0:T(8,128)(2,1)S(1)}, u32[]{:S(2)}, u32[]{:S(2)}) collective-permute-start(bf16[192,256]{1,0:T(8,128)(2,1)S(1)} %shard_map.180.refs_0_.refs_4_), channel_id=1, source_target_pairs={{0,2},{1,3},{2,0},{3,1},{4,6},{5,7},{6,4},{7,5},{8,10},{9,11},{10,... | collective-permute-start | bytes 294920 | tf_op jit(solution)/shard_map/ppermute | solution.py:388
  17.4 0.0 collective-permute-start.13
  17.5 1.6 %collective-permute-start.14 = (bf16[192,256]{1,0:T(8,128)(2,1)S(1)}, bf16[192,256]{1,0:T(8,128)(2,1)S(1)}, u32[]{:S(2)}, u32[]{:S(2)}) collective-permute-start(bf16[192,256]{1,0:T(8,128)(2,1)S(1)} %shard_map.180.refs_0_.refs_4_), channel_id=1, source_target_pairs={{0,3},{1,2},{2,1},{3,0},{4,7},{5,6},{6,5},{7,4},{8,11},{9,10},{10,... | collective-permute-start | bytes 294920 | tf_op jit(solution)/shard_map/ppermute | solution.py:388
  19.1 1.0 %shard_map.181 = (f32[256,256]{1,0:T(8,128)S(1)}, bf16[512,256]{1,0:T(8,128)(2,1)S(1)}, bf16[256,256]{1,0:T(8,128)(2,1)S(1)}) custom-call(bf16[224,256]{1,0:T(8,128)(2,1)S(1)} %get-tuple-element.24.own_ref, bf16[224,256]{1,0:T(8,128)(2,1)S(1)} %collective-permute-done.4.one_ref, bf16[224,256]{1,0:T(8,128)(2,1)S(1)} %collective-permute-done.5.two_ref, ...), custom_call_target="tpu_custom_call" | custom-call | flops 3000000000 | bytes 1737728 | tf_op jit(solution)/shard_map/pallas_call | solution.py:375
  20.1 0.0 collective-permute-done.7.refs_0_.refs_2_
  20.1 0.0 collective-permute-done.8.refs_1_.refs_3_
  20.1 1.3 %shard_map.182 = (bf16[128,128]{1,0:T(8,128)(2,1)S(1)}, bf16[128,128]{1,0:T(8,128)(2,1)S(1)}, bf16[128,128]{1,0:T(8,128)(2,1)S(1)}, bf16[128,128]{1,0:T(8,128)(2,1)S(1)}) custom-call(bf16[16,256]{1,0:T(8,128)(2,1)S(1)} %shard_map.178.near_bias_ref, bf16[16,256]{1,0:T(8,128)(2,1)S(1)} %collective-permute-done.3.after_bias_ref.far_bias_ref, ...), custom_call_target="tpu_custom_call" | custom-call | flops 3000000000 | bytes 1490944 | tf_op jit(solution)/shard_map/pallas_call | solution.py:375
  21.4 2.0 %collective-permute-start.10 = (bf16[128,128]{1,0:T(8,128)(2,1)S(1)}, bf16[128,128]{1,0:T(8,128)(2,1)S(1)}, u32[]{:S(2)}, u32[]{:S(2)}) collective-permute-start(bf16[128,128]{1,0:T(8,128)(2,1)S(1)} %get-tuple-element.35), channel_id=1, source_target_pairs={{0,4},{4,0},{8,12},{12,8},{16,20},{20,16},{24,28},{28,24},{1,5},{5... | collective-permute-start | bytes 98312 | tf_op jit(solution)/shard_map/ppermute | solution.py:388
  23.4 1.0 %collective-permute-start.11 = (bf16[128,128]{1,0:T(8,128)(2,1)S(1)}, bf16[128,128]{1,0:T(8,128)(2,1)S(1)}, u32[]{:S(2)}, u32[]{:S(2)}) collective-permute-start(bf16[128,128]{1,0:T(8,128)(2,1)S(1)} %get-tuple-element.36), channel_id=1, source_target_pairs={{0,20},{4,16},{8,28},{12,24},{16,4},{20,0},{24,12},{28,8},{1,21},{... | collective-permute-start | bytes 98312 | tf_op jit(solution)/shard_map/ppermute | solution.py:388
  24.4 0.0 collective-permute-done.12.refs_5_
  24.4 0.5 %collective-permute-start.9 = (bf16[128,128]{1,0:T(8,128)(2,1)S(1)}, bf16[128,128]{1,0:T(8,128)(2,1)S(1)}, u32[]{:S(2)}, u32[]{:S(2)}) collective-permute-start(bf16[128,128]{1,0:T(8,128)(2,1)S(1)} %get-tuple-element.34), channel_id=1, source_target_pairs={{0,16},{4,20},{8,24},{12,28},{16,0},{20,4},{24,8},{28,12},{1,17},{... | collective-permute-start | bytes 98312 | tf_op jit(solution)/shard_map/ppermute | solution.py:388
  25.0 0.0 collective-permute-done.13.refs_6_
  25.0 0.0 collective-permute-done.14.refs_7_
  25.0 2.4 %shard_map.183.pair_ref = bf16[128,32]{1,0:T(8,128)(2,1)S(1)} custom-call(bf16[320,256]{1,0:T(8,128)(2,1)S(1)} %get-tuple-element.22.refs_0_, bf16[320,256]{1,0:T(8,128)(2,1)S(1)} %collective-permute-done.refs_1_, bf16[320,256]{1,0:T(8,128)(2,1)S(1)} %collective-permute-done.7.refs_0_.refs_2_, bf16[320,256]{1,0:T(8,128)(2,1)S(1)} %collective-permute-done.8.refs_1_.refs_3_, ...), custom_call_target="tpu_custom_call" | custom-call | bytes 1319936 | tf_op jit(solution)/shard_map/pallas_call | solution.py:375
  27.4 0.0 collective-permute-done.10.row_ref
  27.4 0.9 %collective-permute-done.11.both_ref = bf16[128,128]{1,0:T(8,128)(2,1)S(1)} collective-permute-done((bf16[128,128]{1,0:T(8,128)(2,1)S(1)}, bf16[128,128]{1,0:T(8,128)(2,1)S(1)}, u32[]{:S(2)}, u32[]{:S(2)}) %collective-permute-start.11) | collective-permute-done | bytes 32800 | tf_op jit(solution)/shard_map/ppermute | solution.py:388
  28.2 0.3 %collective-permute-done.9.branch_ref = bf16[128,128]{1,0:T(8,128)(2,1)S(1)} collective-permute-done((bf16[128,128]{1,0:T(8,128)(2,1)S(1)}, bf16[128,128]{1,0:T(8,128)(2,1)S(1)}, u32[]{:S(2)}, u32[]{:S(2)}) %collective-permute-start.9) | collective-permute-done | bytes 32800 | tf_op jit(solution)/shard_map/ppermute | solution.py:388
  28.6 0.7 %shard_map.184 = (bf16[512,128]{1,0:T(8,128)(2,1)}, bf16[128,32]{1,0:T(8,128)(2,1)}) custom-call(bf16[128,128]{1,0:T(8,128)(2,1)S(1)} %get-tuple-element.33.own_ref, bf16[128,128]{1,0:T(8,128)(2,1)S(1)} %collective-permute-done.9.branch_ref, bf16[128,128]{1,0:T(8,128)(2,1)S(1)} %collective-permute-done.10.row_ref, ...), custom_call_target="tpu_custom_call" | custom-call | bytes 278528 | tf_op jit(solution)/shard_map/pallas_call | solution.py:375
  (27 shorter events, 0.1 us)
Async XLA Ops:
  0.6 1.0 %copy-start.1 = (bf16[64,8,256]{2,1,0:T(8,128)(2,1)S(1)}, bf16[64,8,256]{2,1,0:T(8,128)(2,1)}, u32[]{:S(2)}) copy-start(bf16[64,8,256]{2,1,0:T(8,128)(2,1)} %param.17) | copy-start | bytes 786436
  0.6 0.9 %copy-start.4 = (bf16[256,2,32]{0,2,1:T(8,128)(2,1)S(1)}, bf16[256,2,32]{0,2,1:T(8,128)(2,1)}, u32[]{:S(2)}) copy-start(bf16[256,2,32]{0,2,1:T(8,128)(2,1)} %param.23) | copy-start | bytes 98308
  0.7 0.9 %copy-start.3 = (bf16[32,8,32]{2,1,0:T(8,128)(2,1)S(1)}, bf16[32,8,32]{2,1,0:T(8,128)(2,1)}, u32[]{:S(2)}) copy-start(bf16[32,8,32]{2,1,0:T(8,128)(2,1)} %pair_ref.1) | copy-start | bytes 49156
  0.7 0.9 %copy-start.5 = (bf16[4,32,128]{2,1,0:T(8,128)(2,1)S(1)}, bf16[4,32,128]{2,1,0:T(8,128)(2,1)}, u32[]{:S(2)}) copy-start(bf16[4,32,128]{2,1,0:T(8,128)(2,1)} %input_ref.1) | copy-start | bytes 98308
  0.7 0.9 %copy-start.6 = (bf16[128,128]{1,0:T(8,128)(2,1)S(1)}, bf16[128,128]{1,0:T(8,128)(2,1)}, u32[]{:S(2)}) copy-start(bf16[128,128]{1,0:T(8,128)(2,1)} %up_ref.1) | copy-start | bytes 98308
  0.7 0.9 %copy-start.7 = (bf16[128,128]{1,0:T(8,128)(2,1)S(1)}, bf16[128,128]{1,0:T(8,128)(2,1)}, u32[]{:S(2)}) copy-start(bf16[128,128]{1,0:T(8,128)(2,1)} %down_ref.1) | copy-start | bytes 98308
  0.7 0.9 %copy-start.9 = (bf16[128,32]{0,1:T(8,128)(2,1)S(1)}, bf16[128,32]{0,1:T(8,128)(2,1)}, u32[]{:S(2)}) copy-start(bf16[128,32]{0,1:T(8,128)(2,1)} %param.30) | copy-start | bytes 24580
  0.7 0.9 %copy-start.14 = (f32[32]{0:T(128)S(1)}, f32[32]{0:T(128)}, u32[]{:S(2)}) copy-start(f32[32]{0:T(128)} %param.29) | copy-start | bytes 388
  0.7 12.1 %copy-start.16 = (bf16[256,4,256]{2,1,0:T(4,128)(2,1)S(1)}, bf16[256,4,256]{2,1,0:T(4,128)(2,1)}, u32[]{:S(2)}) copy-start(bf16[256,4,256]{2,1,0:T(4,128)(2,1)} %param.21) | copy-start | bytes 1572868
  0.7 0.9 %copy-start.8 = (bf16[32,128]{1,0:T(8,128)(2,1)S(1)}, bf16[32,128]{1,0:T(8,128)(2,1)}, u32[]{:S(2)}) copy-start(bf16[32,128]{1,0:T(8,128)(2,1)} %gate_ref.1) | copy-start | bytes 24580
  0.7 0.9 %copy-start.10 = (f32[256]{0:T(256)S(1)}, f32[256]{0:T(256)}, u32[]{:S(2)}) copy-start(f32[256]{0:T(256)} %param.20) | copy-start | bytes 3076
  2.2 7.4 %collective-permute-start = (bf16[320,256]{1,0:T(8,128)(2,1)S(1)}, bf16[320,256]{1,0:T(8,128)(2,1)S(1)}, u32[]{:S(2)}, u32[]{:S(2)}) collective-permute-start(bf16[320,256]{1,0:T(8,128)(2,1)S(1)} %get-tuple-element.22.refs_0_), channel_id=1, source_target_pairs={{0,2},{1,3},{2,0},{3,1},{4,6},{5,7},{6,4},{7,5},{8,10},{9,11},{10,... | collective-permute-start | bytes 491528 | tf_op jit(solution)/shard_map/ppermute | solution.py:388
  5.2 11.2 %collective-permute-start.5 = (bf16[224,256]{1,0:T(8,128)(2,1)S(1)}, bf16[224,256]{1,0:T(8,128)(2,1)S(1)}, u32[]{:S(2)}, u32[]{:S(2)}) collective-permute-start(bf16[224,256]{1,0:T(8,128)(2,1)S(1)} %get-tuple-element.24.own_ref), channel_id=1, source_target_pairs={{0,8},{4,12},{8,0},{12,4},{1,9},{5,13},{9,1},{13,5},{2,10},{6,14},... | collective-permute-start | bytes 344072 | tf_op jit(solution)/shard_map/ppermute | solution.py:388
  7.8 8.6 %collective-permute-start.4 = (bf16[224,256]{1,0:T(8,128)(2,1)S(1)}, bf16[224,256]{1,0:T(8,128)(2,1)S(1)}, u32[]{:S(2)}, u32[]{:S(2)}) collective-permute-start(bf16[224,256]{1,0:T(8,128)(2,1)S(1)} %get-tuple-element.25), channel_id=1, source_target_pairs={{0,4},{4,0},{8,12},{12,8},{1,5},{5,1},{9,13},{13,9},{2,6},{6,2},{1... | collective-permute-start | bytes 344072 | tf_op jit(solution)/shard_map/ppermute | solution.py:388
  9.4 7.4 %collective-permute-start.6 = (bf16[224,256]{1,0:T(8,128)(2,1)S(1)}, bf16[224,256]{1,0:T(8,128)(2,1)S(1)}, u32[]{:S(2)}, u32[]{:S(2)}) collective-permute-start(bf16[224,256]{1,0:T(8,128)(2,1)S(1)} %get-tuple-element.25), channel_id=1, source_target_pairs={{0,12},{4,8},{8,4},{12,0},{1,13},{5,9},{9,5},{13,1},{2,14},{6,10},... | collective-permute-start | bytes 344072 | tf_op jit(solution)/shard_map/ppermute | solution.py:388
  9.6 1.4 %copy-start.15 = (bf16[128,8]{0,1:T(8,128)(2,1)S(1)}, bf16[128,8]{0,1:T(8,128)(2,1)}, u32[]{:S(2)}) copy-start(bf16[128,8]{0,1:T(8,128)(2,1)} %param.25) | copy-start | bytes 6148
  9.6 1.2 %collective-permute-start.1 = (bf16[32,256]{1,0:T(8,128)(2,1)S(1)}, bf16[32,256]{1,0:T(8,128)(2,1)S(1)}, u32[]{:S(2)}, u32[]{:S(2)}) collective-permute-start(bf16[32,256]{1,0:T(8,128)(2,1)S(1)} %get-tuple-element.23), channel_id=1, source_target_pairs={{0,1},{1,0},{2,3},{3,2},{4,5},{5,4},{6,7},{7,6},{8,9},{9,8},{10,11... | collective-permute-start | bytes 49160 | tf_op jit(solution)/shard_map/ppermute | solution.py:388
  9.6 1.3 %collective-permute-start.2 = (bf16[32,256]{1,0:T(8,128)(2,1)S(1)}, bf16[32,256]{1,0:T(8,128)(2,1)S(1)}, u32[]{:S(2)}, u32[]{:S(2)}) collective-permute-start(bf16[32,256]{1,0:T(8,128)(2,1)S(1)} %slice.4), channel_id=1, source_target_pairs={{0,1},{1,0},{2,3},{3,2},{4,5},{5,4},{6,7},{7,6},{8,9},{9,8},{10,11... | collective-permute-start | bytes 49160 | tf_op jit(solution)/shard_map/ppermute | solution.py:388
  11.3 5.5 %collective-permute-start.3 = (bf16[16,256]{1,0:T(8,128)(2,1)S(1)}, bf16[16,256]{1,0:T(8,128)(2,1)S(1)}, u32[]{:S(2)}, u32[]{:S(2)}) collective-permute-start(bf16[16,256]{1,0:T(8,128)(2,1)S(1)} %shard_map.178.near_bias_ref), channel_id=1, source_target_pairs={{0,4},{4,0},{8,12},{12,8},{1,5},{5,1},{9,13},{13,9},{2,6},{6,2},{1... | collective-permute-start | bytes 24584 | tf_op jit(solution)/shard_map/ppermute | solution.py:388
  12.8 7.3 %collective-permute-start.7 = (bf16[320,256]{1,0:T(8,128)(2,1)S(1)}, bf16[320,256]{1,0:T(8,128)(2,1)S(1)}, u32[]{:S(2)}, u32[]{:S(2)}) collective-permute-start(bf16[320,256]{1,0:T(8,128)(2,1)S(1)} %get-tuple-element.22.refs_0_), channel_id=1, source_target_pairs={{0,1},{1,0},{2,3},{3,2},{4,5},{5,4},{6,7},{7,6},{8,9},{9,8},{10,11... | collective-permute-start | bytes 491528 | tf_op jit(solution)/shard_map/ppermute | solution.py:388
  12.8 1.0 %copy-start = (bf16[32,32,128]{2,1,0:T(8,128)(2,1)S(1)}, bf16[32,32,128]{2,1,0:T(8,128)(2,1)}, u32[]{:S(2)}) copy-start(bf16[32,32,128]{2,1,0:T(8,128)(2,1)} %param.24) | copy-start | bytes 786436
  12.8 1.0 %copy-start.2 = (bf16[256,256]{1,0:T(8,128)(2,1)S(1)}, bf16[256,256]{1,0:T(8,128)(2,1)}, u32[]{:S(2)}) copy-start(bf16[256,256]{1,0:T(8,128)(2,1)} %refs_1_.1) | copy-start | bytes 393220
  12.8 1.0 %copy-start.13 = (f32[128]{0:T(128)S(1)}, f32[128]{0:T(128)}, u32[]{:S(2)}) copy-start(f32[128]{0:T(128)} %param.31) | copy-start | bytes 1540
  12.9 0.9 %copy-start.11 = (f32[256]{0:T(256)S(1)}, f32[256]{0:T(256)}, u32[]{:S(2)}) copy-start(f32[256]{0:T(256)} %param.19) | copy-start | bytes 3076
  13.0 0.9 %copy-start.12 = (f32[128]{0:T(128)S(1)}, f32[128]{0:T(128)}, u32[]{:S(2)}) copy-start(f32[128]{0:T(128)} %param.26) | copy-start | bytes 1540
  16.4 3.7 %collective-permute-start.8 = (bf16[320,256]{1,0:T(8,128)(2,1)S(1)}, bf16[320,256]{1,0:T(8,128)(2,1)S(1)}, u32[]{:S(2)}, u32[]{:S(2)}) collective-permute-start(bf16[320,256]{1,0:T(8,128)(2,1)S(1)} %collective-permute-done.refs_1_), channel_id=1, source_target_pairs={{0,1},{1,0},{2,3},{3,2},{4,5},{5,4},{6,7},{7,6},{8,9},{9,8},{10,11... | collective-permute-start | bytes 491528 | tf_op jit(solution)/shard_map/ppermute | solution.py:388
  16.9 7.6 %collective-permute-start.12 = (bf16[192,256]{1,0:T(8,128)(2,1)S(1)}, bf16[192,256]{1,0:T(8,128)(2,1)S(1)}, u32[]{:S(2)}, u32[]{:S(2)}) collective-permute-start(bf16[192,256]{1,0:T(8,128)(2,1)S(1)} %shard_map.180.refs_0_.refs_4_), channel_id=1, source_target_pairs={{0,2},{1,3},{2,0},{3,1},{4,6},{5,7},{6,4},{7,5},{8,10},{9,11},{10,... | collective-permute-start | bytes 294920 | tf_op jit(solution)/shard_map/ppermute | solution.py:388
  17.4 7.5 %collective-permute-start.13 = (bf16[192,256]{1,0:T(8,128)(2,1)S(1)}, bf16[192,256]{1,0:T(8,128)(2,1)S(1)}, u32[]{:S(2)}, u32[]{:S(2)}) collective-permute-start(bf16[192,256]{1,0:T(8,128)(2,1)S(1)} %shard_map.180.refs_0_.refs_4_), channel_id=1, source_target_pairs={{0,1},{1,0},{2,3},{3,2},{4,5},{5,4},{6,7},{7,6},{8,9},{9,8},{10,11... | collective-permute-start | bytes 294920 | tf_op jit(solution)/shard_map/ppermute | solution.py:388
  17.5 7.5 %collective-permute-start.14 = (bf16[192,256]{1,0:T(8,128)(2,1)S(1)}, bf16[192,256]{1,0:T(8,128)(2,1)S(1)}, u32[]{:S(2)}, u32[]{:S(2)}) collective-permute-start(bf16[192,256]{1,0:T(8,128)(2,1)S(1)} %shard_map.180.refs_0_.refs_4_), channel_id=1, source_target_pairs={{0,3},{1,2},{2,1},{3,0},{4,7},{5,6},{6,5},{7,4},{8,11},{9,10},{10,... | collective-permute-start | bytes 294920 | tf_op jit(solution)/shard_map/ppermute | solution.py:388
  21.4 6.0 %collective-permute-start.10 = (bf16[128,128]{1,0:T(8,128)(2,1)S(1)}, bf16[128,128]{1,0:T(8,128)(2,1)S(1)}, u32[]{:S(2)}, u32[]{:S(2)}) collective-permute-start(bf16[128,128]{1,0:T(8,128)(2,1)S(1)} %get-tuple-element.35), channel_id=1, source_target_pairs={{0,4},{4,0},{8,12},{12,8},{16,20},{20,16},{24,28},{28,24},{1,5},{5... | collective-permute-start | bytes 98312 | tf_op jit(solution)/shard_map/ppermute | solution.py:388
  23.4 4.8 %collective-permute-start.11 = (bf16[128,128]{1,0:T(8,128)(2,1)S(1)}, bf16[128,128]{1,0:T(8,128)(2,1)S(1)}, u32[]{:S(2)}, u32[]{:S(2)}) collective-permute-start(bf16[128,128]{1,0:T(8,128)(2,1)S(1)} %get-tuple-element.36), channel_id=1, source_target_pairs={{0,20},{4,16},{8,28},{12,24},{16,4},{20,0},{24,12},{28,8},{1,21},{... | collective-permute-start | bytes 98312 | tf_op jit(solution)/shard_map/ppermute | solution.py:388
  24.4 4.1 %collective-permute-start.9 = (bf16[128,128]{1,0:T(8,128)(2,1)S(1)}, bf16[128,128]{1,0:T(8,128)(2,1)S(1)}, u32[]{:S(2)}, u32[]{:S(2)}) collective-permute-start(bf16[128,128]{1,0:T(8,128)(2,1)S(1)} %get-tuple-element.34), channel_id=1, source_target_pairs={{0,16},{4,20},{8,24},{12,28},{16,0},{20,4},{24,8},{28,12},{1,17},{... | collective-permute-start | bytes 98312 | tf_op jit(solution)/shard_map/ppermute | solution.py:388

commit v4 on v3

--- a/solution.py
+++ b/solution.py
@@ -341,19 +341,10 @@
     )
 
 
-def group_maximum(values, group):
-    tiles = []
-    for start in range(0, values.shape[1], 128):
-        tile = values[:, start : start + 128]
-        lane = lax.broadcasted_iota(jnp.int32, tile.shape, 1)
-        step = 1
-        while step < group:
-            ahead = pltpu.roll(tile, 128 - step, 1)
-            behind = pltpu.roll(tile, step, 1)
-            tile = jnp.maximum(tile, jnp.where((lane & step) == 0, ahead, behind))
-            step *= 2
-        tiles.append(tile)
-    return jnp.concatenate(tiles, axis=1)
+def head_mask(groups, rows, head_size):
+    shape = (groups * rows, groups * head_size)
+    row = lax.broadcasted_iota(jnp.int32, shape, 0) // rows
+    return row == lax.broadcasted_iota(jnp.int32, shape, 1) // head_size
 
 
 def same_group(rows, columns, group):
@@ -394,14 +385,13 @@
 
 def send_kernel(
     sizes, rows_ref, pair_ref, gain_ref, weight_ref, input_ref, gate_ref, tri_gain_ref, output_ref, up_ref,
-    down_ref, token_ref, same_ref, other_ref, shared_ref, flat_ref, wide,
+    down_ref, token_ref, same_ref, other_ref, shared_ref, wide,
 ):
     sequences, local_rows, residues, chan_local, outer_width = sizes
     part = sequences // 4
     part_rows = part * local_rows
     pair = widened(pair_ref[...])
     flat_pair = rounded(jnp.concatenate([pair[:, i, :] for i in range(local_rows)], axis=1))
-    flat_ref[...] = flat_pair
     shared_ref[0:chan_local, :] = flat_pair
     at = chan_local + sequences
     narrow = gate_ref.shape[1]
@@ -432,6 +422,13 @@
     other_ref[base : base + sequences, :] = same_ref[base : base + sequences, :]
 
 
+def pack_kernel(chan_local, own_ref, other_ref, pair_ref, rest_ref):
+    rest = own_ref.shape[0] - chan_local
+    for k, ref in enumerate((own_ref, other_ref)):
+        pair_ref[k * chan_local : (k + 1) * chan_local, :] = ref[:chan_local, :]
+        rest_ref[k * rest : (k + 1) * rest, :] = ref[chan_local:, :]
+
+
 def keep_kernel(*refs):
     count = len(refs) // 2
     for source, target in zip(refs[:count], refs[count:]):
@@ -486,32 +483,34 @@
     values_ref[...] = rounded(product(normed, weight_ref[:, 2 * heads : 3 * heads]))
     gate_ref[...] = rounded(jax.nn.sigmoid(product(query_rows, weight_ref[:, 3 * heads :])))
     groups = heads // head_size
-    mask = same_group(groups * residues, heads, head_size)
+    mask = head_mask(groups, half, head_size)
     for s in range(part):
-        one = keys[s * residues : (s + 1) * residues]
+        one = query[s * half : (s + 1) * half]
         spread = jnp.where(mask, jnp.concatenate([one] * groups, axis=0), jnp.bfloat16(0))
-        score_ref[s * half : (s + 1) * half, :] = product(
-            query[s * half : (s + 1) * half], spread, 1, 1
-        )
-
-
-def bias_kernel(chan_local, pair_refs, matrix_ref, bias_ref, full, flat):
+        score_ref[s * residues : (s + 1) * residues, :] = product(
+            keys[s * residues : (s + 1) * residues], spread, 1, 1
+        )
+
+
+def bias_kernel(chan_local, local_rows, pair_refs, matrix_ref, bias_ref, full):
     groups = matrix_ref.shape[0]
-    residues = flat.shape[1] // groups
-    local_rows = flat.shape[0]
+    residues = bias_ref.shape[0]
     seq = lax.axis_index("seq")
     for distance, ref in zip((0, 2, 1, 3), pair_refs):
         place = pl.ds(pl.multiple_of((seq ^ distance) * chan_local, chan_local), chan_local)
         full[place, :] = widened(ref[0:chan_local, :])
     plain = rounded(layer_normalize(full[...], 0))
-    bias = product(matrix_ref[...], plain)
+    bias = rounded(product(matrix_ref[...], plain).T)
+    lanes = bias_ref.shape[1]
+    half = lanes // groups
+    head = lax.broadcasted_iota(jnp.int32, (groups, lanes), 0)
+    lane = lax.broadcasted_iota(jnp.int32, (groups, lanes), 1)
+    first = lax.rem(lax.axis_index("row"), 2) * local_rows
+    total = jnp.zeros(bias_ref.shape, jnp.float32)
     for i in range(local_rows):
-        for h in range(groups):
-            flat[i : i + 1, h * residues : (h + 1) * residues] = bias[
-                h : h + 1, i * residues : (i + 1) * residues
-            ]
-    rows = rounded(flat[...])
-    bias_ref[...] = jnp.concatenate([rows, rows], axis=0)
+        pick = jnp.where(lane == head * half + first + i, jnp.bfloat16(1), jnp.bfloat16(0))
+        total += product(bias[i * residues : (i + 1) * residues, :], pick)
+    bias_ref[...] = rounded(total)
 
 
 def mix_kernel(
@@ -527,21 +526,17 @@
     groups = heads // head_size
     row = lax.axis_index("row")
     branch = lax.axis_index("branch")
-    first = lax.broadcasted_iota(jnp.int32, near_bias_ref.shape, 0) // local_rows == lax.rem(row, 2)
-    bias_rows = jnp.where(first, widened(near_bias_ref[...]), widened(far_bias_ref[...]))
-    scores = (
-        score_ref[...].reshape(part, half, groups * residues) + bias_rows[None]
-    ).reshape(part * half, groups * residues)
-    weights = rounded(jnp.exp(scores - group_maximum(scores, residues)))
-    mask = same_group(groups * residues, heads, head_size)
-    ones = jnp.where(mask, jnp.bfloat16(1), jnp.bfloat16(0))
-    totals = product(weights, ones)
+    bias = widened(near_bias_ref[...]) + widened(far_bias_ref[...])
+    scores = score_ref[...].reshape(part, residues, groups * half) + bias[None]
+    weights = jnp.exp(scores - jnp.max(scores, axis=1, keepdims=True))
+    weights = rounded(weights / jnp.sum(weights, axis=1, keepdims=True))
+    mask = head_mask(groups, half, head_size)
     attended = []
     for s in range(part):
-        one = values_ref[s * residues : (s + 1) * residues, :]
-        spread = jnp.where(mask, jnp.concatenate([one] * groups, axis=0), jnp.bfloat16(0))
-        attended.append(product(weights[s * half : (s + 1) * half], spread))
-    mixed = rounded(widened(gate_ref[...]) * (jnp.concatenate(attended, axis=0) / totals))
+        every = product(weights[s], values_ref[s * residues : (s + 1) * residues, :], 0, 0)
+        every = jnp.where(mask, every, 0.0).reshape(groups, half, heads)
+        attended.append(jnp.sum(every, axis=0))
+    mixed = rounded(widened(gate_ref[...]) * jnp.concatenate(attended, axis=0))
     projected = product(mixed, mixing_ref[...])
     width = projected.shape[1]
     module[...] = projected.reshape(part, half, width)
@@ -574,7 +569,7 @@
 
 
 def pair_kernel(
-    sizes, shared_refs, pair_refs, gain_ref, transition_gain_ref, outer_weight_ref, seq_total, hidden_local,
+    sizes, row_refs, rest_refs, pair_refs, gain_ref, transition_gain_ref, outer_weight_ref, seq_total, hidden_local,
     output_ref, rows, columns, gates, outer, outer_flat, ordered, final,
 ):
     sequences, local_rows, residues, chan_local, outer_width = sizes
@@ -584,10 +579,9 @@
     width = 4 * chan_local
     chan = chan_local
     gain = as_column(gain_ref[...])
-    at = chan + sequences
-    weight_refs = [ref.at[at:, 0:width] for ref in shared_refs]
-    hidden_refs = [ref.at[at:, width:] for ref in shared_refs]
-    for distance, row_ref, pair_ref, weight_ref in zip((0, 2, 1, 3), shared_refs, pair_refs, weight_refs):
+    weight_refs = [ref.at[sequences:, 0:width] for ref in rest_refs]
+    hidden_refs = [ref.at[sequences:, width:] for ref in rest_refs]
+    for distance, row_ref, pair_ref, weight_ref in zip((0, 2, 1, 3), row_refs, pair_refs, weight_refs):
         place = pl.ds(pl.multiple_of((seq ^ distance) * chan, chan), chan)
         rows[place, :] = row_ref[0:chan, :]
         for k in range(2):
@@ -634,7 +628,7 @@
         down += product(hidden, down_weight, 1, 1)
     pair_next = widened(rounded(first_update + down))
 
-    lefts = jnp.concatenate([ref[chan : chan + sequences, :] for ref in shared_refs], axis=0)
+    lefts = jnp.concatenate([ref[:sequences, :] for ref in rest_refs], axis=0)
     base = 2 * chan
     rights = jnp.concatenate(
         [
@@ -692,30 +686,29 @@
     (token,) = kernel_call(start_kernel, [shape(8, 128, dtype=full_type)], [], flops=5 * 10**9)
     hidden_local = transition_up_weight.shape[0]
     shared_rows = chan_local + sequences + 7 * chan_local
-    same, other, shared, pair_flat = kernel_call(
+    same, other, shared = kernel_call(
         functools.partial(send_kernel, sizes),
         [shape(message_rows, width), shape(message_rows, width),
-         shape(shared_rows, width), shape(chan_local, local_rows * residues)],
+         shape(shared_rows, width)],
         [rows_flat, pairwise_input, product_gain[None], outer_weight_flat, triangle_input_weight,
          triangle_gate_weight, triangle_gain[None], triangle_output_weight.T, transition_up_weight,
          transition_down_weight, token],
         [pltpu.VMEM((sequences * local_rows, 128), full_type)],
     )
     shared_x = exchange(shared, "seq", 2)
-    shared_core = exchange(shared, "seq", 1)
-    shared_both = exchange(shared_x, "seq", 1)
-    shareds = (shared, shared_x, shared_core, shared_both)
+    pair_two, rest_two = kernel_call(
+        functools.partial(pack_kernel, chan_local),
+        [shape(2 * chan_local, width), shape(2 * (shared_rows - chan_local), width)],
+        [shared, shared_x],
+    )
+    pair_core = exchange(pair_two, "seq", 1)
+    rest_core = exchange(rest_two, "seq", 1)
     from_three = exchange(other, "row", 3)
     from_two = exchange(same, "row", 2)
     from_one = exchange(other, "row", 1)
     received = (same, from_one, from_two, from_three)
 
-    pair_core = exchange(pair_flat, "seq", 1)
-    pair_both = exchange(shared_x[0:chan_local], "seq", 1)
-    pairs = (shared, shared_x, pair_core, pair_both)
-
-
-    late_weight = lax.optimization_barrier((attention_weight, pair_flat))[0]
+    late_weight = lax.optimization_barrier((attention_weight, shared))[0]
     kept = [late_weight.reshape(width, 4 * heads), mixing_weight,
             outer_output_weight.reshape(outer_width * outer_width, pair_width),
             alignment_gain[None], pairwise_gain[None], transition_gain[None]]
@@ -724,15 +717,14 @@
     )
 
     def bias_body(*refs):
-        bias_kernel(chan_local, refs[:4], *refs[4:])
+        bias_kernel(chan_local, local_rows, (refs[0], refs[1], refs[2].at[:chan_local], refs[2].at[chan_local:]), *refs[3:])
 
     (near_bias,) = kernel_call(
         bias_body,
-        [shape(half, groups * residues)],
-        [*pairs, bias_matrix.T],
+        [shape(residues, groups * half)],
+        [shared, shared_x, pair_core, bias_matrix.T],
         [
             pltpu.VMEM((pair_width, local_rows * residues), full_type),
-            pltpu.VMEM((local_rows, groups * residues), full_type),
         ],
         flops=BIAS_COST,
     )
@@ -750,7 +742,7 @@
 
     scores, values, gate = kernel_call(
         functools.partial(score_kernel, sizes),
-        [shape(part * half, groups * residues, dtype=full_type), shape(part * residues, heads), shape(part * half, heads)],
+        [shape(part * residues, groups * half, dtype=full_type), shape(part * residues, heads), shape(part * half, heads)],
         [*received, row_gain, attention_kept, relay],
         [pltpu.VMEM((part, residues, width), full_type)],
         flops=3 * 10**9,
@@ -759,7 +751,7 @@
     near_here, near_there, far_here, far_there = kernel_call(
         functools.partial(mix_kernel, sizes),
         [shape(part_rows, width // 2)] * 4,
-        [near_bias, far_bias, scores, values, gate, mixing_kept, same, from_one, shared_core, shared_both],
+        [near_bias, far_bias, scores, values, gate, mixing_kept, same, from_one, rest_core, relay_core],
         [pltpu.VMEM((part, half, width), full_type)],
         flops=3 * 10**9,
     )
@@ -770,12 +762,16 @@
     from_row = exchange(far_here, axes, 1)
 
     def pair_body(*refs):
-        pair_kernel(sizes, refs[:4], refs[4:8], *refs[8:11], sequences * 4, hidden_local, *refs[11:])
+        own, other, pair, rest = refs[:4]
+        count = rest.shape[0] // 2
+        row_refs = (own, other, pair.at[:chan_local], pair.at[chan_local:])
+        rest_refs = (own.at[chan_local:], other.at[chan_local:], rest.at[:count], rest.at[count:])
+        pair_kernel(sizes, row_refs, rest_refs, refs[4:8], *refs[8:11], sequences * 4, hidden_local, *refs[11:])
 
     (pair_done,) = kernel_call(
         pair_body,
         [shape(local_rows * half, chan_local)],
-        [*shareds, *relays, pair_gain, last_gain, outer_kept],
+        [shared, shared_x, pair_core, rest_core, *relays, pair_gain, last_gain, outer_kept],
         [
             pltpu.VMEM((pair_width, local_rows * residues), half_type),
             pltpu.VMEM((2, pair_width, local_rows * residues), half_type),

time: 29.4 us -> 28.6 us (0.973)
  Pallas kernels: 6.37 us -> 5.73 us
    pallas_call x9 -> x10, Pallas kernels: 6.37 us -> 5.73 us  [kernel_call(): pl.pallas_call(body, out_shape=outputs, in_specs=[hbm if i in in_hbm else...]
    ppermute x15 -> x13, waiting for transfers between devices: 4.98 us -> 4.86 us  [exchange(): lax.ppermute(value, axes, [(i, i ^ distance) for i in range(members)])]
    ppermute x15 -> x13, starting transfers between devices: 15.2 us -> 15.2 us  [exchange(): lax.ppermute(value, axes, [(i, i ^ distance) for i in range(members)])]
  transfers between devices with their start and end apart: 15 -> 13, of which waited for: 6 -> 5; matrix products, arithmetic and copies ran while one was open for 0% -> 0% of each run, Pallas kernels for 18% -> 16%
where the time goes in v4:
time: 28.6 us; the launch traced here: 28.5 us
  starting transfers between devices  15.2 us (53%)
  Pallas kernels  5.73 us (20%)
  waiting for transfers between devices  4.86 us (17%)
  local copies, waits for them, and re-layouts  1.85 us (6%)
  between operations  0.88 us (3%)
    ppermute x13, starting transfers between devices, exchange(): lax.ppermute(value, axes, [(i, i ^ distance) for i in range(members)])  15.2 us
    pallas_call x10, Pallas kernels, kernel_call(): pl.pallas_call(body, out_shape=outputs, in_specs=[hbm if i in in_hbm else...  5.73 us
    ppermute x13, waiting for transfers between devices, exchange(): lax.ppermute(value, axes, [(i, i ^ distance) for i in range(members)])  4.86 us
    unnamed x35, local copies, waits for them, and re-layouts  1.85 us
  transfers between devices with their start and end apart: 13, of which 5 were waited for; matrix products, arithmetic and copies ran while one was open for 0% of the time, Pallas kernels for 16%

profile of v4, /device:TPU:0, one launch (start us, length us, event | category | flops | bytes accessed | tf_op | source)
XLA Modules:
  0.0 28.5 jit_solution(12081705785204260573)
XLA Ops:
  0.6 0.0 copy-start.1
  0.6 0.0 copy-start.4
  0.7 0.0 copy-start.3
  0.7 0.0 copy-start.5
  0.7 0.0 copy-start.8
  0.7 0.0 copy-start.10
  0.7 0.8 %copy-done.1 = bf16[64,8,256]{2,1,0:T(8,128)(2,1)S(1)} copy-done((bf16[64,8,256]{2,1,0:T(8,128)(2,1)S(1)}, bf16[64,8,256]{2,1,0:T(8,128)(2,1)}, u32[]{:S(2)}) %copy-start.1) | copy-done | bytes 262168
  1.6 0.0 copy-done.3
  1.6 0.0 copy-start.16
  1.7 0.6 %shard_map.177 = (bf16[224,256]{1,0:T(8,128)(2,1)S(1)}, bf16[224,256]{1,0:T(8,128)(2,1)S(1)}, bf16[320,256]{1,0:T(8,128)(2,1)S(1)}) custom-call(bf16[512,256]{1,0:T(8,128)(2,1)S(1)} %bitcast.20, bf16[32,8,32]{2,1,0:T(8,128)(2,1)S(1)} %copy-done.3, f32[1,256]{1,0:T(1,128)S(1)} %bitcast.23, bf16[64,256]{1,0:T(8,128)(2,1)S(1)} %bitcast.21, ...), custom_call_target="tpu_custom_call" | custom-call | bytes 824448 | tf_op jit(solution)/shard_map/pallas_call | solution.py:366
  2.2 3.0 %collective-permute-start = (bf16[320,256]{1,0:T(8,128)(2,1)S(1)}, bf16[320,256]{1,0:T(8,128)(2,1)S(1)}, u32[]{:S(2)}, u32[]{:S(2)}) collective-permute-start(bf16[320,256]{1,0:T(8,128)(2,1)S(1)} %get-tuple-element.23.own_ref.refs_0_), channel_id=1, source_target_pairs={{0,2},{1,3},{2,0},{3,1},{4,6},{5,7},{6,4},{7,5},{8,10},{9,11},{10,... | collective-permute-start | bytes 491528 | tf_op jit(solution)/shard_map/ppermute | solution.py:379
  5.2 2.6 %collective-permute-start.4 = (bf16[224,256]{1,0:T(8,128)(2,1)S(1)}, bf16[224,256]{1,0:T(8,128)(2,1)S(1)}, u32[]{:S(2)}, u32[]{:S(2)}) collective-permute-start(bf16[224,256]{1,0:T(8,128)(2,1)S(1)} %get-tuple-element.25.own_ref), channel_id=1, source_target_pairs={{0,8},{4,12},{8,0},{12,4},{1,9},{5,13},{9,1},{13,5},{2,10},{6,14},... | collective-permute-start | bytes 344072 | tf_op jit(solution)/shard_map/ppermute | solution.py:379
  7.8 1.6 %collective-permute-start.3 = (bf16[224,256]{1,0:T(8,128)(2,1)S(1)}, bf16[224,256]{1,0:T(8,128)(2,1)S(1)}, u32[]{:S(2)}, u32[]{:S(2)}) collective-permute-start(bf16[224,256]{1,0:T(8,128)(2,1)S(1)} %get-tuple-element.26), channel_id=1, source_target_pairs={{0,4},{4,0},{8,12},{12,8},{1,5},{5,1},{9,13},{13,9},{2,6},{6,2},{1... | collective-permute-start | bytes 344072 | tf_op jit(solution)/shard_map/ppermute | solution.py:379
  9.4 0.2 collective-permute-start.5
  9.6 0.0 collective-permute-done.other_ref.refs_1_
  9.6 0.0 copy-start.15
  9.6 0.1 collective-permute-start.1
  9.7 0.5 %collective-permute-start.6 = (bf16[576,256]{1,0:T(8,128)(2,1)S(1)}, bf16[576,256]{1,0:T(8,128)(2,1)S(1)}, u32[]{:S(2)}, u32[]{:S(2)}) collective-permute-start(bf16[576,256]{1,0:T(8,128)(2,1)S(1)} %get-tuple-element.34), channel_id=1, source_target_pairs={{0,1},{1,0},{2,3},{3,2},{4,5},{5,4},{6,7},{7,6},{8,9},{9,8},{10,11... | collective-permute-start | bytes 884744 | tf_op jit(solution)/shard_map/ppermute | solution.py:379
  10.2 0.7 %collective-permute-done.1.refs_2_ = bf16[64,256]{1,0:T(8,128)(2,1)S(1)} collective-permute-done((bf16[64,256]{1,0:T(8,128)(2,1)S(1)}, bf16[64,256]{1,0:T(8,128)(2,1)S(1)}, u32[]{:S(2)}, u32[]{:S(2)}) %collective-permute-start.1) | collective-permute-done | bytes 32800 | tf_op jit(solution)/shard_map/ppermute | solution.py:379
  10.9 0.4 %shard_map.179.near_bias_ref = bf16[32,128]{1,0:T(8,128)(2,1)S(1)} custom-call(bf16[320,256]{1,0:T(8,128)(2,1)S(1)} %get-tuple-element.23.own_ref.refs_0_, bf16[320,256]{1,0:T(8,128)(2,1)S(1)} %collective-permute-done.other_ref.refs_1_, bf16[64,256]{1,0:T(8,128)(2,1)S(1)} %collective-permute-done.1.refs_2_, bf16[8,128]{1,0:T(8,128)(2,1)S(1)} %bitcast.28), custom_call_target="tpu_custom_call" | custom-call | flops 175000000 | bytes 370688 | tf_op jit(solution)/shard_map/pallas_call | solution.py:366
  11.3 1.7 %collective-permute-start.2 = (bf16[32,128]{1,0:T(8,128)(2,1)S(1)}, bf16[32,128]{1,0:T(8,128)(2,1)S(1)}, u32[]{:S(2)}, u32[]{:S(2)}) collective-permute-start(bf16[32,128]{1,0:T(8,128)(2,1)S(1)} %shard_map.179.near_bias_ref), channel_id=1, source_target_pairs={{0,4},{4,0},{8,12},{12,8},{1,5},{5,1},{9,13},{13,9},{2,6},{6,2},{1... | collective-permute-start | bytes 24584 | tf_op jit(solution)/shard_map/ppermute | solution.py:379
  13.0 0.1 copy.19
  13.1 0.0 copy-start.11
  13.1 0.0 copy-start.12
  13.1 0.8 %copy-done = bf16[32,32,128]{2,1,0:T(8,128)(2,1)S(1)} copy-done((bf16[32,32,128]{2,1,0:T(8,128)(2,1)S(1)}, bf16[32,32,128]{2,1,0:T(8,128)(2,1)}, u32[]{:S(2)}) %copy-start) | copy-done | bytes 262168
  14.0 0.0 copy-done.2
  14.0 0.1 shard_map.180
  14.1 2.4 %collective-permute-done.4.two_ref = bf16[224,256]{1,0:T(8,128)(2,1)S(1)} collective-permute-done((bf16[224,256]{1,0:T(8,128)(2,1)S(1)}, bf16[224,256]{1,0:T(8,128)(2,1)S(1)}, u32[]{:S(2)}, u32[]{:S(2)}) %collective-permute-start.4) | collective-permute-done | bytes 114720 | tf_op jit(solution)/shard_map/ppermute | solution.py:379
  16.5 0.0 collective-permute-done.3.one_ref
  16.5 0.4 %collective-permute-done.5.three_ref = bf16[224,256]{1,0:T(8,128)(2,1)S(1)} collective-permute-done((bf16[224,256]{1,0:T(8,128)(2,1)S(1)}, bf16[224,256]{1,0:T(8,128)(2,1)S(1)}, u32[]{:S(2)}, u32[]{:S(2)}) %collective-permute-start.5) | collective-permute-done | bytes 114720 | tf_op jit(solution)/shard_map/ppermute | solution.py:379
  16.8 0.0 collective-permute-done.2.after_bias_ref.far_bias_ref
  16.9 0.1 collective-permute-start.7
  16.9 0.6 %collective-permute-start.11 = (bf16[192,256]{1,0:T(8,128)(2,1)S(1)}, bf16[192,256]{1,0:T(8,128)(2,1)S(1)}, u32[]{:S(2)}, u32[]{:S(2)}) collective-permute-start(bf16[192,256]{1,0:T(8,128)(2,1)S(1)} %shard_map.181.refs_0_.refs_4_), channel_id=1, source_target_pairs={{0,2},{1,3},{2,0},{3,1},{4,6},{5,7},{6,4},{7,5},{8,10},{9,11},{10,... | collective-permute-start | bytes 294920 | tf_op jit(solution)/shard_map/ppermute | solution.py:379
  17.5 1.3 %collective-permute-start.12 = (bf16[192,256]{1,0:T(8,128)(2,1)S(1)}, bf16[192,256]{1,0:T(8,128)(2,1)S(1)}, u32[]{:S(2)}, u32[]{:S(2)}) collective-permute-start(bf16[192,256]{1,0:T(8,128)(2,1)S(1)} %shard_map.181.refs_0_.refs_4_), channel_id=1, source_target_pairs={{0,3},{1,2},{2,1},{3,0},{4,7},{5,6},{6,5},{7,4},{8,11},{9,10},{10,... | collective-permute-start | bytes 294920 | tf_op jit(solution)/shard_map/ppermute | solution.py:379
  18.8 0.9 %shard_map.182 = (f32[512,128]{1,0:T(8,128)S(1)}, bf16[512,256]{1,0:T(8,128)(2,1)S(1)}, bf16[256,256]{1,0:T(8,128)(2,1)S(1)}) custom-call(bf16[224,256]{1,0:T(8,128)(2,1)S(1)} %get-tuple-element.25.own_ref, bf16[224,256]{1,0:T(8,128)(2,1)S(1)} %collective-permute-done.3.one_ref, bf16[224,256]{1,0:T(8,128)(2,1)S(1)} %collective-permute-done.4.two_ref, ...), custom_call_target="tpu_custom_call" | custom-call | flops 3000000000 | bytes 1737728 | tf_op jit(solution)/shard_map/pallas_call | solution.py:366
  19.7 0.0 collective-permute-done.7.refs_1_.refs_6_
  19.7 0.0 collective-permute-done.6.refs_0_.refs_3_
  19.7 0.7 %shard_map.183 = (bf16[128,128]{1,0:T(8,128)(2,1)S(1)}, bf16[128,128]{1,0:T(8,128)(2,1)S(1)}, bf16[128,128]{1,0:T(8,128)(2,1)S(1)}, bf16[128,128]{1,0:T(8,128)(2,1)S(1)}) custom-call(bf16[32,128]{1,0:T(8,128)(2,1)S(1)} %shard_map.179.near_bias_ref, bf16[32,128]{1,0:T(8,128)(2,1)S(1)} %collective-permute-done.2.after_bias_ref.far_bias_ref, ...), custom_call_target="tpu_custom_call" | custom-call | flops 3000000000 | bytes 1556480 | tf_op jit(solution)/shard_map/pallas_call | solution.py:366
  20.4 2.9 %collective-permute-start.10 = (bf16[128,128]{1,0:T(8,128)(2,1)S(1)}, bf16[128,128]{1,0:T(8,128)(2,1)S(1)}, u32[]{:S(2)}, u32[]{:S(2)}) collective-permute-start(bf16[128,128]{1,0:T(8,128)(2,1)S(1)} %get-tuple-element.38), channel_id=1, source_target_pairs={{0,20},{4,16},{8,28},{12,24},{16,4},{20,0},{24,12},{28,8},{1,21},{... | collective-permute-start | bytes 98312 | tf_op jit(solution)/shard_map/ppermute | solution.py:379
  23.4 0.5 %collective-permute-start.8 = (bf16[128,128]{1,0:T(8,128)(2,1)S(1)}, bf16[128,128]{1,0:T(8,128)(2,1)S(1)}, u32[]{:S(2)}, u32[]{:S(2)}) collective-permute-start(bf16[128,128]{1,0:T(8,128)(2,1)S(1)} %get-tuple-element.36), channel_id=1, source_target_pairs={{0,16},{4,20},{8,24},{12,28},{16,0},{20,4},{24,8},{28,12},{1,17},{... | collective-permute-start | bytes 98312 | tf_op jit(solution)/shard_map/ppermute | solution.py:379
  23.9 0.1 collective-permute-start.9
  24.0 0.0 collective-permute-done.11.refs_5_
  24.0 0.0 collective-permute-done.12.refs_7_
  24.0 2.4 %shard_map.184.pair_ref = bf16[128,32]{1,0:T(8,128)(2,1)S(1)} custom-call(bf16[320,256]{1,0:T(8,128)(2,1)S(1)} %get-tuple-element.23.own_ref.refs_0_, bf16[320,256]{1,0:T(8,128)(2,1)S(1)} %collective-permute-done.other_ref.refs_1_, bf16[64,256]{1,0:T(8,128)(2,1)S(1)} %collective-permute-done.1.refs_2_, ...), custom_call_target="tpu_custom_call" | custom-call | bytes 1319936 | tf_op jit(solution)/shard_map/pallas_call | solution.py:366
  26.4 0.0 collective-permute-done.10.both_ref
  26.4 0.9 %collective-permute-done.8.branch_ref = bf16[128,128]{1,0:T(8,128)(2,1)S(1)} collective-permute-done((bf16[128,128]{1,0:T(8,128)(2,1)S(1)}, bf16[128,128]{1,0:T(8,128)(2,1)S(1)}, u32[]{:S(2)}, u32[]{:S(2)}) %collective-permute-start.8) | collective-permute-done | bytes 32800 | tf_op jit(solution)/shard_map/ppermute | solution.py:379
  27.3 0.5 %collective-permute-done.9.row_ref = bf16[128,128]{1,0:T(8,128)(2,1)S(1)} collective-permute-done((bf16[128,128]{1,0:T(8,128)(2,1)S(1)}, bf16[128,128]{1,0:T(8,128)(2,1)S(1)}, u32[]{:S(2)}, u32[]{:S(2)}) %collective-permute-start.9) | collective-permute-done | bytes 32800 | tf_op jit(solution)/shard_map/ppermute | solution.py:379
  27.8 0.7 %shard_map.185 = (bf16[512,128]{1,0:T(8,128)(2,1)}, bf16[128,32]{1,0:T(8,128)(2,1)}) custom-call(bf16[128,128]{1,0:T(8,128)(2,1)S(1)} %get-tuple-element.35.own_ref, bf16[128,128]{1,0:T(8,128)(2,1)S(1)} %collective-permute-done.8.branch_ref, bf16[128,128]{1,0:T(8,128)(2,1)S(1)} %collective-permute-done.9.row_ref, ...), custom_call_target="tpu_custom_call" | custom-call | bytes 278528 | tf_op jit(solution)/shard_map/pallas_call | solution.py:366
  (23 shorter events, 0.1 us)
Async XLA Ops:
  0.6 1.0 %copy-start.1 = (bf16[64,8,256]{2,1,0:T(8,128)(2,1)S(1)}, bf16[64,8,256]{2,1,0:T(8,128)(2,1)}, u32[]{:S(2)}) copy-start(bf16[64,8,256]{2,1,0:T(8,128)(2,1)} %param.17) | copy-start | bytes 786436
  0.6 0.9 %copy-start.4 = (bf16[256,2,32]{0,2,1:T(8,128)(2,1)S(1)}, bf16[256,2,32]{0,2,1:T(8,128)(2,1)}, u32[]{:S(2)}) copy-start(bf16[256,2,32]{0,2,1:T(8,128)(2,1)} %param.23) | copy-start | bytes 98308
  0.7 0.9 %copy-start.3 = (bf16[32,8,32]{2,1,0:T(8,128)(2,1)S(1)}, bf16[32,8,32]{2,1,0:T(8,128)(2,1)}, u32[]{:S(2)}) copy-start(bf16[32,8,32]{2,1,0:T(8,128)(2,1)} %pair_ref.1) | copy-start | bytes 49156
  0.7 0.9 %copy-start.5 = (bf16[4,32,128]{2,1,0:T(8,128)(2,1)S(1)}, bf16[4,32,128]{2,1,0:T(8,128)(2,1)}, u32[]{:S(2)}) copy-start(bf16[4,32,128]{2,1,0:T(8,128)(2,1)} %input_ref.1) | copy-start | bytes 98308
  0.7 0.9 %copy-start.6 = (bf16[128,128]{1,0:T(8,128)(2,1)S(1)}, bf16[128,128]{1,0:T(8,128)(2,1)}, u32[]{:S(2)}) copy-start(bf16[128,128]{1,0:T(8,128)(2,1)} %up_ref.1) | copy-start | bytes 98308
  0.7 0.9 %copy-start.7 = (bf16[128,128]{1,0:T(8,128)(2,1)S(1)}, bf16[128,128]{1,0:T(8,128)(2,1)}, u32[]{:S(2)}) copy-start(bf16[128,128]{1,0:T(8,128)(2,1)} %down_ref.1) | copy-start | bytes 98308
  0.7 0.9 %copy-start.9 = (bf16[128,32]{0,1:T(8,128)(2,1)S(1)}, bf16[128,32]{0,1:T(8,128)(2,1)}, u32[]{:S(2)}) copy-start(bf16[128,32]{0,1:T(8,128)(2,1)} %param.30) | copy-start | bytes 24580
  0.7 0.9 %copy-start.14 = (f32[32]{0:T(128)S(1)}, f32[32]{0:T(128)}, u32[]{:S(2)}) copy-start(f32[32]{0:T(128)} %param.29) | copy-start | bytes 388
  0.7 0.9 %copy-start.8 = (bf16[32,128]{1,0:T(8,128)(2,1)S(1)}, bf16[32,128]{1,0:T(8,128)(2,1)}, u32[]{:S(2)}) copy-start(bf16[32,128]{1,0:T(8,128)(2,1)} %gate_ref.1) | copy-start | bytes 24580
  0.7 0.9 %copy-start.10 = (f32[256]{0:T(256)S(1)}, f32[256]{0:T(256)}, u32[]{:S(2)}) copy-start(f32[256]{0:T(256)} %param.20) | copy-start | bytes 3076
  1.6 11.4 %copy-start.16 = (bf16[256,4,256]{2,1,0:T(4,128)(2,1)S(1)}, bf16[256,4,256]{2,1,0:T(4,128)(2,1)}, u32[]{:S(2)}) copy-start(bf16[256,4,256]{2,1,0:T(4,128)(2,1)} %param.21) | copy-start | bytes 1572868
  2.2 7.4 %collective-permute-start = (bf16[320,256]{1,0:T(8,128)(2,1)S(1)}, bf16[320,256]{1,0:T(8,128)(2,1)S(1)}, u32[]{:S(2)}, u32[]{:S(2)}) collective-permute-start(bf16[320,256]{1,0:T(8,128)(2,1)S(1)} %get-tuple-element.23.own_ref.refs_0_), channel_id=1, source_target_pairs={{0,2},{1,3},{2,0},{3,1},{4,6},{5,7},{6,4},{7,5},{8,10},{9,11},{10,... | collective-permute-start | bytes 491528 | tf_op jit(solution)/shard_map/ppermute | solution.py:379
  5.2 11.2 %collective-permute-start.4 = (bf16[224,256]{1,0:T(8,128)(2,1)S(1)}, bf16[224,256]{1,0:T(8,128)(2,1)S(1)}, u32[]{:S(2)}, u32[]{:S(2)}) collective-permute-start(bf16[224,256]{1,0:T(8,128)(2,1)S(1)} %get-tuple-element.25.own_ref), channel_id=1, source_target_pairs={{0,8},{4,12},{8,0},{12,4},{1,9},{5,13},{9,1},{13,5},{2,10},{6,14},... | collective-permute-start | bytes 344072 | tf_op jit(solution)/shard_map/ppermute | solution.py:379
  7.8 8.7 %collective-permute-start.3 = (bf16[224,256]{1,0:T(8,128)(2,1)S(1)}, bf16[224,256]{1,0:T(8,128)(2,1)S(1)}, u32[]{:S(2)}, u32[]{:S(2)}) collective-permute-start(bf16[224,256]{1,0:T(8,128)(2,1)S(1)} %get-tuple-element.26), channel_id=1, source_target_pairs={{0,4},{4,0},{8,12},{12,8},{1,5},{5,1},{9,13},{13,9},{2,6},{6,2},{1... | collective-permute-start | bytes 344072 | tf_op jit(solution)/shard_map/ppermute | solution.py:379
  9.4 7.4 %collective-permute-start.5 = (bf16[224,256]{1,0:T(8,128)(2,1)S(1)}, bf16[224,256]{1,0:T(8,128)(2,1)S(1)}, u32[]{:S(2)}, u32[]{:S(2)}) collective-permute-start(bf16[224,256]{1,0:T(8,128)(2,1)S(1)} %get-tuple-element.26), channel_id=1, source_target_pairs={{0,12},{4,8},{8,4},{12,0},{1,13},{5,9},{9,5},{13,1},{2,14},{6,10},... | collective-permute-start | bytes 344072 | tf_op jit(solution)/shard_map/ppermute | solution.py:379
  9.6 1.3 %copy-start.15 = (bf16[128,8]{0,1:T(8,128)(2,1)S(1)}, bf16[128,8]{0,1:T(8,128)(2,1)}, u32[]{:S(2)}) copy-start(bf16[128,8]{0,1:T(8,128)(2,1)} %param.25) | copy-start | bytes 6148
  9.6 1.3 %collective-permute-start.1 = (bf16[64,256]{1,0:T(8,128)(2,1)S(1)}, bf16[64,256]{1,0:T(8,128)(2,1)S(1)}, u32[]{:S(2)}, u32[]{:S(2)}) collective-permute-start(bf16[64,256]{1,0:T(8,128)(2,1)S(1)} %get-tuple-element.24), channel_id=1, source_target_pairs={{0,1},{1,0},{2,3},{3,2},{4,5},{5,4},{6,7},{7,6},{8,9},{9,8},{10,11... | collective-permute-start | bytes 98312 | tf_op jit(solution)/shard_map/ppermute | solution.py:379
  9.7 10.0 %collective-permute-start.6 = (bf16[576,256]{1,0:T(8,128)(2,1)S(1)}, bf16[576,256]{1,0:T(8,128)(2,1)S(1)}, u32[]{:S(2)}, u32[]{:S(2)}) collective-permute-start(bf16[576,256]{1,0:T(8,128)(2,1)S(1)} %get-tuple-element.34), channel_id=1, source_target_pairs={{0,1},{1,0},{2,3},{3,2},{4,5},{5,4},{6,7},{7,6},{8,9},{9,8},{10,11... | collective-permute-start | bytes 884744 | tf_op jit(solution)/shard_map/ppermute | solution.py:379
  11.3 5.5 %collective-permute-start.2 = (bf16[32,128]{1,0:T(8,128)(2,1)S(1)}, bf16[32,128]{1,0:T(8,128)(2,1)S(1)}, u32[]{:S(2)}, u32[]{:S(2)}) collective-permute-start(bf16[32,128]{1,0:T(8,128)(2,1)S(1)} %shard_map.179.near_bias_ref), channel_id=1, source_target_pairs={{0,4},{4,0},{8,12},{12,8},{1,5},{5,1},{9,13},{13,9},{2,6},{6,2},{1... | collective-permute-start | bytes 24584 | tf_op jit(solution)/shard_map/ppermute | solution.py:379
  13.0 1.0 %copy-start = (bf16[32,32,128]{2,1,0:T(8,128)(2,1)S(1)}, bf16[32,32,128]{2,1,0:T(8,128)(2,1)}, u32[]{:S(2)}) copy-start(bf16[32,32,128]{2,1,0:T(8,128)(2,1)} %param.24) | copy-start | bytes 786436
  13.0 1.0 %copy-start.2 = (bf16[256,256]{1,0:T(8,128)(2,1)S(1)}, bf16[256,256]{1,0:T(8,128)(2,1)}, u32[]{:S(2)}) copy-start(bf16[256,256]{1,0:T(8,128)(2,1)} %refs_1_.1) | copy-start | bytes 393220
  13.0 1.0 %copy-start.13 = (f32[128]{0:T(128)S(1)}, f32[128]{0:T(128)}, u32[]{:S(2)}) copy-start(f32[128]{0:T(128)} %param.31) | copy-start | bytes 1540
  13.1 0.9 %copy-start.11 = (f32[256]{0:T(256)S(1)}, f32[256]{0:T(256)}, u32[]{:S(2)}) copy-start(f32[256]{0:T(256)} %param.19) | copy-start | bytes 3076
  13.1 0.9 %copy-start.12 = (f32[128]{0:T(128)S(1)}, f32[128]{0:T(128)}, u32[]{:S(2)}) copy-start(f32[128]{0:T(128)} %param.26) | copy-start | bytes 1540
  16.9 2.8 %collective-permute-start.7 = (bf16[192,256]{1,0:T(8,128)(2,1)S(1)}, bf16[192,256]{1,0:T(8,128)(2,1)S(1)}, u32[]{:S(2)}, u32[]{:S(2)}) collective-permute-start(bf16[192,256]{1,0:T(8,128)(2,1)S(1)} %shard_map.181.refs_0_.refs_4_), channel_id=1, source_target_pairs={{0,1},{1,0},{2,3},{3,2},{4,5},{5,4},{6,7},{7,6},{8,9},{9,8},{10,11... | collective-permute-start | bytes 294920 | tf_op jit(solution)/shard_map/ppermute | solution.py:379
  16.9 7.1 %collective-permute-start.11 = (bf16[192,256]{1,0:T(8,128)(2,1)S(1)}, bf16[192,256]{1,0:T(8,128)(2,1)S(1)}, u32[]{:S(2)}, u32[]{:S(2)}) collective-permute-start(bf16[192,256]{1,0:T(8,128)(2,1)S(1)} %shard_map.181.refs_0_.refs_4_), channel_id=1, source_target_pairs={{0,2},{1,3},{2,0},{3,1},{4,6},{5,7},{6,4},{7,5},{8,10},{9,11},{10,... | collective-permute-start | bytes 294920 | tf_op jit(solution)/shard_map/ppermute | solution.py:379
  17.5 6.5 %collective-permute-start.12 = (bf16[192,256]{1,0:T(8,128)(2,1)S(1)}, bf16[192,256]{1,0:T(8,128)(2,1)S(1)}, u32[]{:S(2)}, u32[]{:S(2)}) collective-permute-start(bf16[192,256]{1,0:T(8,128)(2,1)S(1)} %shard_map.181.refs_0_.refs_4_), channel_id=1, source_target_pairs={{0,3},{1,2},{2,1},{3,0},{4,7},{5,6},{6,5},{7,4},{8,11},{9,10},{10,... | collective-permute-start | bytes 294920 | tf_op jit(solution)/shard_map/ppermute | solution.py:379
  20.4 6.0 %collective-permute-start.10 = (bf16[128,128]{1,0:T(8,128)(2,1)S(1)}, bf16[128,128]{1,0:T(8,128)(2,1)S(1)}, u32[]{:S(2)}, u32[]{:S(2)}) collective-permute-start(bf16[128,128]{1,0:T(8,128)(2,1)S(1)} %get-tuple-element.38), channel_id=1, source_target_pairs={{0,20},{4,16},{8,28},{12,24},{16,4},{20,0},{24,12},{28,8},{1,21},{... | collective-permute-start | bytes 98312 | tf_op jit(solution)/shard_map/ppermute | solution.py:379
  23.4 3.9 %collective-permute-start.8 = (bf16[128,128]{1,0:T(8,128)(2,1)S(1)}, bf16[128,128]{1,0:T(8,128)(2,1)S(1)}, u32[]{:S(2)}, u32[]{:S(2)}) collective-permute-start(bf16[128,128]{1,0:T(8,128)(2,1)S(1)} %get-tuple-element.36), channel_id=1, source_target_pairs={{0,16},{4,20},{8,24},{12,28},{16,0},{20,4},{24,8},{28,12},{1,17},{... | collective-permute-start | bytes 98312 | tf_op jit(solution)/shard_map/ppermute | solution.py:379
  23.9 3.9 %collective-permute-start.9 = (bf16[128,128]{1,0:T(8,128)(2,1)S(1)}, bf16[128,128]{1,0:T(8,128)(2,1)S(1)}, u32[]{:S(2)}, u32[]{:S(2)}) collective-permute-start(bf16[128,128]{1,0:T(8,128)(2,1)S(1)} %get-tuple-element.37), channel_id=1, source_target_pairs={{0,4},{4,0},{8,12},{12,8},{16,20},{20,16},{24,28},{28,24},{1,5},{5... | collective-permute-start | bytes 98312 | tf_op jit(solution)/shard_map/ppermute | solution.py:379

commit v5 on v4

--- a/solution.py
+++ b/solution.py
@@ -433,6 +433,10 @@
     count = len(refs) // 2
     for source, target in zip(refs[:count], refs[count:]):
         target[...] = source[...]
+
+
+def arrive_kernel(*refs):
+    refs[-1][...] = jnp.zeros_like(refs[-1])
 
 
 def relay_kernel(sizes, own_ref, one_ref, two_ref, three_ref, after_bias_ref, after_keep_ref, relay_ref):
@@ -553,7 +557,7 @@
         there[...] = jnp.where(branch == 0, high, low)
 
 
-def place_kernel(own_ref, branch_ref, row_ref, both_ref, pair_ref, output_ref, pair_output_ref):
+def place_kernel(own_ref, branch_ref, row_ref, both_ref, pair_ref, token_ref, output_ref, pair_output_ref):
     pair_output_ref[...] = pair_ref[...]
     rows = own_ref.shape[0]
     branch = lax.axis_index("branch")
@@ -782,10 +786,11 @@
             pltpu.VMEM((local_rows * half, pair_width), full_type),
         ],
     )
+    (arrived,) = kernel_call(arrive_kernel, [shape(8, 128, dtype=full_type)], [from_row])
     alignment_flat, pairwise_output = kernel_call(
         place_kernel,
         [shape(sequences * local_rows, width // 2), shape(local_rows * half, chan_local)],
-        [near_here, from_branch, from_row, from_both, pair_done],
+        [near_here, from_branch, from_row, from_both, pair_done, arrived],
     )
     return (
         alignment_flat.reshape(sequences, local_rows, width // 2),

time: 28.6 us -> 28.4 us (level)
    pallas_call x10 -> x11, Pallas kernels: 5.73 us -> 5.73 us  [kernel_call(): pl.pallas_call(body, out_shape=outputs, in_specs=[hbm if i in in_hbm else...]
where the time goes in v5:
time: 28.4 us; the launch traced here: 28.3 us
  starting transfers between devices  15.1 us (53%)
  Pallas kernels  5.73 us (20%)
  waiting for transfers between devices  4.66 us (16%)
  local copies, waits for them, and re-layouts  1.85 us (7%)
  between operations  0.89 us (3%)
    ppermute x13, starting transfers between devices, exchange(): lax.ppermute(value, axes, [(i, i ^ distance) for i in range(members)])  15.1 us
    pallas_call x11, Pallas kernels, kernel_call(): pl.pallas_call(body, out_shape=outputs, in_specs=[hbm if i in in_hbm else...  5.73 us
    ppermute x13, waiting for transfers between devices, exchange(): lax.ppermute(value, axes, [(i, i ^ distance) for i in range(members)])  4.66 us
    unnamed x35, local copies, waits for them, and re-layouts  1.85 us
  transfers between devices with their start and end apart: 13, of which 5 were waited for; matrix products, arithmetic and copies ran while one was open for 0% of the time, Pallas kernels for 16%

profile of v5, /device:TPU:0, one launch (start us, length us, event | category | flops | bytes accessed | tf_op | source)
XLA Modules:
  0.0 28.3 jit_solution(4621973551865642181)
XLA Ops:
  0.7 0.0 copy-start.8
  0.7 0.0 copy-start.10
  0.7 0.8 %copy-done.1 = bf16[64,8,256]{2,1,0:T(8,128)(2,1)S(1)} copy-done((bf16[64,8,256]{2,1,0:T(8,128)(2,1)S(1)}, bf16[64,8,256]{2,1,0:T(8,128)(2,1)}, u32[]{:S(2)}) %copy-start.1) | copy-done | bytes 262168
  1.6 0.0 copy-done.6
  1.6 0.0 copy-done.7
  1.6 0.0 copy-done.9
  1.6 0.0 copy-done.14
  1.6 0.0 copy-done.8
  1.6 0.0 copy-start.16
  1.7 0.6 %shard_map.177 = (bf16[224,256]{1,0:T(8,128)(2,1)S(1)}, bf16[224,256]{1,0:T(8,128)(2,1)S(1)}, bf16[320,256]{1,0:T(8,128)(2,1)S(1)}) custom-call(bf16[512,256]{1,0:T(8,128)(2,1)S(1)} %bitcast.20, bf16[32,8,32]{2,1,0:T(8,128)(2,1)S(1)} %copy-done.3, f32[1,256]{1,0:T(1,128)S(1)} %bitcast.23, bf16[64,256]{1,0:T(8,128)(2,1)S(1)} %bitcast.21, ...), custom_call_target="tpu_custom_call" | custom-call | bytes 824448 | tf_op jit(solution)/shard_map/pallas_call | solution.py:366
  2.2 3.0 %collective-permute-start = (bf16[320,256]{1,0:T(8,128)(2,1)S(1)}, bf16[320,256]{1,0:T(8,128)(2,1)S(1)}, u32[]{:S(2)}, u32[]{:S(2)}) collective-permute-start(bf16[320,256]{1,0:T(8,128)(2,1)S(1)} %get-tuple-element.23.own_ref.refs_0_), channel_id=1, source_target_pairs={{0,2},{1,3},{2,0},{3,1},{4,6},{5,7},{6,4},{7,5},{8,10},{9,11},{10,... | collective-permute-start | bytes 491528 | tf_op jit(solution)/shard_map/ppermute | solution.py:379
  5.2 2.6 %collective-permute-start.4 = (bf16[224,256]{1,0:T(8,128)(2,1)S(1)}, bf16[224,256]{1,0:T(8,128)(2,1)S(1)}, u32[]{:S(2)}, u32[]{:S(2)}) collective-permute-start(bf16[224,256]{1,0:T(8,128)(2,1)S(1)} %get-tuple-element.25.own_ref), channel_id=1, source_target_pairs={{0,8},{4,12},{8,0},{12,4},{1,9},{5,13},{9,1},{13,5},{2,10},{6,14},... | collective-permute-start | bytes 344072 | tf_op jit(solution)/shard_map/ppermute | solution.py:379
  7.8 1.6 %collective-permute-start.3 = (bf16[224,256]{1,0:T(8,128)(2,1)S(1)}, bf16[224,256]{1,0:T(8,128)(2,1)S(1)}, u32[]{:S(2)}, u32[]{:S(2)}) collective-permute-start(bf16[224,256]{1,0:T(8,128)(2,1)S(1)} %get-tuple-element.26), channel_id=1, source_target_pairs={{0,4},{4,0},{8,12},{12,8},{1,5},{5,1},{9,13},{13,9},{2,6},{6,2},{1... | collective-permute-start | bytes 344072 | tf_op jit(solution)/shard_map/ppermute | solution.py:379
  9.4 0.2 collective-permute-start.5
  9.6 0.0 collective-permute-done.other_ref.refs_1_
  9.6 0.0 copy-start.15
  9.6 0.1 collective-permute-start.1
  9.7 0.5 %collective-permute-start.6 = (bf16[576,256]{1,0:T(8,128)(2,1)S(1)}, bf16[576,256]{1,0:T(8,128)(2,1)S(1)}, u32[]{:S(2)}, u32[]{:S(2)}) collective-permute-start(bf16[576,256]{1,0:T(8,128)(2,1)S(1)} %get-tuple-element.34), channel_id=1, source_target_pairs={{0,1},{1,0},{2,3},{3,2},{4,5},{5,4},{6,7},{7,6},{8,9},{9,8},{10,11... | collective-permute-start | bytes 884744 | tf_op jit(solution)/shard_map/ppermute | solution.py:379
  10.2 0.7 %collective-permute-done.1.refs_2_ = bf16[64,256]{1,0:T(8,128)(2,1)S(1)} collective-permute-done((bf16[64,256]{1,0:T(8,128)(2,1)S(1)}, bf16[64,256]{1,0:T(8,128)(2,1)S(1)}, u32[]{:S(2)}, u32[]{:S(2)}) %collective-permute-start.1) | collective-permute-done | bytes 32800 | tf_op jit(solution)/shard_map/ppermute | solution.py:379
  10.9 0.4 %shard_map.179.near_bias_ref = bf16[32,128]{1,0:T(8,128)(2,1)S(1)} custom-call(bf16[320,256]{1,0:T(8,128)(2,1)S(1)} %get-tuple-element.23.own_ref.refs_0_, bf16[320,256]{1,0:T(8,128)(2,1)S(1)} %collective-permute-done.other_ref.refs_1_, bf16[64,256]{1,0:T(8,128)(2,1)S(1)} %collective-permute-done.1.refs_2_, bf16[8,128]{1,0:T(8,128)(2,1)S(1)} %bitcast.28), custom_call_target="tpu_custom_call" | custom-call | flops 175000000 | bytes 370688 | tf_op jit(solution)/shard_map/pallas_call | solution.py:366
  11.3 1.7 %collective-permute-start.2 = (bf16[32,128]{1,0:T(8,128)(2,1)S(1)}, bf16[32,128]{1,0:T(8,128)(2,1)S(1)}, u32[]{:S(2)}, u32[]{:S(2)}) collective-permute-start(bf16[32,128]{1,0:T(8,128)(2,1)S(1)} %shard_map.179.near_bias_ref), channel_id=1, source_target_pairs={{0,4},{4,0},{8,12},{12,8},{1,5},{5,1},{9,13},{13,9},{2,6},{6,2},{1... | collective-permute-start | bytes 24584 | tf_op jit(solution)/shard_map/ppermute | solution.py:379
  13.0 0.1 copy.19
  13.1 0.0 copy-start.11
  13.1 0.0 copy-start.12
  13.1 0.8 %copy-done = bf16[32,32,128]{2,1,0:T(8,128)(2,1)S(1)} copy-done((bf16[32,32,128]{2,1,0:T(8,128)(2,1)S(1)}, bf16[32,32,128]{2,1,0:T(8,128)(2,1)}, u32[]{:S(2)}) %copy-start) | copy-done | bytes 262168
  14.0 0.0 copy-done.2
  14.0 0.1 shard_map.180
  14.1 2.4 %collective-permute-done.4.two_ref = bf16[224,256]{1,0:T(8,128)(2,1)S(1)} collective-permute-done((bf16[224,256]{1,0:T(8,128)(2,1)S(1)}, bf16[224,256]{1,0:T(8,128)(2,1)S(1)}, u32[]{:S(2)}, u32[]{:S(2)}) %collective-permute-start.4) | collective-permute-done | bytes 114720 | tf_op jit(solution)/shard_map/ppermute | solution.py:379
  16.5 0.0 collective-permute-done.3.one_ref
  16.5 0.4 %collective-permute-done.5.three_ref = bf16[224,256]{1,0:T(8,128)(2,1)S(1)} collective-permute-done((bf16[224,256]{1,0:T(8,128)(2,1)S(1)}, bf16[224,256]{1,0:T(8,128)(2,1)S(1)}, u32[]{:S(2)}, u32[]{:S(2)}) %collective-permute-start.5) | collective-permute-done | bytes 114720 | tf_op jit(solution)/shard_map/ppermute | solution.py:379
  16.8 0.0 collective-permute-done.2.after_bias_ref.far_bias_ref
  16.9 0.1 collective-permute-start.7
  16.9 0.6 %collective-permute-start.11 = (bf16[192,256]{1,0:T(8,128)(2,1)S(1)}, bf16[192,256]{1,0:T(8,128)(2,1)S(1)}, u32[]{:S(2)}, u32[]{:S(2)}) collective-permute-start(bf16[192,256]{1,0:T(8,128)(2,1)S(1)} %shard_map.181.refs_0_.refs_4_), channel_id=1, source_target_pairs={{0,2},{1,3},{2,0},{3,1},{4,6},{5,7},{6,4},{7,5},{8,10},{9,11},{10,... | collective-permute-start | bytes 294920 | tf_op jit(solution)/shard_map/ppermute | solution.py:379
  17.5 1.3 %collective-permute-start.12 = (bf16[192,256]{1,0:T(8,128)(2,1)S(1)}, bf16[192,256]{1,0:T(8,128)(2,1)S(1)}, u32[]{:S(2)}, u32[]{:S(2)}) collective-permute-start(bf16[192,256]{1,0:T(8,128)(2,1)S(1)} %shard_map.181.refs_0_.refs_4_), channel_id=1, source_target_pairs={{0,3},{1,2},{2,1},{3,0},{4,7},{5,6},{6,5},{7,4},{8,11},{9,10},{10,... | collective-permute-start | bytes 294920 | tf_op jit(solution)/shard_map/ppermute | solution.py:379
  18.8 0.9 %shard_map.182 = (f32[512,128]{1,0:T(8,128)S(1)}, bf16[512,256]{1,0:T(8,128)(2,1)S(1)}, bf16[256,256]{1,0:T(8,128)(2,1)S(1)}) custom-call(bf16[224,256]{1,0:T(8,128)(2,1)S(1)} %get-tuple-element.25.own_ref, bf16[224,256]{1,0:T(8,128)(2,1)S(1)} %collective-permute-done.3.one_ref, bf16[224,256]{1,0:T(8,128)(2,1)S(1)} %collective-permute-done.4.two_ref, ...), custom_call_target="tpu_custom_call" | custom-call | flops 3000000000 | bytes 1737728 | tf_op jit(solution)/shard_map/pallas_call | solution.py:366
  19.7 0.0 collective-permute-done.7.refs_1_.refs_6_
  19.7 0.0 collective-permute-done.6.refs_0_.refs_3_
  19.7 0.7 %shard_map.183 = (bf16[128,128]{1,0:T(8,128)(2,1)S(1)}, bf16[128,128]{1,0:T(8,128)(2,1)S(1)}, bf16[128,128]{1,0:T(8,128)(2,1)S(1)}, bf16[128,128]{1,0:T(8,128)(2,1)S(1)}) custom-call(bf16[32,128]{1,0:T(8,128)(2,1)S(1)} %shard_map.179.near_bias_ref, bf16[32,128]{1,0:T(8,128)(2,1)S(1)} %collective-permute-done.2.after_bias_ref.far_bias_ref, ...), custom_call_target="tpu_custom_call" | custom-call | flops 3000000000 | bytes 1556480 | tf_op jit(solution)/shard_map/pallas_call | solution.py:366
  20.4 2.0 %collective-permute-start.9 = (bf16[128,128]{1,0:T(8,128)(2,1)S(1)}, bf16[128,128]{1,0:T(8,128)(2,1)S(1)}, u32[]{:S(2)}, u32[]{:S(2)}) collective-permute-start(bf16[128,128]{1,0:T(8,128)(2,1)S(1)} %get-tuple-element.37), channel_id=1, source_target_pairs={{0,4},{4,0},{8,12},{12,8},{16,20},{20,16},{24,28},{28,24},{1,5},{5... | collective-permute-start | bytes 98312 | tf_op jit(solution)/shard_map/ppermute | solution.py:379
  22.4 1.0 %collective-permute-start.10 = (bf16[128,128]{1,0:T(8,128)(2,1)S(1)}, bf16[128,128]{1,0:T(8,128)(2,1)S(1)}, u32[]{:S(2)}, u32[]{:S(2)}) collective-permute-start(bf16[128,128]{1,0:T(8,128)(2,1)S(1)} %get-tuple-element.38), channel_id=1, source_target_pairs={{0,20},{4,16},{8,28},{12,24},{16,4},{20,0},{24,12},{28,8},{1,21},{... | collective-permute-start | bytes 98312 | tf_op jit(solution)/shard_map/ppermute | solution.py:379
  23.4 0.5 %collective-permute-start.8 = (bf16[128,128]{1,0:T(8,128)(2,1)S(1)}, bf16[128,128]{1,0:T(8,128)(2,1)S(1)}, u32[]{:S(2)}, u32[]{:S(2)}) collective-permute-start(bf16[128,128]{1,0:T(8,128)(2,1)S(1)} %get-tuple-element.36), channel_id=1, source_target_pairs={{0,16},{4,20},{8,24},{12,28},{16,0},{20,4},{24,8},{28,12},{1,17},{... | collective-permute-start | bytes 98312 | tf_op jit(solution)/shard_map/ppermute | solution.py:379
  24.0 0.0 collective-permute-done.11.refs_5_
  24.0 0.0 collective-permute-done.12.refs_7_
  24.0 2.4 %shard_map.184.pair_ref = bf16[128,32]{1,0:T(8,128)(2,1)S(1)} custom-call(bf16[320,256]{1,0:T(8,128)(2,1)S(1)} %get-tuple-element.23.own_ref.refs_0_, bf16[320,256]{1,0:T(8,128)(2,1)S(1)} %collective-permute-done.other_ref.refs_1_, bf16[64,256]{1,0:T(8,128)(2,1)S(1)} %collective-permute-done.1.refs_2_, ...), custom_call_target="tpu_custom_call" | custom-call | bytes 1319936 | tf_op jit(solution)/shard_map/pallas_call | solution.py:366
  26.4 0.0 collective-permute-done.9.refs_0_.row_ref
  26.4 0.9 %collective-permute-done.10.both_ref = bf16[128,128]{1,0:T(8,128)(2,1)S(1)} collective-permute-done((bf16[128,128]{1,0:T(8,128)(2,1)S(1)}, bf16[128,128]{1,0:T(8,128)(2,1)S(1)}, u32[]{:S(2)}, u32[]{:S(2)}) %collective-permute-start.10) | collective-permute-done | bytes 32800 | tf_op jit(solution)/shard_map/ppermute | solution.py:379
  27.3 0.3 %collective-permute-done.8.branch_ref = bf16[128,128]{1,0:T(8,128)(2,1)S(1)} collective-permute-done((bf16[128,128]{1,0:T(8,128)(2,1)S(1)}, bf16[128,128]{1,0:T(8,128)(2,1)S(1)}, u32[]{:S(2)}, u32[]{:S(2)}) %collective-permute-start.8) | collective-permute-done | bytes 32800 | tf_op jit(solution)/shard_map/ppermute | solution.py:379
  27.6 0.7 %shard_map.186 = (bf16[512,128]{1,0:T(8,128)(2,1)}, bf16[128,32]{1,0:T(8,128)(2,1)}) custom-call(bf16[128,128]{1,0:T(8,128)(2,1)S(1)} %get-tuple-element.35.own_ref, bf16[128,128]{1,0:T(8,128)(2,1)S(1)} %collective-permute-done.8.branch_ref, bf16[128,128]{1,0:T(8,128)(2,1)S(1)} %collective-permute-done.9.refs_0_.row_ref, ...), custom_call_target="tpu_custom_call" | custom-call | bytes 282624 | tf_op jit(solution)/shard_map/pallas_call | solution.py:366
  (24 shorter events, 0.1 us)
Async XLA Ops:
  0.6 1.0 %copy-start.1 = (bf16[64,8,256]{2,1,0:T(8,128)(2,1)S(1)}, bf16[64,8,256]{2,1,0:T(8,128)(2,1)}, u32[]{:S(2)}) copy-start(bf16[64,8,256]{2,1,0:T(8,128)(2,1)} %param.17) | copy-start | bytes 786436
  0.6 0.9 %copy-start.4 = (bf16[256,2,32]{0,2,1:T(8,128)(2,1)S(1)}, bf16[256,2,32]{0,2,1:T(8,128)(2,1)}, u32[]{:S(2)}) copy-start(bf16[256,2,32]{0,2,1:T(8,128)(2,1)} %param.23) | copy-start | bytes 98308
  0.7 0.9 %copy-start.3 = (bf16[32,8,32]{2,1,0:T(8,128)(2,1)S(1)}, bf16[32,8,32]{2,1,0:T(8,128)(2,1)}, u32[]{:S(2)}) copy-start(bf16[32,8,32]{2,1,0:T(8,128)(2,1)} %pair_ref.1) | copy-start | bytes 49156
  0.7 0.9 %copy-start.5 = (bf16[4,32,128]{2,1,0:T(8,128)(2,1)S(1)}, bf16[4,32,128]{2,1,0:T(8,128)(2,1)}, u32[]{:S(2)}) copy-start(bf16[4,32,128]{2,1,0:T(8,128)(2,1)} %input_ref.1) | copy-start | bytes 98308
  0.7 0.9 %copy-start.6 = (bf16[128,128]{1,0:T(8,128)(2,1)S(1)}, bf16[128,128]{1,0:T(8,128)(2,1)}, u32[]{:S(2)}) copy-start(bf16[128,128]{1,0:T(8,128)(2,1)} %up_ref.1) | copy-start | bytes 98308
  0.7 0.9 %copy-start.7 = (bf16[128,128]{1,0:T(8,128)(2,1)S(1)}, bf16[128,128]{1,0:T(8,128)(2,1)}, u32[]{:S(2)}) copy-start(bf16[128,128]{1,0:T(8,128)(2,1)} %down_ref.1) | copy-start | bytes 98308
  0.7 0.9 %copy-start.9 = (bf16[128,32]{0,1:T(8,128)(2,1)S(1)}, bf16[128,32]{0,1:T(8,128)(2,1)}, u32[]{:S(2)}) copy-start(bf16[128,32]{0,1:T(8,128)(2,1)} %param.30) | copy-start | bytes 24580
  0.7 0.9 %copy-start.14 = (f32[32]{0:T(128)S(1)}, f32[32]{0:T(128)}, u32[]{:S(2)}) copy-start(f32[32]{0:T(128)} %param.29) | copy-start | bytes 388
  0.7 0.9 %copy-start.8 = (bf16[32,128]{1,0:T(8,128)(2,1)S(1)}, bf16[32,128]{1,0:T(8,128)(2,1)}, u32[]{:S(2)}) copy-start(bf16[32,128]{1,0:T(8,128)(2,1)} %gate_ref.1) | copy-start | bytes 24580
  0.7 0.9 %copy-start.10 = (f32[256]{0:T(256)S(1)}, f32[256]{0:T(256)}, u32[]{:S(2)}) copy-start(f32[256]{0:T(256)} %param.20) | copy-start | bytes 3076
  1.6 11.4 %copy-start.16 = (bf16[256,4,256]{2,1,0:T(4,128)(2,1)S(1)}, bf16[256,4,256]{2,1,0:T(4,128)(2,1)}, u32[]{:S(2)}) copy-start(bf16[256,4,256]{2,1,0:T(4,128)(2,1)} %param.21) | copy-start | bytes 1572868
  2.2 7.4 %collective-permute-start = (bf16[320,256]{1,0:T(8,128)(2,1)S(1)}, bf16[320,256]{1,0:T(8,128)(2,1)S(1)}, u32[]{:S(2)}, u32[]{:S(2)}) collective-permute-start(bf16[320,256]{1,0:T(8,128)(2,1)S(1)} %get-tuple-element.23.own_ref.refs_0_), channel_id=1, source_target_pairs={{0,2},{1,3},{2,0},{3,1},{4,6},{5,7},{6,4},{7,5},{8,10},{9,11},{10,... | collective-permute-start | bytes 491528 | tf_op jit(solution)/shard_map/ppermute | solution.py:379
  5.2 11.2 %collective-permute-start.4 = (bf16[224,256]{1,0:T(8,128)(2,1)S(1)}, bf16[224,256]{1,0:T(8,128)(2,1)S(1)}, u32[]{:S(2)}, u32[]{:S(2)}) collective-permute-start(bf16[224,256]{1,0:T(8,128)(2,1)S(1)} %get-tuple-element.25.own_ref), channel_id=1, source_target_pairs={{0,8},{4,12},{8,0},{12,4},{1,9},{5,13},{9,1},{13,5},{2,10},{6,14},... | collective-permute-start | bytes 344072 | tf_op jit(solution)/shard_map/ppermute | solution.py:379
  7.8 8.7 %collective-permute-start.3 = (bf16[224,256]{1,0:T(8,128)(2,1)S(1)}, bf16[224,256]{1,0:T(8,128)(2,1)S(1)}, u32[]{:S(2)}, u32[]{:S(2)}) collective-permute-start(bf16[224,256]{1,0:T(8,128)(2,1)S(1)} %get-tuple-element.26), channel_id=1, source_target_pairs={{0,4},{4,0},{8,12},{12,8},{1,5},{5,1},{9,13},{13,9},{2,6},{6,2},{1... | collective-permute-start | bytes 344072 | tf_op jit(solution)/shard_map/ppermute | solution.py:379
  9.4 7.4 %collective-permute-start.5 = (bf16[224,256]{1,0:T(8,128)(2,1)S(1)}, bf16[224,256]{1,0:T(8,128)(2,1)S(1)}, u32[]{:S(2)}, u32[]{:S(2)}) collective-permute-start(bf16[224,256]{1,0:T(8,128)(2,1)S(1)} %get-tuple-element.26), channel_id=1, source_target_pairs={{0,12},{4,8},{8,4},{12,0},{1,13},{5,9},{9,5},{13,1},{2,14},{6,10},... | collective-permute-start | bytes 344072 | tf_op jit(solution)/shard_map/ppermute | solution.py:379
  9.6 1.3 %copy-start.15 = (bf16[128,8]{0,1:T(8,128)(2,1)S(1)}, bf16[128,8]{0,1:T(8,128)(2,1)}, u32[]{:S(2)}) copy-start(bf16[128,8]{0,1:T(8,128)(2,1)} %param.25) | copy-start | bytes 6148
  9.6 1.3 %collective-permute-start.1 = (bf16[64,256]{1,0:T(8,128)(2,1)S(1)}, bf16[64,256]{1,0:T(8,128)(2,1)S(1)}, u32[]{:S(2)}, u32[]{:S(2)}) collective-permute-start(bf16[64,256]{1,0:T(8,128)(2,1)S(1)} %get-tuple-element.24), channel_id=1, source_target_pairs={{0,1},{1,0},{2,3},{3,2},{4,5},{5,4},{6,7},{7,6},{8,9},{9,8},{10,11... | collective-permute-start | bytes 98312 | tf_op jit(solution)/shard_map/ppermute | solution.py:379
  9.7 10.0 %collective-permute-start.6 = (bf16[576,256]{1,0:T(8,128)(2,1)S(1)}, bf16[576,256]{1,0:T(8,128)(2,1)S(1)}, u32[]{:S(2)}, u32[]{:S(2)}) collective-permute-start(bf16[576,256]{1,0:T(8,128)(2,1)S(1)} %get-tuple-element.34), channel_id=1, source_target_pairs={{0,1},{1,0},{2,3},{3,2},{4,5},{5,4},{6,7},{7,6},{8,9},{9,8},{10,11... | collective-permute-start | bytes 884744 | tf_op jit(solution)/shard_map/ppermute | solution.py:379
  11.3 5.5 %collective-permute-start.2 = (bf16[32,128]{1,0:T(8,128)(2,1)S(1)}, bf16[32,128]{1,0:T(8,128)(2,1)S(1)}, u32[]{:S(2)}, u32[]{:S(2)}) collective-permute-start(bf16[32,128]{1,0:T(8,128)(2,1)S(1)} %shard_map.179.near_bias_ref), channel_id=1, source_target_pairs={{0,4},{4,0},{8,12},{12,8},{1,5},{5,1},{9,13},{13,9},{2,6},{6,2},{1... | collective-permute-start | bytes 24584 | tf_op jit(solution)/shard_map/ppermute | solution.py:379
  13.0 1.0 %copy-start = (bf16[32,32,128]{2,1,0:T(8,128)(2,1)S(1)}, bf16[32,32,128]{2,1,0:T(8,128)(2,1)}, u32[]{:S(2)}) copy-start(bf16[32,32,128]{2,1,0:T(8,128)(2,1)} %param.24) | copy-start | bytes 786436
  13.0 1.0 %copy-start.2 = (bf16[256,256]{1,0:T(8,128)(2,1)S(1)}, bf16[256,256]{1,0:T(8,128)(2,1)}, u32[]{:S(2)}) copy-start(bf16[256,256]{1,0:T(8,128)(2,1)} %refs_1_.1) | copy-start | bytes 393220
  13.0 1.0 %copy-start.13 = (f32[128]{0:T(128)S(1)}, f32[128]{0:T(128)}, u32[]{:S(2)}) copy-start(f32[128]{0:T(128)} %param.31) | copy-start | bytes 1540
  13.1 0.9 %copy-start.11 = (f32[256]{0:T(256)S(1)}, f32[256]{0:T(256)}, u32[]{:S(2)}) copy-start(f32[256]{0:T(256)} %param.19) | copy-start | bytes 3076
  13.1 0.9 %copy-start.12 = (f32[128]{0:T(128)S(1)}, f32[128]{0:T(128)}, u32[]{:S(2)}) copy-start(f32[128]{0:T(128)} %param.26) | copy-start | bytes 1540
  16.9 2.8 %collective-permute-start.7 = (bf16[192,256]{1,0:T(8,128)(2,1)S(1)}, bf16[192,256]{1,0:T(8,128)(2,1)S(1)}, u32[]{:S(2)}, u32[]{:S(2)}) collective-permute-start(bf16[192,256]{1,0:T(8,128)(2,1)S(1)} %shard_map.181.refs_0_.refs_4_), channel_id=1, source_target_pairs={{0,1},{1,0},{2,3},{3,2},{4,5},{5,4},{6,7},{7,6},{8,9},{9,8},{10,11... | collective-permute-start | bytes 294920 | tf_op jit(solution)/shard_map/ppermute | solution.py:379
  16.9 7.0 %collective-permute-start.11 = (bf16[192,256]{1,0:T(8,128)(2,1)S(1)}, bf16[192,256]{1,0:T(8,128)(2,1)S(1)}, u32[]{:S(2)}, u32[]{:S(2)}) collective-permute-start(bf16[192,256]{1,0:T(8,128)(2,1)S(1)} %shard_map.181.refs_0_.refs_4_), channel_id=1, source_target_pairs={{0,2},{1,3},{2,0},{3,1},{4,6},{5,7},{6,4},{7,5},{8,10},{9,11},{10,... | collective-permute-start | bytes 294920 | tf_op jit(solution)/shard_map/ppermute | solution.py:379
  17.5 6.4 %collective-permute-start.12 = (bf16[192,256]{1,0:T(8,128)(2,1)S(1)}, bf16[192,256]{1,0:T(8,128)(2,1)S(1)}, u32[]{:S(2)}, u32[]{:S(2)}) collective-permute-start(bf16[192,256]{1,0:T(8,128)(2,1)S(1)} %shard_map.181.refs_0_.refs_4_), channel_id=1, source_target_pairs={{0,3},{1,2},{2,1},{3,0},{4,7},{5,6},{6,5},{7,4},{8,11},{9,10},{10,... | collective-permute-start | bytes 294920 | tf_op jit(solution)/shard_map/ppermute | solution.py:379
  20.4 6.0 %collective-permute-start.9 = (bf16[128,128]{1,0:T(8,128)(2,1)S(1)}, bf16[128,128]{1,0:T(8,128)(2,1)S(1)}, u32[]{:S(2)}, u32[]{:S(2)}) collective-permute-start(bf16[128,128]{1,0:T(8,128)(2,1)S(1)} %get-tuple-element.37), channel_id=1, source_target_pairs={{0,4},{4,0},{8,12},{12,8},{16,20},{20,16},{24,28},{28,24},{1,5},{5... | collective-permute-start | bytes 98312 | tf_op jit(solution)/shard_map/ppermute | solution.py:379
  22.4 4.8 %collective-permute-start.10 = (bf16[128,128]{1,0:T(8,128)(2,1)S(1)}, bf16[128,128]{1,0:T(8,128)(2,1)S(1)}, u32[]{:S(2)}, u32[]{:S(2)}) collective-permute-start(bf16[128,128]{1,0:T(8,128)(2,1)S(1)} %get-tuple-element.38), channel_id=1, source_target_pairs={{0,20},{4,16},{8,28},{12,24},{16,4},{20,0},{24,12},{28,8},{1,21},{... | collective-permute-start | bytes 98312 | tf_op jit(solution)/shard_map/ppermute | solution.py:379
  23.4 4.1 %collective-permute-start.8 = (bf16[128,128]{1,0:T(8,128)(2,1)S(1)}, bf16[128,128]{1,0:T(8,128)(2,1)S(1)}, u32[]{:S(2)}, u32[]{:S(2)}) collective-permute-start(bf16[128,128]{1,0:T(8,128)(2,1)S(1)} %get-tuple-element.36), channel_id=1, source_target_pairs={{0,16},{4,20},{8,24},{12,28},{16,0},{20,4},{24,8},{28,12},{1,17},{... | collective-permute-start | bytes 98312 | tf_op jit(solution)/shard_map/ppermute | solution.py:379

commit v6 on v5

--- a/solution.py
+++ b/solution.py
@@ -468,7 +468,6 @@
     part = sequences // 4
     part_rows = part * local_rows
     width = gain_ref.shape[1]
-    head_size = 32
     row = lax.axis_index("row")
     for distance, ref in enumerate((own_ref, one_ref, two_ref, three_ref)):
         shard = row ^ distance
@@ -482,11 +481,12 @@
     here = module[:, pl.ds(pl.multiple_of(row // 2 * half, half), half), :]
     query_rows = rounded(here.reshape(part * half, width))
     heads = values_ref.shape[1]
+    groups = score_ref.shape[1] // half
+    head_size = heads // groups
     query = rounded(product(query_rows, weight_ref[:, 0:heads]) * head_size ** (-0.5))
     keys = rounded(product(normed, weight_ref[:, heads : 2 * heads]))
     values_ref[...] = rounded(product(normed, weight_ref[:, 2 * heads : 3 * heads]))
     gate_ref[...] = rounded(jax.nn.sigmoid(product(query_rows, weight_ref[:, 3 * heads :])))
-    groups = heads // head_size
     mask = head_mask(groups, half, head_size)
     for s in range(part):
         one = query[s * half : (s + 1) * half]
@@ -526,8 +526,8 @@
     part_rows = part * local_rows
     half = residues // 2
     heads = values_ref.shape[1]
-    head_size = 32
-    groups = heads // head_size
+    groups = score_ref.shape[1] // half
+    head_size = heads // groups
     row = lax.axis_index("row")
     branch = lax.axis_index("branch")
     bias = widened(near_bias_ref[...]) + widened(far_bias_ref[...])
@@ -798,13 +798,13 @@
     )
 
 
-def is_compact(mesh, residues):
-    return mesh.shape["row"] == 4 and mesh.shape["seq"] == 4 and mesh.shape["branch"] == 2
+def is_compact(mesh):
+    return (mesh.shape["branch"], mesh.shape["row"], mesh.shape["seq"]) == (2, 4, 4)
 
 
 def solution(mesh):
     return jax.shard_map(
-        compact_shards if is_compact(mesh, None) else shards,
+        compact_shards if is_compact(mesh) else shards,
         mesh=mesh,
         in_specs=(
             P("seq", "row", None),

time: 28.4 us -> 28.4 us (level)
  no operation moved by 1% of the time
where the time goes in v6:
time: 28.4 us; the launch traced here: 28.3 us
  starting transfers between devices  15.1 us (53%)
  Pallas kernels  5.73 us (20%)
  waiting for transfers between devices  4.66 us (16%)
  local copies, waits for them, and re-layouts  1.85 us (7%)
  between operations  0.89 us (3%)
    ppermute x13, starting transfers between devices, exchange(): lax.ppermute(value, axes, [(i, i ^ distance) for i in range(members)])  15.1 us
    pallas_call x11, Pallas kernels, kernel_call(): pl.pallas_call(body, out_shape=outputs, in_specs=[hbm if i in in_hbm else...  5.73 us
    ppermute x13, waiting for transfers between devices, exchange(): lax.ppermute(value, axes, [(i, i ^ distance) for i in range(members)])  4.66 us
    unnamed x35, local copies, waits for them, and re-layouts  1.85 us
  transfers between devices with their start and end apart: 13, of which 5 were waited for; matrix products, arithmetic and copies ran while one was open for 0% of the time, Pallas kernels for 16%

profile of v6, /device:TPU:0, one launch (start us, length us, event | category | flops | bytes accessed | tf_op | source)
XLA Modules:
  0.0 28.3 jit_solution(4621973551865642181)
XLA Ops:
  0.7 0.0 copy-start.8
  0.7 0.0 copy-start.10
  0.7 0.8 %copy-done.1 = bf16[64,8,256]{2,1,0:T(8,128)(2,1)S(1)} copy-done((bf16[64,8,256]{2,1,0:T(8,128)(2,1)S(1)}, bf16[64,8,256]{2,1,0:T(8,128)(2,1)}, u32[]{:S(2)}) %copy-start.1) | copy-done | bytes 262168
  1.6 0.0 copy-done.6
  1.6 0.0 copy-done.7
  1.6 0.0 copy-done.9
  1.6 0.0 copy-done.14
  1.6 0.0 copy-done.8
  1.6 0.0 copy-start.16
  1.7 0.6 %shard_map.177 = (bf16[224,256]{1,0:T(8,128)(2,1)S(1)}, bf16[224,256]{1,0:T(8,128)(2,1)S(1)}, bf16[320,256]{1,0:T(8,128)(2,1)S(1)}) custom-call(bf16[512,256]{1,0:T(8,128)(2,1)S(1)} %bitcast.20, bf16[32,8,32]{2,1,0:T(8,128)(2,1)S(1)} %copy-done.3, f32[1,256]{1,0:T(1,128)S(1)} %bitcast.23, bf16[64,256]{1,0:T(8,128)(2,1)S(1)} %bitcast.21, ...), custom_call_target="tpu_custom_call" | custom-call | bytes 824448 | tf_op jit(solution)/shard_map/pallas_call | solution.py:366
  2.2 3.0 %collective-permute-start = (bf16[320,256]{1,0:T(8,128)(2,1)S(1)}, bf16[320,256]{1,0:T(8,128)(2,1)S(1)}, u32[]{:S(2)}, u32[]{:S(2)}) collective-permute-start(bf16[320,256]{1,0:T(8,128)(2,1)S(1)} %get-tuple-element.23.own_ref.refs_0_), channel_id=1, source_target_pairs={{0,2},{1,3},{2,0},{3,1},{4,6},{5,7},{6,4},{7,5},{8,10},{9,11},{10,... | collective-permute-start | bytes 491528 | tf_op jit(solution)/shard_map/ppermute | solution.py:379
  5.2 2.6 %collective-permute-start.4 = (bf16[224,256]{1,0:T(8,128)(2,1)S(1)}, bf16[224,256]{1,0:T(8,128)(2,1)S(1)}, u32[]{:S(2)}, u32[]{:S(2)}) collective-permute-start(bf16[224,256]{1,0:T(8,128)(2,1)S(1)} %get-tuple-element.25.own_ref), channel_id=1, source_target_pairs={{0,8},{4,12},{8,0},{12,4},{1,9},{5,13},{9,1},{13,5},{2,10},{6,14},... | collective-permute-start | bytes 344072 | tf_op jit(solution)/shard_map/ppermute | solution.py:379
  7.8 1.6 %collective-permute-start.3 = (bf16[224,256]{1,0:T(8,128)(2,1)S(1)}, bf16[224,256]{1,0:T(8,128)(2,1)S(1)}, u32[]{:S(2)}, u32[]{:S(2)}) collective-permute-start(bf16[224,256]{1,0:T(8,128)(2,1)S(1)} %get-tuple-element.26), channel_id=1, source_target_pairs={{0,4},{4,0},{8,12},{12,8},{1,5},{5,1},{9,13},{13,9},{2,6},{6,2},{1... | collective-permute-start | bytes 344072 | tf_op jit(solution)/shard_map/ppermute | solution.py:379
  9.4 0.2 collective-permute-start.5
  9.6 0.0 collective-permute-done.other_ref.refs_1_
  9.6 0.0 copy-start.15
  9.6 0.1 collective-permute-start.1
  9.7 0.5 %collective-permute-start.6 = (bf16[576,256]{1,0:T(8,128)(2,1)S(1)}, bf16[576,256]{1,0:T(8,128)(2,1)S(1)}, u32[]{:S(2)}, u32[]{:S(2)}) collective-permute-start(bf16[576,256]{1,0:T(8,128)(2,1)S(1)} %get-tuple-element.34), channel_id=1, source_target_pairs={{0,1},{1,0},{2,3},{3,2},{4,5},{5,4},{6,7},{7,6},{8,9},{9,8},{10,11... | collective-permute-start | bytes 884744 | tf_op jit(solution)/shard_map/ppermute | solution.py:379
  10.2 0.7 %collective-permute-done.1.refs_2_ = bf16[64,256]{1,0:T(8,128)(2,1)S(1)} collective-permute-done((bf16[64,256]{1,0:T(8,128)(2,1)S(1)}, bf16[64,256]{1,0:T(8,128)(2,1)S(1)}, u32[]{:S(2)}, u32[]{:S(2)}) %collective-permute-start.1) | collective-permute-done | bytes 32800 | tf_op jit(solution)/shard_map/ppermute | solution.py:379
  10.9 0.4 %shard_map.179.near_bias_ref = bf16[32,128]{1,0:T(8,128)(2,1)S(1)} custom-call(bf16[320,256]{1,0:T(8,128)(2,1)S(1)} %get-tuple-element.23.own_ref.refs_0_, bf16[320,256]{1,0:T(8,128)(2,1)S(1)} %collective-permute-done.other_ref.refs_1_, bf16[64,256]{1,0:T(8,128)(2,1)S(1)} %collective-permute-done.1.refs_2_, bf16[8,128]{1,0:T(8,128)(2,1)S(1)} %bitcast.28), custom_call_target="tpu_custom_call" | custom-call | flops 175000000 | bytes 370688 | tf_op jit(solution)/shard_map/pallas_call | solution.py:366
  11.3 1.7 %collective-permute-start.2 = (bf16[32,128]{1,0:T(8,128)(2,1)S(1)}, bf16[32,128]{1,0:T(8,128)(2,1)S(1)}, u32[]{:S(2)}, u32[]{:S(2)}) collective-permute-start(bf16[32,128]{1,0:T(8,128)(2,1)S(1)} %shard_map.179.near_bias_ref), channel_id=1, source_target_pairs={{0,4},{4,0},{8,12},{12,8},{1,5},{5,1},{9,13},{13,9},{2,6},{6,2},{1... | collective-permute-start | bytes 24584 | tf_op jit(solution)/shard_map/ppermute | solution.py:379
  13.0 0.1 copy.19
  13.1 0.0 copy-start.11
  13.1 0.0 copy-start.12
  13.1 0.8 %copy-done = bf16[32,32,128]{2,1,0:T(8,128)(2,1)S(1)} copy-done((bf16[32,32,128]{2,1,0:T(8,128)(2,1)S(1)}, bf16[32,32,128]{2,1,0:T(8,128)(2,1)}, u32[]{:S(2)}) %copy-start) | copy-done | bytes 262168
  14.0 0.0 copy-done.2
  14.0 0.1 shard_map.180
  14.1 2.4 %collective-permute-done.4.two_ref = bf16[224,256]{1,0:T(8,128)(2,1)S(1)} collective-permute-done((bf16[224,256]{1,0:T(8,128)(2,1)S(1)}, bf16[224,256]{1,0:T(8,128)(2,1)S(1)}, u32[]{:S(2)}, u32[]{:S(2)}) %collective-permute-start.4) | collective-permute-done | bytes 114720 | tf_op jit(solution)/shard_map/ppermute | solution.py:379
  16.5 0.0 collective-permute-done.3.one_ref
  16.5 0.4 %collective-permute-done.5.three_ref = bf16[224,256]{1,0:T(8,128)(2,1)S(1)} collective-permute-done((bf16[224,256]{1,0:T(8,128)(2,1)S(1)}, bf16[224,256]{1,0:T(8,128)(2,1)S(1)}, u32[]{:S(2)}, u32[]{:S(2)}) %collective-permute-start.5) | collective-permute-done | bytes 114720 | tf_op jit(solution)/shard_map/ppermute | solution.py:379
  16.8 0.0 collective-permute-done.2.after_bias_ref.far_bias_ref
  16.9 0.1 collective-permute-start.7
  16.9 0.6 %collective-permute-start.11 = (bf16[192,256]{1,0:T(8,128)(2,1)S(1)}, bf16[192,256]{1,0:T(8,128)(2,1)S(1)}, u32[]{:S(2)}, u32[]{:S(2)}) collective-permute-start(bf16[192,256]{1,0:T(8,128)(2,1)S(1)} %shard_map.181.refs_0_.refs_4_), channel_id=1, source_target_pairs={{0,2},{1,3},{2,0},{3,1},{4,6},{5,7},{6,4},{7,5},{8,10},{9,11},{10,... | collective-permute-start | bytes 294920 | tf_op jit(solution)/shard_map/ppermute | solution.py:379
  17.5 1.3 %collective-permute-start.12 = (bf16[192,256]{1,0:T(8,128)(2,1)S(1)}, bf16[192,256]{1,0:T(8,128)(2,1)S(1)}, u32[]{:S(2)}, u32[]{:S(2)}) collective-permute-start(bf16[192,256]{1,0:T(8,128)(2,1)S(1)} %shard_map.181.refs_0_.refs_4_), channel_id=1, source_target_pairs={{0,3},{1,2},{2,1},{3,0},{4,7},{5,6},{6,5},{7,4},{8,11},{9,10},{10,... | collective-permute-start | bytes 294920 | tf_op jit(solution)/shard_map/ppermute | solution.py:379
  18.8 0.9 %shard_map.182 = (f32[512,128]{1,0:T(8,128)S(1)}, bf16[512,256]{1,0:T(8,128)(2,1)S(1)}, bf16[256,256]{1,0:T(8,128)(2,1)S(1)}) custom-call(bf16[224,256]{1,0:T(8,128)(2,1)S(1)} %get-tuple-element.25.own_ref, bf16[224,256]{1,0:T(8,128)(2,1)S(1)} %collective-permute-done.3.one_ref, bf16[224,256]{1,0:T(8,128)(2,1)S(1)} %collective-permute-done.4.two_ref, ...), custom_call_target="tpu_custom_call" | custom-call | flops 3000000000 | bytes 1737728 | tf_op jit(solution)/shard_map/pallas_call | solution.py:366
  19.7 0.0 collective-permute-done.7.refs_1_.refs_6_
  19.7 0.0 collective-permute-done.6.refs_0_.refs_3_
  19.7 0.7 %shard_map.183 = (bf16[128,128]{1,0:T(8,128)(2,1)S(1)}, bf16[128,128]{1,0:T(8,128)(2,1)S(1)}, bf16[128,128]{1,0:T(8,128)(2,1)S(1)}, bf16[128,128]{1,0:T(8,128)(2,1)S(1)}) custom-call(bf16[32,128]{1,0:T(8,128)(2,1)S(1)} %shard_map.179.near_bias_ref, bf16[32,128]{1,0:T(8,128)(2,1)S(1)} %collective-permute-done.2.after_bias_ref.far_bias_ref, ...), custom_call_target="tpu_custom_call" | custom-call | flops 3000000000 | bytes 1556480 | tf_op jit(solution)/shard_map/pallas_call | solution.py:366
  20.4 2.0 %collective-permute-start.9 = (bf16[128,128]{1,0:T(8,128)(2,1)S(1)}, bf16[128,128]{1,0:T(8,128)(2,1)S(1)}, u32[]{:S(2)}, u32[]{:S(2)}) collective-permute-start(bf16[128,128]{1,0:T(8,128)(2,1)S(1)} %get-tuple-element.37), channel_id=1, source_target_pairs={{0,4},{4,0},{8,12},{12,8},{16,20},{20,16},{24,28},{28,24},{1,5},{5... | collective-permute-start | bytes 98312 | tf_op jit(solution)/shard_map/ppermute | solution.py:379
  22.4 1.0 %collective-permute-start.10 = (bf16[128,128]{1,0:T(8,128)(2,1)S(1)}, bf16[128,128]{1,0:T(8,128)(2,1)S(1)}, u32[]{:S(2)}, u32[]{:S(2)}) collective-permute-start(bf16[128,128]{1,0:T(8,128)(2,1)S(1)} %get-tuple-element.38), channel_id=1, source_target_pairs={{0,20},{4,16},{8,28},{12,24},{16,4},{20,0},{24,12},{28,8},{1,21},{... | collective-permute-start | bytes 98312 | tf_op jit(solution)/shard_map/ppermute | solution.py:379
  23.4 0.5 %collective-permute-start.8 = (bf16[128,128]{1,0:T(8,128)(2,1)S(1)}, bf16[128,128]{1,0:T(8,128)(2,1)S(1)}, u32[]{:S(2)}, u32[]{:S(2)}) collective-permute-start(bf16[128,128]{1,0:T(8,128)(2,1)S(1)} %get-tuple-element.36), channel_id=1, source_target_pairs={{0,16},{4,20},{8,24},{12,28},{16,0},{20,4},{24,8},{28,12},{1,17},{... | collective-permute-start | bytes 98312 | tf_op jit(solution)/shard_map/ppermute | solution.py:379
  24.0 0.0 collective-permute-done.11.refs_5_
  24.0 0.0 collective-permute-done.12.refs_7_
  24.0 2.4 %shard_map.184.pair_ref = bf16[128,32]{1,0:T(8,128)(2,1)S(1)} custom-call(bf16[320,256]{1,0:T(8,128)(2,1)S(1)} %get-tuple-element.23.own_ref.refs_0_, bf16[320,256]{1,0:T(8,128)(2,1)S(1)} %collective-permute-done.other_ref.refs_1_, bf16[64,256]{1,0:T(8,128)(2,1)S(1)} %collective-permute-done.1.refs_2_, ...), custom_call_target="tpu_custom_call" | custom-call | bytes 1319936 | tf_op jit(solution)/shard_map/pallas_call | solution.py:366
  26.4 0.0 collective-permute-done.9.refs_0_.row_ref
  26.4 0.9 %collective-permute-done.10.both_ref = bf16[128,128]{1,0:T(8,128)(2,1)S(1)} collective-permute-done((bf16[128,128]{1,0:T(8,128)(2,1)S(1)}, bf16[128,128]{1,0:T(8,128)(2,1)S(1)}, u32[]{:S(2)}, u32[]{:S(2)}) %collective-permute-start.10) | collective-permute-done | bytes 32800 | tf_op jit(solution)/shard_map/ppermute | solution.py:379
  27.3 0.3 %collective-permute-done.8.branch_ref = bf16[128,128]{1,0:T(8,128)(2,1)S(1)} collective-permute-done((bf16[128,128]{1,0:T(8,128)(2,1)S(1)}, bf16[128,128]{1,0:T(8,128)(2,1)S(1)}, u32[]{:S(2)}, u32[]{:S(2)}) %collective-permute-start.8) | collective-permute-done | bytes 32800 | tf_op jit(solution)/shard_map/ppermute | solution.py:379
  27.6 0.7 %shard_map.186 = (bf16[512,128]{1,0:T(8,128)(2,1)}, bf16[128,32]{1,0:T(8,128)(2,1)}) custom-call(bf16[128,128]{1,0:T(8,128)(2,1)S(1)} %get-tuple-element.35.own_ref, bf16[128,128]{1,0:T(8,128)(2,1)S(1)} %collective-permute-done.8.branch_ref, bf16[128,128]{1,0:T(8,128)(2,1)S(1)} %collective-permute-done.9.refs_0_.row_ref, ...), custom_call_target="tpu_custom_call" | custom-call | bytes 282624 | tf_op jit(solution)/shard_map/pallas_call | solution.py:366
  (24 shorter events, 0.1 us)
Async XLA Ops:
  0.6 1.0 %copy-start.1 = (bf16[64,8,256]{2,1,0:T(8,128)(2,1)S(1)}, bf16[64,8,256]{2,1,0:T(8,128)(2,1)}, u32[]{:S(2)}) copy-start(bf16[64,8,256]{2,1,0:T(8,128)(2,1)} %param.17) | copy-start | bytes 786436
  0.6 0.9 %copy-start.4 = (bf16[256,2,32]{0,2,1:T(8,128)(2,1)S(1)}, bf16[256,2,32]{0,2,1:T(8,128)(2,1)}, u32[]{:S(2)}) copy-start(bf16[256,2,32]{0,2,1:T(8,128)(2,1)} %param.23) | copy-start | bytes 98308
  0.7 0.9 %copy-start.3 = (bf16[32,8,32]{2,1,0:T(8,128)(2,1)S(1)}, bf16[32,8,32]{2,1,0:T(8,128)(2,1)}, u32[]{:S(2)}) copy-start(bf16[32,8,32]{2,1,0:T(8,128)(2,1)} %pair_ref.1) | copy-start | bytes 49156
  0.7 0.9 %copy-start.5 = (bf16[4,32,128]{2,1,0:T(8,128)(2,1)S(1)}, bf16[4,32,128]{2,1,0:T(8,128)(2,1)}, u32[]{:S(2)}) copy-start(bf16[4,32,128]{2,1,0:T(8,128)(2,1)} %input_ref.1) | copy-start | bytes 98308
  0.7 0.9 %copy-start.6 = (bf16[128,128]{1,0:T(8,128)(2,1)S(1)}, bf16[128,128]{1,0:T(8,128)(2,1)}, u32[]{:S(2)}) copy-start(bf16[128,128]{1,0:T(8,128)(2,1)} %up_ref.1) | copy-start | bytes 98308
  0.7 0.9 %copy-start.7 = (bf16[128,128]{1,0:T(8,128)(2,1)S(1)}, bf16[128,128]{1,0:T(8,128)(2,1)}, u32[]{:S(2)}) copy-start(bf16[128,128]{1,0:T(8,128)(2,1)} %down_ref.1) | copy-start | bytes 98308
  0.7 0.9 %copy-start.9 = (bf16[128,32]{0,1:T(8,128)(2,1)S(1)}, bf16[128,32]{0,1:T(8,128)(2,1)}, u32[]{:S(2)}) copy-start(bf16[128,32]{0,1:T(8,128)(2,1)} %param.30) | copy-start | bytes 24580
  0.7 0.9 %copy-start.14 = (f32[32]{0:T(128)S(1)}, f32[32]{0:T(128)}, u32[]{:S(2)}) copy-start(f32[32]{0:T(128)} %param.29) | copy-start | bytes 388
  0.7 0.9 %copy-start.8 = (bf16[32,128]{1,0:T(8,128)(2,1)S(1)}, bf16[32,128]{1,0:T(8,128)(2,1)}, u32[]{:S(2)}) copy-start(bf16[32,128]{1,0:T(8,128)(2,1)} %gate_ref.1) | copy-start | bytes 24580
  0.7 0.9 %copy-start.10 = (f32[256]{0:T(256)S(1)}, f32[256]{0:T(256)}, u32[]{:S(2)}) copy-start(f32[256]{0:T(256)} %param.20) | copy-start | bytes 3076
  1.6 11.4 %copy-start.16 = (bf16[256,4,256]{2,1,0:T(4,128)(2,1)S(1)}, bf16[256,4,256]{2,1,0:T(4,128)(2,1)}, u32[]{:S(2)}) copy-start(bf16[256,4,256]{2,1,0:T(4,128)(2,1)} %param.21) | copy-start | bytes 1572868
  2.2 7.4 %collective-permute-start = (bf16[320,256]{1,0:T(8,128)(2,1)S(1)}, bf16[320,256]{1,0:T(8,128)(2,1)S(1)}, u32[]{:S(2)}, u32[]{:S(2)}) collective-permute-start(bf16[320,256]{1,0:T(8,128)(2,1)S(1)} %get-tuple-element.23.own_ref.refs_0_), channel_id=1, source_target_pairs={{0,2},{1,3},{2,0},{3,1},{4,6},{5,7},{6,4},{7,5},{8,10},{9,11},{10,... | collective-permute-start | bytes 491528 | tf_op jit(solution)/shard_map/ppermute | solution.py:379
  5.2 11.2 %collective-permute-start.4 = (bf16[224,256]{1,0:T(8,128)(2,1)S(1)}, bf16[224,256]{1,0:T(8,128)(2,1)S(1)}, u32[]{:S(2)}, u32[]{:S(2)}) collective-permute-start(bf16[224,256]{1,0:T(8,128)(2,1)S(1)} %get-tuple-element.25.own_ref), channel_id=1, source_target_pairs={{0,8},{4,12},{8,0},{12,4},{1,9},{5,13},{9,1},{13,5},{2,10},{6,14},... | collective-permute-start | bytes 344072 | tf_op jit(solution)/shard_map/ppermute | solution.py:379
  7.8 8.7 %collective-permute-start.3 = (bf16[224,256]{1,0:T(8,128)(2,1)S(1)}, bf16[224,256]{1,0:T(8,128)(2,1)S(1)}, u32[]{:S(2)}, u32[]{:S(2)}) collective-permute-start(bf16[224,256]{1,0:T(8,128)(2,1)S(1)} %get-tuple-element.26), channel_id=1, source_target_pairs={{0,4},{4,0},{8,12},{12,8},{1,5},{5,1},{9,13},{13,9},{2,6},{6,2},{1... | collective-permute-start | bytes 344072 | tf_op jit(solution)/shard_map/ppermute | solution.py:379
  9.4 7.4 %collective-permute-start.5 = (bf16[224,256]{1,0:T(8,128)(2,1)S(1)}, bf16[224,256]{1,0:T(8,128)(2,1)S(1)}, u32[]{:S(2)}, u32[]{:S(2)}) collective-permute-start(bf16[224,256]{1,0:T(8,128)(2,1)S(1)} %get-tuple-element.26), channel_id=1, source_target_pairs={{0,12},{4,8},{8,4},{12,0},{1,13},{5,9},{9,5},{13,1},{2,14},{6,10},... | collective-permute-start | bytes 344072 | tf_op jit(solution)/shard_map/ppermute | solution.py:379
  9.6 1.3 %copy-start.15 = (bf16[128,8]{0,1:T(8,128)(2,1)S(1)}, bf16[128,8]{0,1:T(8,128)(2,1)}, u32[]{:S(2)}) copy-start(bf16[128,8]{0,1:T(8,128)(2,1)} %param.25) | copy-start | bytes 6148
  9.6 1.3 %collective-permute-start.1 = (bf16[64,256]{1,0:T(8,128)(2,1)S(1)}, bf16[64,256]{1,0:T(8,128)(2,1)S(1)}, u32[]{:S(2)}, u32[]{:S(2)}) collective-permute-start(bf16[64,256]{1,0:T(8,128)(2,1)S(1)} %get-tuple-element.24), channel_id=1, source_target_pairs={{0,1},{1,0},{2,3},{3,2},{4,5},{5,4},{6,7},{7,6},{8,9},{9,8},{10,11... | collective-permute-start | bytes 98312 | tf_op jit(solution)/shard_map/ppermute | solution.py:379
  9.7 10.0 %collective-permute-start.6 = (bf16[576,256]{1,0:T(8,128)(2,1)S(1)}, bf16[576,256]{1,0:T(8,128)(2,1)S(1)}, u32[]{:S(2)}, u32[]{:S(2)}) collective-permute-start(bf16[576,256]{1,0:T(8,128)(2,1)S(1)} %get-tuple-element.34), channel_id=1, source_target_pairs={{0,1},{1,0},{2,3},{3,2},{4,5},{5,4},{6,7},{7,6},{8,9},{9,8},{10,11... | collective-permute-start | bytes 884744 | tf_op jit(solution)/shard_map/ppermute | solution.py:379
  11.3 5.5 %collective-permute-start.2 = (bf16[32,128]{1,0:T(8,128)(2,1)S(1)}, bf16[32,128]{1,0:T(8,128)(2,1)S(1)}, u32[]{:S(2)}, u32[]{:S(2)}) collective-permute-start(bf16[32,128]{1,0:T(8,128)(2,1)S(1)} %shard_map.179.near_bias_ref), channel_id=1, source_target_pairs={{0,4},{4,0},{8,12},{12,8},{1,5},{5,1},{9,13},{13,9},{2,6},{6,2},{1... | collective-permute-start | bytes 24584 | tf_op jit(solution)/shard_map/ppermute | solution.py:379
  13.0 1.0 %copy-start = (bf16[32,32,128]{2,1,0:T(8,128)(2,1)S(1)}, bf16[32,32,128]{2,1,0:T(8,128)(2,1)}, u32[]{:S(2)}) copy-start(bf16[32,32,128]{2,1,0:T(8,128)(2,1)} %param.24) | copy-start | bytes 786436
  13.0 1.0 %copy-start.2 = (bf16[256,256]{1,0:T(8,128)(2,1)S(1)}, bf16[256,256]{1,0:T(8,128)(2,1)}, u32[]{:S(2)}) copy-start(bf16[256,256]{1,0:T(8,128)(2,1)} %refs_1_.1) | copy-start | bytes 393220
  13.0 1.0 %copy-start.13 = (f32[128]{0:T(128)S(1)}, f32[128]{0:T(128)}, u32[]{:S(2)}) copy-start(f32[128]{0:T(128)} %param.31) | copy-start | bytes 1540
  13.1 0.9 %copy-start.11 = (f32[256]{0:T(256)S(1)}, f32[256]{0:T(256)}, u32[]{:S(2)}) copy-start(f32[256]{0:T(256)} %param.19) | copy-start | bytes 3076
  13.1 0.9 %copy-start.12 = (f32[128]{0:T(128)S(1)}, f32[128]{0:T(128)}, u32[]{:S(2)}) copy-start(f32[128]{0:T(128)} %param.26) | copy-start | bytes 1540
  16.9 2.8 %collective-permute-start.7 = (bf16[192,256]{1,0:T(8,128)(2,1)S(1)}, bf16[192,256]{1,0:T(8,128)(2,1)S(1)}, u32[]{:S(2)}, u32[]{:S(2)}) collective-permute-start(bf16[192,256]{1,0:T(8,128)(2,1)S(1)} %shard_map.181.refs_0_.refs_4_), channel_id=1, source_target_pairs={{0,1},{1,0},{2,3},{3,2},{4,5},{5,4},{6,7},{7,6},{8,9},{9,8},{10,11... | collective-permute-start | bytes 294920 | tf_op jit(solution)/shard_map/ppermute | solution.py:379
  16.9 7.0 %collective-permute-start.11 = (bf16[192,256]{1,0:T(8,128)(2,1)S(1)}, bf16[192,256]{1,0:T(8,128)(2,1)S(1)}, u32[]{:S(2)}, u32[]{:S(2)}) collective-permute-start(bf16[192,256]{1,0:T(8,128)(2,1)S(1)} %shard_map.181.refs_0_.refs_4_), channel_id=1, source_target_pairs={{0,2},{1,3},{2,0},{3,1},{4,6},{5,7},{6,4},{7,5},{8,10},{9,11},{10,... | collective-permute-start | bytes 294920 | tf_op jit(solution)/shard_map/ppermute | solution.py:379
  17.5 6.4 %collective-permute-start.12 = (bf16[192,256]{1,0:T(8,128)(2,1)S(1)}, bf16[192,256]{1,0:T(8,128)(2,1)S(1)}, u32[]{:S(2)}, u32[]{:S(2)}) collective-permute-start(bf16[192,256]{1,0:T(8,128)(2,1)S(1)} %shard_map.181.refs_0_.refs_4_), channel_id=1, source_target_pairs={{0,3},{1,2},{2,1},{3,0},{4,7},{5,6},{6,5},{7,4},{8,11},{9,10},{10,... | collective-permute-start | bytes 294920 | tf_op jit(solution)/shard_map/ppermute | solution.py:379
  20.4 6.0 %collective-permute-start.9 = (bf16[128,128]{1,0:T(8,128)(2,1)S(1)}, bf16[128,128]{1,0:T(8,128)(2,1)S(1)}, u32[]{:S(2)}, u32[]{:S(2)}) collective-permute-start(bf16[128,128]{1,0:T(8,128)(2,1)S(1)} %get-tuple-element.37), channel_id=1, source_target_pairs={{0,4},{4,0},{8,12},{12,8},{16,20},{20,16},{24,28},{28,24},{1,5},{5... | collective-permute-start | bytes 98312 | tf_op jit(solution)/shard_map/ppermute | solution.py:379
  22.4 4.8 %collective-permute-start.10 = (bf16[128,128]{1,0:T(8,128)(2,1)S(1)}, bf16[128,128]{1,0:T(8,128)(2,1)S(1)}, u32[]{:S(2)}, u32[]{:S(2)}) collective-permute-start(bf16[128,128]{1,0:T(8,128)(2,1)S(1)} %get-tuple-element.38), channel_id=1, source_target_pairs={{0,20},{4,16},{8,28},{12,24},{16,4},{20,0},{24,12},{28,8},{1,21},{... | collective-permute-start | bytes 98312 | tf_op jit(solution)/shard_map/ppermute | solution.py:379
  23.4 4.1 %collective-permute-start.8 = (bf16[128,128]{1,0:T(8,128)(2,1)S(1)}, bf16[128,128]{1,0:T(8,128)(2,1)S(1)}, u32[]{:S(2)}, u32[]{:S(2)}) collective-permute-start(bf16[128,128]{1,0:T(8,128)(2,1)S(1)} %get-tuple-element.36), channel_id=1, source_target_pairs={{0,16},{4,20},{8,24},{12,28},{16,0},{20,4},{24,8},{28,12},{1,17},{... | collective-permute-start | bytes 98312 | tf_op jit(solution)/shard_map/ppermute | solution.py:379

commit v7 on v6

--- a/solution.py
+++ b/solution.py
@@ -484,8 +484,9 @@
     groups = score_ref.shape[1] // half
     head_size = heads // groups
     query = rounded(product(query_rows, weight_ref[:, 0:heads]) * head_size ** (-0.5))
-    keys = rounded(product(normed, weight_ref[:, heads : 2 * heads]))
-    values_ref[...] = rounded(product(normed, weight_ref[:, 2 * heads : 3 * heads]))
+    both = rounded(product(normed, weight_ref[:, heads : 3 * heads]))
+    keys = both[:, :heads]
+    values_ref[...] = both[:, heads:]
     gate_ref[...] = rounded(jax.nn.sigmoid(product(query_rows, weight_ref[:, 3 * heads :])))
     mask = head_mask(groups, half, head_size)
     for s in range(part):
@@ -533,7 +534,7 @@
     bias = widened(near_bias_ref[...]) + widened(far_bias_ref[...])
     scores = score_ref[...].reshape(part, residues, groups * half) + bias[None]
     weights = jnp.exp(scores - jnp.max(scores, axis=1, keepdims=True))
-    weights = rounded(weights / jnp.sum(weights, axis=1, keepdims=True))
+    weights = rounded(weights * (1.0 / jnp.sum(weights, axis=1, keepdims=True)))
     mask = head_mask(groups, half, head_size)
     attended = []
     for s in range(part):

time: 28.4 us -> 28.4 us (level)
  no operation moved by 1% of the time
where the time goes in v7:
time: 28.4 us; the launch traced here: 28.3 us
  starting transfers between devices  15.1 us (53%)
  Pallas kernels  5.73 us (20%)
  waiting for transfers between devices  4.66 us (16%)
  local copies, waits for them, and re-layouts  1.85 us (7%)
  between operations  0.89 us (3%)
    ppermute x13, starting transfers between devices, exchange(): lax.ppermute(value, axes, [(i, i ^ distance) for i in range(members)])  15.1 us
    pallas_call x11, Pallas kernels, kernel_call(): pl.pallas_call(body, out_shape=outputs, in_specs=[hbm if i in in_hbm else...  5.73 us
    ppermute x13, waiting for transfers between devices, exchange(): lax.ppermute(value, axes, [(i, i ^ distance) for i in range(members)])  4.66 us
    unnamed x35, local copies, waits for them, and re-layouts  1.85 us
  transfers between devices with their start and end apart: 13, of which 5 were waited for; matrix products, arithmetic and copies ran while one was open for 0% of the time, Pallas kernels for 16%

profile of v7, /device:TPU:0, one launch (start us, length us, event | category | flops | bytes accessed | tf_op | source)
XLA Modules:
  0.0 28.3 jit_solution(4621973551865642181)
XLA Ops:
  0.7 0.0 copy-start.8
  0.7 0.0 copy-start.10
  0.7 0.8 %copy-done.1 = bf16[64,8,256]{2,1,0:T(8,128)(2,1)S(1)} copy-done((bf16[64,8,256]{2,1,0:T(8,128)(2,1)S(1)}, bf16[64,8,256]{2,1,0:T(8,128)(2,1)}, u32[]{:S(2)}) %copy-start.1) | copy-done | bytes 262168
  1.6 0.0 copy-done.6
  1.6 0.0 copy-done.7
  1.6 0.0 copy-done.9
  1.6 0.0 copy-done.14
  1.6 0.0 copy-done.8
  1.6 0.0 copy-start.16
  1.7 0.6 %shard_map.177 = (bf16[224,256]{1,0:T(8,128)(2,1)S(1)}, bf16[224,256]{1,0:T(8,128)(2,1)S(1)}, bf16[320,256]{1,0:T(8,128)(2,1)S(1)}) custom-call(bf16[512,256]{1,0:T(8,128)(2,1)S(1)} %bitcast.20, bf16[32,8,32]{2,1,0:T(8,128)(2,1)S(1)} %copy-done.3, f32[1,256]{1,0:T(1,128)S(1)} %bitcast.23, bf16[64,256]{1,0:T(8,128)(2,1)S(1)} %bitcast.21, ...), custom_call_target="tpu_custom_call" | custom-call | bytes 824448 | tf_op jit(solution)/shard_map/pallas_call | solution.py:366
  2.2 3.0 %collective-permute-start = (bf16[320,256]{1,0:T(8,128)(2,1)S(1)}, bf16[320,256]{1,0:T(8,128)(2,1)S(1)}, u32[]{:S(2)}, u32[]{:S(2)}) collective-permute-start(bf16[320,256]{1,0:T(8,128)(2,1)S(1)} %get-tuple-element.23.own_ref.refs_0_), channel_id=1, source_target_pairs={{0,2},{1,3},{2,0},{3,1},{4,6},{5,7},{6,4},{7,5},{8,10},{9,11},{10,... | collective-permute-start | bytes 491528 | tf_op jit(solution)/shard_map/ppermute | solution.py:379
  5.2 2.6 %collective-permute-start.4 = (bf16[224,256]{1,0:T(8,128)(2,1)S(1)}, bf16[224,256]{1,0:T(8,128)(2,1)S(1)}, u32[]{:S(2)}, u32[]{:S(2)}) collective-permute-start(bf16[224,256]{1,0:T(8,128)(2,1)S(1)} %get-tuple-element.25.own_ref), channel_id=1, source_target_pairs={{0,8},{4,12},{8,0},{12,4},{1,9},{5,13},{9,1},{13,5},{2,10},{6,14},... | collective-permute-start | bytes 344072 | tf_op jit(solution)/shard_map/ppermute | solution.py:379
  7.8 1.6 %collective-permute-start.3 = (bf16[224,256]{1,0:T(8,128)(2,1)S(1)}, bf16[224,256]{1,0:T(8,128)(2,1)S(1)}, u32[]{:S(2)}, u32[]{:S(2)}) collective-permute-start(bf16[224,256]{1,0:T(8,128)(2,1)S(1)} %get-tuple-element.26), channel_id=1, source_target_pairs={{0,4},{4,0},{8,12},{12,8},{1,5},{5,1},{9,13},{13,9},{2,6},{6,2},{1... | collective-permute-start | bytes 344072 | tf_op jit(solution)/shard_map/ppermute | solution.py:379
  9.4 0.2 collective-permute-start.5
  9.6 0.0 collective-permute-done.other_ref.refs_1_
  9.6 0.0 copy-start.15
  9.6 0.1 collective-permute-start.1
  9.7 0.5 %collective-permute-start.6 = (bf16[576,256]{1,0:T(8,128)(2,1)S(1)}, bf16[576,256]{1,0:T(8,128)(2,1)S(1)}, u32[]{:S(2)}, u32[]{:S(2)}) collective-permute-start(bf16[576,256]{1,0:T(8,128)(2,1)S(1)} %get-tuple-element.34), channel_id=1, source_target_pairs={{0,1},{1,0},{2,3},{3,2},{4,5},{5,4},{6,7},{7,6},{8,9},{9,8},{10,11... | collective-permute-start | bytes 884744 | tf_op jit(solution)/shard_map/ppermute | solution.py:379
  10.2 0.7 %collective-permute-done.1.refs_2_ = bf16[64,256]{1,0:T(8,128)(2,1)S(1)} collective-permute-done((bf16[64,256]{1,0:T(8,128)(2,1)S(1)}, bf16[64,256]{1,0:T(8,128)(2,1)S(1)}, u32[]{:S(2)}, u32[]{:S(2)}) %collective-permute-start.1) | collective-permute-done | bytes 32800 | tf_op jit(solution)/shard_map/ppermute | solution.py:379
  10.9 0.4 %shard_map.179.near_bias_ref = bf16[32,128]{1,0:T(8,128)(2,1)S(1)} custom-call(bf16[320,256]{1,0:T(8,128)(2,1)S(1)} %get-tuple-element.23.own_ref.refs_0_, bf16[320,256]{1,0:T(8,128)(2,1)S(1)} %collective-permute-done.other_ref.refs_1_, bf16[64,256]{1,0:T(8,128)(2,1)S(1)} %collective-permute-done.1.refs_2_, bf16[8,128]{1,0:T(8,128)(2,1)S(1)} %bitcast.28), custom_call_target="tpu_custom_call" | custom-call | flops 175000000 | bytes 370688 | tf_op jit(solution)/shard_map/pallas_call | solution.py:366
  11.3 1.7 %collective-permute-start.2 = (bf16[32,128]{1,0:T(8,128)(2,1)S(1)}, bf16[32,128]{1,0:T(8,128)(2,1)S(1)}, u32[]{:S(2)}, u32[]{:S(2)}) collective-permute-start(bf16[32,128]{1,0:T(8,128)(2,1)S(1)} %shard_map.179.near_bias_ref), channel_id=1, source_target_pairs={{0,4},{4,0},{8,12},{12,8},{1,5},{5,1},{9,13},{13,9},{2,6},{6,2},{1... | collective-permute-start | bytes 24584 | tf_op jit(solution)/shard_map/ppermute | solution.py:379
  13.0 0.1 copy.19
  13.1 0.0 copy-start.11
  13.1 0.0 copy-start.12
  13.1 0.8 %copy-done = bf16[32,32,128]{2,1,0:T(8,128)(2,1)S(1)} copy-done((bf16[32,32,128]{2,1,0:T(8,128)(2,1)S(1)}, bf16[32,32,128]{2,1,0:T(8,128)(2,1)}, u32[]{:S(2)}) %copy-start) | copy-done | bytes 262168
  14.0 0.0 copy-done.2
  14.0 0.1 shard_map.180
  14.1 2.4 %collective-permute-done.4.two_ref = bf16[224,256]{1,0:T(8,128)(2,1)S(1)} collective-permute-done((bf16[224,256]{1,0:T(8,128)(2,1)S(1)}, bf16[224,256]{1,0:T(8,128)(2,1)S(1)}, u32[]{:S(2)}, u32[]{:S(2)}) %collective-permute-start.4) | collective-permute-done | bytes 114720 | tf_op jit(solution)/shard_map/ppermute | solution.py:379
  16.5 0.0 collective-permute-done.3.one_ref
  16.5 0.4 %collective-permute-done.5.three_ref = bf16[224,256]{1,0:T(8,128)(2,1)S(1)} collective-permute-done((bf16[224,256]{1,0:T(8,128)(2,1)S(1)}, bf16[224,256]{1,0:T(8,128)(2,1)S(1)}, u32[]{:S(2)}, u32[]{:S(2)}) %collective-permute-start.5) | collective-permute-done | bytes 114720 | tf_op jit(solution)/shard_map/ppermute | solution.py:379
  16.8 0.0 collective-permute-done.2.after_bias_ref.far_bias_ref
  16.9 0.1 collective-permute-start.7
  16.9 0.6 %collective-permute-start.11 = (bf16[192,256]{1,0:T(8,128)(2,1)S(1)}, bf16[192,256]{1,0:T(8,128)(2,1)S(1)}, u32[]{:S(2)}, u32[]{:S(2)}) collective-permute-start(bf16[192,256]{1,0:T(8,128)(2,1)S(1)} %shard_map.181.refs_0_.refs_4_), channel_id=1, source_target_pairs={{0,2},{1,3},{2,0},{3,1},{4,6},{5,7},{6,4},{7,5},{8,10},{9,11},{10,... | collective-permute-start | bytes 294920 | tf_op jit(solution)/shard_map/ppermute | solution.py:379
  17.5 1.3 %collective-permute-start.12 = (bf16[192,256]{1,0:T(8,128)(2,1)S(1)}, bf16[192,256]{1,0:T(8,128)(2,1)S(1)}, u32[]{:S(2)}, u32[]{:S(2)}) collective-permute-start(bf16[192,256]{1,0:T(8,128)(2,1)S(1)} %shard_map.181.refs_0_.refs_4_), channel_id=1, source_target_pairs={{0,3},{1,2},{2,1},{3,0},{4,7},{5,6},{6,5},{7,4},{8,11},{9,10},{10,... | collective-permute-start | bytes 294920 | tf_op jit(solution)/shard_map/ppermute | solution.py:379
  18.8 0.9 %shard_map.182 = (f32[512,128]{1,0:T(8,128)S(1)}, bf16[512,256]{1,0:T(8,128)(2,1)S(1)}, bf16[256,256]{1,0:T(8,128)(2,1)S(1)}) custom-call(bf16[224,256]{1,0:T(8,128)(2,1)S(1)} %get-tuple-element.25.own_ref, bf16[224,256]{1,0:T(8,128)(2,1)S(1)} %collective-permute-done.3.one_ref, bf16[224,256]{1,0:T(8,128)(2,1)S(1)} %collective-permute-done.4.two_ref, ...), custom_call_target="tpu_custom_call" | custom-call | flops 3000000000 | bytes 1737728 | tf_op jit(solution)/shard_map/pallas_call | solution.py:366
  19.7 0.0 collective-permute-done.7.refs_1_.refs_6_
  19.7 0.0 collective-permute-done.6.refs_0_.refs_3_
  19.7 0.7 %shard_map.183 = (bf16[128,128]{1,0:T(8,128)(2,1)S(1)}, bf16[128,128]{1,0:T(8,128)(2,1)S(1)}, bf16[128,128]{1,0:T(8,128)(2,1)S(1)}, bf16[128,128]{1,0:T(8,128)(2,1)S(1)}) custom-call(bf16[32,128]{1,0:T(8,128)(2,1)S(1)} %shard_map.179.near_bias_ref, bf16[32,128]{1,0:T(8,128)(2,1)S(1)} %collective-permute-done.2.after_bias_ref.far_bias_ref, ...), custom_call_target="tpu_custom_call" | custom-call | flops 3000000000 | bytes 1556480 | tf_op jit(solution)/shard_map/pallas_call | solution.py:366
  20.4 2.0 %collective-permute-start.9 = (bf16[128,128]{1,0:T(8,128)(2,1)S(1)}, bf16[128,128]{1,0:T(8,128)(2,1)S(1)}, u32[]{:S(2)}, u32[]{:S(2)}) collective-permute-start(bf16[128,128]{1,0:T(8,128)(2,1)S(1)} %get-tuple-element.37), channel_id=1, source_target_pairs={{0,4},{4,0},{8,12},{12,8},{16,20},{20,16},{24,28},{28,24},{1,5},{5... | collective-permute-start | bytes 98312 | tf_op jit(solution)/shard_map/ppermute | solution.py:379
  22.4 1.0 %collective-permute-start.10 = (bf16[128,128]{1,0:T(8,128)(2,1)S(1)}, bf16[128,128]{1,0:T(8,128)(2,1)S(1)}, u32[]{:S(2)}, u32[]{:S(2)}) collective-permute-start(bf16[128,128]{1,0:T(8,128)(2,1)S(1)} %get-tuple-element.38), channel_id=1, source_target_pairs={{0,20},{4,16},{8,28},{12,24},{16,4},{20,0},{24,12},{28,8},{1,21},{... | collective-permute-start | bytes 98312 | tf_op jit(solution)/shard_map/ppermute | solution.py:379
  23.4 0.5 %collective-permute-start.8 = (bf16[128,128]{1,0:T(8,128)(2,1)S(1)}, bf16[128,128]{1,0:T(8,128)(2,1)S(1)}, u32[]{:S(2)}, u32[]{:S(2)}) collective-permute-start(bf16[128,128]{1,0:T(8,128)(2,1)S(1)} %get-tuple-element.36), channel_id=1, source_target_pairs={{0,16},{4,20},{8,24},{12,28},{16,0},{20,4},{24,8},{28,12},{1,17},{... | collective-permute-start | bytes 98312 | tf_op jit(solution)/shard_map/ppermute | solution.py:379
  24.0 0.0 collective-permute-done.11.refs_5_
  24.0 0.0 collective-permute-done.12.refs_7_
  24.0 2.4 %shard_map.184.pair_ref = bf16[128,32]{1,0:T(8,128)(2,1)S(1)} custom-call(bf16[320,256]{1,0:T(8,128)(2,1)S(1)} %get-tuple-element.23.own_ref.refs_0_, bf16[320,256]{1,0:T(8,128)(2,1)S(1)} %collective-permute-done.other_ref.refs_1_, bf16[64,256]{1,0:T(8,128)(2,1)S(1)} %collective-permute-done.1.refs_2_, ...), custom_call_target="tpu_custom_call" | custom-call | bytes 1319936 | tf_op jit(solution)/shard_map/pallas_call | solution.py:366
  26.4 0.0 collective-permute-done.9.refs_0_.row_ref
  26.4 0.9 %collective-permute-done.10.both_ref = bf16[128,128]{1,0:T(8,128)(2,1)S(1)} collective-permute-done((bf16[128,128]{1,0:T(8,128)(2,1)S(1)}, bf16[128,128]{1,0:T(8,128)(2,1)S(1)}, u32[]{:S(2)}, u32[]{:S(2)}) %collective-permute-start.10) | collective-permute-done | bytes 32800 | tf_op jit(solution)/shard_map/ppermute | solution.py:379
  27.3 0.3 %collective-permute-done.8.branch_ref = bf16[128,128]{1,0:T(8,128)(2,1)S(1)} collective-permute-done((bf16[128,128]{1,0:T(8,128)(2,1)S(1)}, bf16[128,128]{1,0:T(8,128)(2,1)S(1)}, u32[]{:S(2)}, u32[]{:S(2)}) %collective-permute-start.8) | collective-permute-done | bytes 32800 | tf_op jit(solution)/shard_map/ppermute | solution.py:379
  27.6 0.7 %shard_map.186 = (bf16[512,128]{1,0:T(8,128)(2,1)}, bf16[128,32]{1,0:T(8,128)(2,1)}) custom-call(bf16[128,128]{1,0:T(8,128)(2,1)S(1)} %get-tuple-element.35.own_ref, bf16[128,128]{1,0:T(8,128)(2,1)S(1)} %collective-permute-done.8.branch_ref, bf16[128,128]{1,0:T(8,128)(2,1)S(1)} %collective-permute-done.9.refs_0_.row_ref, ...), custom_call_target="tpu_custom_call" | custom-call | bytes 282624 | tf_op jit(solution)/shard_map/pallas_call | solution.py:366
  (24 shorter events, 0.1 us)
Async XLA Ops:
  0.6 1.0 %copy-start.1 = (bf16[64,8,256]{2,1,0:T(8,128)(2,1)S(1)}, bf16[64,8,256]{2,1,0:T(8,128)(2,1)}, u32[]{:S(2)}) copy-start(bf16[64,8,256]{2,1,0:T(8,128)(2,1)} %param.17) | copy-start | bytes 786436
  0.6 0.9 %copy-start.4 = (bf16[256,2,32]{0,2,1:T(8,128)(2,1)S(1)}, bf16[256,2,32]{0,2,1:T(8,128)(2,1)}, u32[]{:S(2)}) copy-start(bf16[256,2,32]{0,2,1:T(8,128)(2,1)} %param.23) | copy-start | bytes 98308
  0.7 0.9 %copy-start.3 = (bf16[32,8,32]{2,1,0:T(8,128)(2,1)S(1)}, bf16[32,8,32]{2,1,0:T(8,128)(2,1)}, u32[]{:S(2)}) copy-start(bf16[32,8,32]{2,1,0:T(8,128)(2,1)} %pair_ref.1) | copy-start | bytes 49156
  0.7 0.9 %copy-start.5 = (bf16[4,32,128]{2,1,0:T(8,128)(2,1)S(1)}, bf16[4,32,128]{2,1,0:T(8,128)(2,1)}, u32[]{:S(2)}) copy-start(bf16[4,32,128]{2,1,0:T(8,128)(2,1)} %input_ref.1) | copy-start | bytes 98308
  0.7 0.9 %copy-start.6 = (bf16[128,128]{1,0:T(8,128)(2,1)S(1)}, bf16[128,128]{1,0:T(8,128)(2,1)}, u32[]{:S(2)}) copy-start(bf16[128,128]{1,0:T(8,128)(2,1)} %up_ref.1) | copy-start | bytes 98308
  0.7 0.9 %copy-start.7 = (bf16[128,128]{1,0:T(8,128)(2,1)S(1)}, bf16[128,128]{1,0:T(8,128)(2,1)}, u32[]{:S(2)}) copy-start(bf16[128,128]{1,0:T(8,128)(2,1)} %down_ref.1) | copy-start | bytes 98308
  0.7 0.9 %copy-start.9 = (bf16[128,32]{0,1:T(8,128)(2,1)S(1)}, bf16[128,32]{0,1:T(8,128)(2,1)}, u32[]{:S(2)}) copy-start(bf16[128,32]{0,1:T(8,128)(2,1)} %param.30) | copy-start | bytes 24580
  0.7 0.9 %copy-start.14 = (f32[32]{0:T(128)S(1)}, f32[32]{0:T(128)}, u32[]{:S(2)}) copy-start(f32[32]{0:T(128)} %param.29) | copy-start | bytes 388
  0.7 0.9 %copy-start.8 = (bf16[32,128]{1,0:T(8,128)(2,1)S(1)}, bf16[32,128]{1,0:T(8,128)(2,1)}, u32[]{:S(2)}) copy-start(bf16[32,128]{1,0:T(8,128)(2,1)} %gate_ref.1) | copy-start | bytes 24580
  0.7 0.9 %copy-start.10 = (f32[256]{0:T(256)S(1)}, f32[256]{0:T(256)}, u32[]{:S(2)}) copy-start(f32[256]{0:T(256)} %param.20) | copy-start | bytes 3076
  1.6 11.4 %copy-start.16 = (bf16[256,4,256]{2,1,0:T(4,128)(2,1)S(1)}, bf16[256,4,256]{2,1,0:T(4,128)(2,1)}, u32[]{:S(2)}) copy-start(bf16[256,4,256]{2,1,0:T(4,128)(2,1)} %param.21) | copy-start | bytes 1572868
  2.2 7.4 %collective-permute-start = (bf16[320,256]{1,0:T(8,128)(2,1)S(1)}, bf16[320,256]{1,0:T(8,128)(2,1)S(1)}, u32[]{:S(2)}, u32[]{:S(2)}) collective-permute-start(bf16[320,256]{1,0:T(8,128)(2,1)S(1)} %get-tuple-element.23.own_ref.refs_0_), channel_id=1, source_target_pairs={{0,2},{1,3},{2,0},{3,1},{4,6},{5,7},{6,4},{7,5},{8,10},{9,11},{10,... | collective-permute-start | bytes 491528 | tf_op jit(solution)/shard_map/ppermute | solution.py:379
  5.2 11.2 %collective-permute-start.4 = (bf16[224,256]{1,0:T(8,128)(2,1)S(1)}, bf16[224,256]{1,0:T(8,128)(2,1)S(1)}, u32[]{:S(2)}, u32[]{:S(2)}) collective-permute-start(bf16[224,256]{1,0:T(8,128)(2,1)S(1)} %get-tuple-element.25.own_ref), channel_id=1, source_target_pairs={{0,8},{4,12},{8,0},{12,4},{1,9},{5,13},{9,1},{13,5},{2,10},{6,14},... | collective-permute-start | bytes 344072 | tf_op jit(solution)/shard_map/ppermute | solution.py:379
  7.8 8.7 %collective-permute-start.3 = (bf16[224,256]{1,0:T(8,128)(2,1)S(1)}, bf16[224,256]{1,0:T(8,128)(2,1)S(1)}, u32[]{:S(2)}, u32[]{:S(2)}) collective-permute-start(bf16[224,256]{1,0:T(8,128)(2,1)S(1)} %get-tuple-element.26), channel_id=1, source_target_pairs={{0,4},{4,0},{8,12},{12,8},{1,5},{5,1},{9,13},{13,9},{2,6},{6,2},{1... | collective-permute-start | bytes 344072 | tf_op jit(solution)/shard_map/ppermute | solution.py:379
  9.4 7.4 %collective-permute-start.5 = (bf16[224,256]{1,0:T(8,128)(2,1)S(1)}, bf16[224,256]{1,0:T(8,128)(2,1)S(1)}, u32[]{:S(2)}, u32[]{:S(2)}) collective-permute-start(bf16[224,256]{1,0:T(8,128)(2,1)S(1)} %get-tuple-element.26), channel_id=1, source_target_pairs={{0,12},{4,8},{8,4},{12,0},{1,13},{5,9},{9,5},{13,1},{2,14},{6,10},... | collective-permute-start | bytes 344072 | tf_op jit(solution)/shard_map/ppermute | solution.py:379
  9.6 1.3 %copy-start.15 = (bf16[128,8]{0,1:T(8,128)(2,1)S(1)}, bf16[128,8]{0,1:T(8,128)(2,1)}, u32[]{:S(2)}) copy-start(bf16[128,8]{0,1:T(8,128)(2,1)} %param.25) | copy-start | bytes 6148
  9.6 1.3 %collective-permute-start.1 = (bf16[64,256]{1,0:T(8,128)(2,1)S(1)}, bf16[64,256]{1,0:T(8,128)(2,1)S(1)}, u32[]{:S(2)}, u32[]{:S(2)}) collective-permute-start(bf16[64,256]{1,0:T(8,128)(2,1)S(1)} %get-tuple-element.24), channel_id=1, source_target_pairs={{0,1},{1,0},{2,3},{3,2},{4,5},{5,4},{6,7},{7,6},{8,9},{9,8},{10,11... | collective-permute-start | bytes 98312 | tf_op jit(solution)/shard_map/ppermute | solution.py:379
  9.7 10.0 %collective-permute-start.6 = (bf16[576,256]{1,0:T(8,128)(2,1)S(1)}, bf16[576,256]{1,0:T(8,128)(2,1)S(1)}, u32[]{:S(2)}, u32[]{:S(2)}) collective-permute-start(bf16[576,256]{1,0:T(8,128)(2,1)S(1)} %get-tuple-element.34), channel_id=1, source_target_pairs={{0,1},{1,0},{2,3},{3,2},{4,5},{5,4},{6,7},{7,6},{8,9},{9,8},{10,11... | collective-permute-start | bytes 884744 | tf_op jit(solution)/shard_map/ppermute | solution.py:379
  11.3 5.5 %collective-permute-start.2 = (bf16[32,128]{1,0:T(8,128)(2,1)S(1)}, bf16[32,128]{1,0:T(8,128)(2,1)S(1)}, u32[]{:S(2)}, u32[]{:S(2)}) collective-permute-start(bf16[32,128]{1,0:T(8,128)(2,1)S(1)} %shard_map.179.near_bias_ref), channel_id=1, source_target_pairs={{0,4},{4,0},{8,12},{12,8},{1,5},{5,1},{9,13},{13,9},{2,6},{6,2},{1... | collective-permute-start | bytes 24584 | tf_op jit(solution)/shard_map/ppermute | solution.py:379
  13.0 1.0 %copy-start = (bf16[32,32,128]{2,1,0:T(8,128)(2,1)S(1)}, bf16[32,32,128]{2,1,0:T(8,128)(2,1)}, u32[]{:S(2)}) copy-start(bf16[32,32,128]{2,1,0:T(8,128)(2,1)} %param.24) | copy-start | bytes 786436
  13.0 1.0 %copy-start.2 = (bf16[256,256]{1,0:T(8,128)(2,1)S(1)}, bf16[256,256]{1,0:T(8,128)(2,1)}, u32[]{:S(2)}) copy-start(bf16[256,256]{1,0:T(8,128)(2,1)} %refs_1_.1) | copy-start | bytes 393220
  13.0 1.0 %copy-start.13 = (f32[128]{0:T(128)S(1)}, f32[128]{0:T(128)}, u32[]{:S(2)}) copy-start(f32[128]{0:T(128)} %param.31) | copy-start | bytes 1540
  13.1 0.9 %copy-start.11 = (f32[256]{0:T(256)S(1)}, f32[256]{0:T(256)}, u32[]{:S(2)}) copy-start(f32[256]{0:T(256)} %param.19) | copy-start | bytes 3076
  13.1 0.9 %copy-start.12 = (f32[128]{0:T(128)S(1)}, f32[128]{0:T(128)}, u32[]{:S(2)}) copy-start(f32[128]{0:T(128)} %param.26) | copy-start | bytes 1540
  16.9 2.8 %collective-permute-start.7 = (bf16[192,256]{1,0:T(8,128)(2,1)S(1)}, bf16[192,256]{1,0:T(8,128)(2,1)S(1)}, u32[]{:S(2)}, u32[]{:S(2)}) collective-permute-start(bf16[192,256]{1,0:T(8,128)(2,1)S(1)} %shard_map.181.refs_0_.refs_4_), channel_id=1, source_target_pairs={{0,1},{1,0},{2,3},{3,2},{4,5},{5,4},{6,7},{7,6},{8,9},{9,8},{10,11... | collective-permute-start | bytes 294920 | tf_op jit(solution)/shard_map/ppermute | solution.py:379
  16.9 7.0 %collective-permute-start.11 = (bf16[192,256]{1,0:T(8,128)(2,1)S(1)}, bf16[192,256]{1,0:T(8,128)(2,1)S(1)}, u32[]{:S(2)}, u32[]{:S(2)}) collective-permute-start(bf16[192,256]{1,0:T(8,128)(2,1)S(1)} %shard_map.181.refs_0_.refs_4_), channel_id=1, source_target_pairs={{0,2},{1,3},{2,0},{3,1},{4,6},{5,7},{6,4},{7,5},{8,10},{9,11},{10,... | collective-permute-start | bytes 294920 | tf_op jit(solution)/shard_map/ppermute | solution.py:379
  17.5 6.4 %collective-permute-start.12 = (bf16[192,256]{1,0:T(8,128)(2,1)S(1)}, bf16[192,256]{1,0:T(8,128)(2,1)S(1)}, u32[]{:S(2)}, u32[]{:S(2)}) collective-permute-start(bf16[192,256]{1,0:T(8,128)(2,1)S(1)} %shard_map.181.refs_0_.refs_4_), channel_id=1, source_target_pairs={{0,3},{1,2},{2,1},{3,0},{4,7},{5,6},{6,5},{7,4},{8,11},{9,10},{10,... | collective-permute-start | bytes 294920 | tf_op jit(solution)/shard_map/ppermute | solution.py:379
  20.4 6.0 %collective-permute-start.9 = (bf16[128,128]{1,0:T(8,128)(2,1)S(1)}, bf16[128,128]{1,0:T(8,128)(2,1)S(1)}, u32[]{:S(2)}, u32[]{:S(2)}) collective-permute-start(bf16[128,128]{1,0:T(8,128)(2,1)S(1)} %get-tuple-element.37), channel_id=1, source_target_pairs={{0,4},{4,0},{8,12},{12,8},{16,20},{20,16},{24,28},{28,24},{1,5},{5... | collective-permute-start | bytes 98312 | tf_op jit(solution)/shard_map/ppermute | solution.py:379
  22.4 4.8 %collective-permute-start.10 = (bf16[128,128]{1,0:T(8,128)(2,1)S(1)}, bf16[128,128]{1,0:T(8,128)(2,1)S(1)}, u32[]{:S(2)}, u32[]{:S(2)}) collective-permute-start(bf16[128,128]{1,0:T(8,128)(2,1)S(1)} %get-tuple-element.38), channel_id=1, source_target_pairs={{0,20},{4,16},{8,28},{12,24},{16,4},{20,0},{24,12},{28,8},{1,21},{... | collective-permute-start | bytes 98312 | tf_op jit(solution)/shard_map/ppermute | solution.py:379
  23.4 4.1 %collective-permute-start.8 = (bf16[128,128]{1,0:T(8,128)(2,1)S(1)}, bf16[128,128]{1,0:T(8,128)(2,1)S(1)}, u32[]{:S(2)}, u32[]{:S(2)}) collective-permute-start(bf16[128,128]{1,0:T(8,128)(2,1)S(1)} %get-tuple-element.36), channel_id=1, source_target_pairs={{0,16},{4,20},{8,24},{12,28},{16,0},{20,4},{24,8},{28,12},{1,17},{... | collective-permute-start | bytes 98312 | tf_op jit(solution)/shard_map/ppermute | solution.py:379
